TPU v7x, 512 devices: a whole 4x4x16 slice. The times are simulated.
512 devices in a mesh: dom: 32 (over z, y_hi), span: 16 (over x, y_lo, core).
Axes of the slice: x: 4, y: 4 (y_hi: 2, y_lo: 2; y = y_hi * 2 + y_lo), z: 16, core: 2. Of those that a mesh axis runs over, the one named last changes fastest.
Arguments:
- entities: bfloat16 [32768, 256], P('dom'), may hold values from -2.5 to 2.5
- operators: bfloat16 [64, 256, 256], P('span'), may hold values from -0.375 to 0.375
- left_rows: int32 [3, 32, 16, 512], P(None, 'dom', 'span'), may hold values from 0 to 1023
- right_rows: int32 [3, 32, 16, 512], P(None, 'dom', 'span'), may hold values from 0 to 1023
- negatives: int32 [3, 32, 16, 1024], P(None, 'dom', 'span'), may hold values from 0 to 1023
- counts: int32 [3, 32, 16, 64], P(None, 'dom', 'span'), may hold values from 1 to 8, as said below
Outputs:
- entity_grad: float32 [32768, 256], P(('dom', 'span'))
- relation_grad: float32 [64, 256, 256], P('span', 'dom')
Inputs may be any that keep to these rules, and one draw needn't show every extreme that they name: `counts`: in every bucket step and partition one relation has all 8 slots live in every group's list.
All inputs are finite; a program needn't handle non-finite values.
Results may differ from a plain program's by a relative error of at most 0.0021.
Values may be sent and summed in bfloat16 or wider, within the bound.
No kernel may reach another device: no remote copies, remote signals or barrier semaphores. Data moves between devices by JAX's collectives and lax.ppermute only.
A program may use at most 64 MiB of HBM per device.

v0:
```python
import jax
import jax.numpy as jnp
from jax import lax
from jax.sharding import PartitionSpec as P


def passed_along(value, axis, steps):
    count = lax.axis_size(axis)
    pairs = [(source, (source + steps) % count) for source in range(count)]
    return lax.ppermute(value, axis, pairs)


def live_slots(count_row, cap):
    return (
        (count_row[:, None] > jnp.arange(cap, dtype=jnp.int32)[None, :])
        .astype(jnp.float32)
        .reshape(-1)
    )


def apply_operators(received, operators):
    return jnp.einsum(
        "srkd,rde->srke", received, operators, preferred_element_type=jnp.float32
    ).astype(jnp.bfloat16)


def apply_transposed(received, operators):
    return jnp.einsum(
        "srke,rde->srkd", received, operators, preferred_element_type=jnp.float32
    ).astype(jnp.bfloat16)


def score_bucket(queries, right_slab, right_index, negative_index, live_mask, neg_scale):
    right_vecs = right_slab[right_index]
    negative_vecs = right_slab[negative_index]
    queries_wide = queries.astype(jnp.float32)
    positive = jnp.sum(queries_wide * right_vecs.astype(jnp.float32), axis=1)
    scores = jnp.einsum("kd,nd->kn", queries, negative_vecs, preferred_element_type=jnp.float32)
    pos_grad = -live_mask * jax.nn.sigmoid(-positive)
    neg_grad = (live_mask[:, None] * jax.nn.sigmoid(scores) * neg_scale).astype(jnp.bfloat16)
    query_grad = pos_grad[:, None] * right_vecs.astype(jnp.float32) + jnp.dot(
        neg_grad, negative_vecs, preferred_element_type=jnp.float32
    )
    query_grad = query_grad.astype(jnp.bfloat16)
    negative_rows = jnp.einsum("kn,kd->nd", neg_grad, queries, preferred_element_type=jnp.float32)
    slab_grad = (
        jnp.zeros(right_slab.shape, jnp.float32)
        .at[right_index]
        .add(pos_grad[:, None] * queries_wide)
    )
    slab_grad = slab_grad.at[negative_index].add(negative_rows)
    return (query_grad, slab_grad)


def shards(entities, operators, left_rows, right_rows, negatives, counts):
    bucket_count = left_rows.shape[0]
    slot_count = left_rows.shape[-1]
    neg_count = negatives.shape[-1]
    groups = lax.axis_size("span")
    rel_own = operators.shape[0]
    relations = rel_own * groups
    cap = slot_count // relations
    part_rows, feature_width = entities.shape
    neg_scale = float(neg_count) ** (-0.5)
    left_index = left_rows.reshape(bucket_count, slot_count)
    right_index = right_rows.reshape(bucket_count, slot_count)
    negative_index = negatives.reshape(bucket_count, neg_count)
    count_rows = counts.reshape(bucket_count, relations)
    right_slabs = [entities]
    for bucket in range(1, bucket_count):
        right_slabs.append(passed_along(right_slabs[-1], "dom", -1))
    left_vecs = [entities[left_index[bucket]] for bucket in range(bucket_count)]
    left_grad = jnp.zeros((part_rows, feature_width), jnp.float32)
    relation_acc = jnp.zeros((rel_own, feature_width, feature_width), jnp.float32)
    for bucket in range(bucket_count):
        owner_block = left_vecs[bucket].reshape(groups, rel_own, cap, feature_width)
        forward_received = lax.all_to_all(
            owner_block, "span", split_axis=0, concat_axis=0, tiled=True
        )
        query_block = lax.all_to_all(
            apply_operators(forward_received, operators),
            "span",
            split_axis=0,
            concat_axis=0,
            tiled=True,
        )
        queries = query_block.reshape(slot_count, feature_width)
        live_mask = live_slots(count_rows[bucket], cap)
        query_grad, slab_grad = score_bucket(
            queries,
            right_slabs[bucket],
            right_index[bucket],
            negative_index[bucket],
            live_mask,
            neg_scale,
        )
        carried = slab_grad if bucket == 0 else passed_along(carried, "dom", -1) + slab_grad
        grad_block = query_grad.reshape(groups, rel_own, cap, feature_width)
        backward_received = lax.all_to_all(
            grad_block, "span", split_axis=0, concat_axis=0, tiled=True
        )
        left_block = lax.all_to_all(
            apply_transposed(backward_received, operators),
            "span",
            split_axis=0,
            concat_axis=0,
            tiled=True,
        )
        left_grad = left_grad.at[left_index[bucket]].add(
            left_block.reshape(slot_count, feature_width).astype(jnp.float32)
        )
        relation_acc = relation_acc + jnp.einsum(
            "srkd,srke->rde",
            forward_received,
            backward_received,
            preferred_element_type=jnp.float32,
        )
    home_grad = passed_along(carried, "dom", bucket_count - 1)
    entity_share = lax.psum_scatter(left_grad + home_grad, "span", scatter_dimension=0, tiled=True)
    relation_share = lax.psum_scatter(relation_acc, "dom", scatter_dimension=1, tiled=True)
    return (entity_share, relation_share)


def solution(mesh):
    in_specs = (
        P("dom", None),
        P("span", None, None),
        P(None, "dom", "span", None),
        P(None, "dom", "span", None),
        P(None, "dom", "span", None),
        P(None, "dom", "span", None),
    )
    out_specs = (P(("dom", "span"), None), P("span", "dom", None))
    return jax.shard_map(shards, mesh=mesh, in_specs=in_specs, out_specs=out_specs, check_vma=False)
```

profile of v0, /device:TPU:24, one launch (start us, length us, event | category | flops | bytes accessed | tf_op | source)
XLA Modules:
  0.0 922.8 jit_solution(14029720000465699313)
XLA Ops:
  7.2 3.3 collective-permute-start.1
  11.2 3.4 gather_fusion
  14.6 8.5 all-to-all-start
  23.8 2.0 gather_fusion.1
  25.8 2.6 gather_fusion.3
  28.4 2.6 gather_fusion.6
  30.9 3.9 gather_fusion.2
  34.9 5.8 all-to-all-start.4
  41.7 5.5 all-to-all-done.4
  47.2 4.6 all-to-all-start.2
  52.8 5.6 all-to-all-done.2
  58.4 4.7 all-to-all-start.1
  64.0 5.6 all-to-all-done.1
  69.6 4.7 all-to-all-start.3
  76.5 3.7 scatter_custom_fusion
  81.9 6.9 scatter_fusion
  88.8 10.3 %collective-permute-start = (f32[1024,256]{1,0:T(8,128)S(1)}, f32[1024,256]{1,0:T(8,128)}, u32[]{:S(2)}, u32[]{:S(2)}) collective-permute-start(f32[1024,256]{1,0:T(8,128)S(1)} %scatter_fusion), channel_id=1, source_target_pairs={{0,496},{16,0},{32,16},{48,32},{64,48},{80,64},{96,80},{112,96},{1... | collective-permute-start | bytes 3145736 | tf_op jit(solution)/shard_map/ppermute | solution.py:10
  99.2 2.6 fusion.2
  101.7 1.9 gather_fusion.4
  104.2 4.9 gather_fusion.5
  112.2 5.8 all-to-all-start.8
  117.9 3.3 collective-permute-start.3
  121.2 2.7 fusion.44
  125.6 6.4 all-to-all-start.5
  132.0 2.3 convolution_bitcast_fusion.1
  134.3 4.1 collective-permute-done.3
  140.3 5.9 all-to-all-start.6
  146.7 4.9 gather_fusion.8
  154.8 5.7 all-to-all-start.10
  160.7 2.6 fusion
  163.4 5.4 scatter_custom_fusion.2
  168.8 8.2 scatter_fusion.1
  177.0 5.7 collective-permute-start.2
  182.8 2.6 fusion.1
  187.1 19.6 %collective-permute-done.2 = f32[1024,256]{1,0:T(8,128)S(1)} collective-permute-done((f32[1024,256]{1,0:T(8,128)}, f32[1024,256]{1,0:T(8,128)S(1)}, u32[]{:S(2)}, u32[]{:S(2)}) %collective-permute-start.2) | collective-permute-done | bytes 1048608 | tf_op jit(solution)/shard_map/ppermute | solution.py:10
  206.8 3.8 scatter_custom_fusion.4
  210.6 6.5 scatter_fusion.2
  217.1 3.1 collective-permute-start.4
  222.2 5.7 all-to-all-start.7
  230.0 4.5 all-to-all-done.7
  234.4 4.8 all-to-all-start.9
  241.3 4.6 all-to-all-done.9
  245.8 4.7 all-to-all-start.11
  251.4 3.7 scatter_custom_fusion.6
  255.2 3.8 scatter_custom_fusion.7
  258.9 3.8 scatter_custom_fusion.8
  263.7 585.0 %reduce-scatter.5.cloned.1.call-done = f32[4,8,256]{2,1,0:T(8,128)} async-done(((f32[4,256,256]{2,1,0:T(8,128)}), f32[4,8,256]{2,1,0:T(8,128)}) %reduce-scatter.5.cloned.1.call-update) | async-done | bytes 32784 | tf_op jit(solution)/shard_map/reduce_scatter | solution.py:120
  848.7 67.0 %reduce-scatter.3.cloned.1.call-done = f32[64,256]{1,0:T(8,128)} async-done(((f32[1024,256]{1,0:T(8,128)}), f32[64,256]{1,0:T(8,128)}) %reduce-scatter.3.cloned.1.call-update) | async-done | bytes 65552 | tf_op jit(solution)/shard_map/reduce_scatter | solution.py:119
  (119 shorter events, 28.6 us)
Async XLA Ops:
  7.2 33.5 %copy-start = (bf16[4,256,256]{2,1,0:T(8,128)(2,1)S(1)}, bf16[4,256,256]{2,1,0:T(8,128)(2,1)}, u32[]{:S(2)}) copy-start(bf16[4,256,256]{2,1,0:T(8,128)(2,1)} %param.7) | copy-start | bytes 1572868
  7.2 94.6 %collective-permute-start.1 = (bf16[1024,256]{1,0:T(8,128)(2,1)}, bf16[1024,256]{1,0:T(8,128)(2,1)S(1)}, u32[]{:S(2)}, u32[]{:S(2)}) collective-permute-start(bf16[1024,256]{1,0:T(8,128)(2,1)} %param.6), channel_id=1, source_target_pairs={{0,496},{16,0},{32,16},{48,32},{64,48},{80,64},{96,80},{112,96},{1... | collective-permute-start | bytes 1572872 | tf_op jit(solution)/shard_map/ppermute | solution.py:10
  11.2 12.0 %copy-start.23 = (s32[3,1,1,64]{3,2,1,0:T(1,128)S(1)}, s32[3,1,1,64]{3,2,1,0:T(1,128)}, u32[]{:S(2)}) copy-start(s32[3,1,1,64]{3,2,1,0:T(1,128)} %param.11) | copy-start | bytes 2308
  11.2 12.0 %copy-start.22 = (s32[3,1,1,512]{3,2,1,0:T(1,128)S(1)}, s32[3,1,1,512]{3,2,1,0:T(1,128)}, u32[]{:S(2)}) copy-start(s32[3,1,1,512]{3,2,1,0:T(1,128)} %param.9) | copy-start | bytes 18436
  11.2 12.0 %copy-start.21 = (s32[3,1,1,1024]{3,2,1,0:T(1,128)S(1)}, s32[3,1,1,1024]{3,2,1,0:T(1,128)}, u32[]{:S(2)}) copy-start(s32[3,1,1,1024]{3,2,1,0:T(1,128)} %param.10) | copy-start | bytes 36868
  11.2 12.6 %copy-start.1 = (bf16[1024,256]{1,0:T(8,128)(2,1)S(1)}, bf16[1024,256]{1,0:T(8,128)(2,1)}, u32[]{:S(2)}) copy-start(bf16[1024,256]{1,0:T(8,128)(2,1)} %param.6) | copy-start | bytes 1572868
  14.6 20.3 %all-to-all-start = ((bf16[16,4,8,256]{3,2,1,0:T(8,128)(2,1)}), bf16[16,4,8,256]{3,2,1,0:T(8,128)(2,1)S(1)}, u32[]{:S(2)}, u32[]{:S(2)}) async-start(bf16[16,4,8,256]{3,2,1,0:T(8,128)(2,1)} %bitcast.5), calls=%async_computation | async-start | bytes 524288 | tf_op jit(solution)/shard_map/all_to_all | solution.py:77
  25.8 48.4 %copy-start.13 = (bf16[512,256]{1,0:T(8,128)(2,1)}, bf16[512,256]{1,0:T(8,128)(2,1)S(1)}, u32[]{:S(2)}) copy-start(bf16[512,256]{1,0:T(8,128)(2,1)S(1)} %gather_fusion.1) | copy-start | bytes 786436
  34.9 39.8 %copy-start.18 = (bf16[1024,256]{1,0:T(8,128)(2,1)}, bf16[1024,256]{1,0:T(8,128)(2,1)S(1)}, u32[]{:S(2)}) copy-start(bf16[1024,256]{1,0:T(8,128)(2,1)S(1)} %gather_fusion.2) | copy-start | bytes 1572868
  34.9 6.8 copy-start.7
  34.9 12.3 %all-to-all-start.4 = ((bf16[16,4,8,256]{3,2,1,0:T(8,128)(2,1)}), bf16[16,4,8,256]{3,2,1,0:T(8,128)(2,1)S(1)}, u32[]{:S(2)}, u32[]{:S(2)}) async-start(bf16[16,4,8,256]{3,2,1,0:T(8,128)(2,1)} %bitcast.30), calls=%async_computation.4 | async-start | bytes 524288 | tf_op jit(solution)/shard_map/all_to_all | solution.py:77
  47.2 5.6 copy-start.9
  47.2 11.2 %all-to-all-start.2 = ((bf16[16,4,8,256]{3,2,1,0:T(8,128)(2,1)}), bf16[16,4,8,256]{3,2,1,0:T(8,128)(2,1)S(1)}, u32[]{:S(2)}, u32[]{:S(2)}) async-start(bf16[16,4,8,256]{3,2,1,0:T(8,128)(2,1)} %bitcast.18), calls=%async_computation.2 | async-start | bytes 524288 | tf_op jit(solution)/shard_map/all_to_all | solution.py:77
  58.4 5.6 copy-start.11
  58.4 11.2 %all-to-all-start.1 = ((bf16[16,4,8,256]{3,2,1,0:T(8,128)(2,1)}), bf16[16,4,8,256]{3,2,1,0:T(8,128)(2,1)S(1)}, u32[]{:S(2)}, u32[]{:S(2)}) async-start(bf16[16,4,8,256]{3,2,1,0:T(8,128)(2,1)} %copy.63), calls=%async_computation.1 | async-start | bytes 524288 | tf_op jit(solution)/shard_map/all_to_all | solution.py:80
  69.6 6.9 copy-start.3
  69.6 34.1 %all-to-all-start.3 = ((bf16[16,4,8,256]{3,2,1,0:T(8,128)(2,1)}), bf16[16,4,8,256]{3,2,1,0:T(8,128)(2,1)S(1)}, u32[]{:S(2)}, u32[]{:S(2)}) async-start(bf16[16,4,8,256]{3,2,1,0:T(8,128)(2,1)} %copy.68), calls=%async_computation.3 | async-start | bytes 524288 | tf_op jit(solution)/shard_map/all_to_all | solution.py:80
  88.8 74.5 %collective-permute-start = (f32[1024,256]{1,0:T(8,128)S(1)}, f32[1024,256]{1,0:T(8,128)}, u32[]{:S(2)}, u32[]{:S(2)}) collective-permute-start(f32[1024,256]{1,0:T(8,128)S(1)} %scatter_fusion), channel_id=1, source_target_pairs={{0,496},{16,0},{32,16},{48,32},{64,48},{80,64},{96,80},{112,96},{1... | collective-permute-start | bytes 3145736 | tf_op jit(solution)/shard_map/ppermute | solution.py:10
  103.7 5.4 copy-start.16
  109.1 1.9 copy-start.17
  109.1 1.9 copy-start.20
  111.0 1.1 copy-start.6
  112.2 13.4 %all-to-all-start.8 = ((bf16[16,4,8,256]{3,2,1,0:T(8,128)(2,1)}), bf16[16,4,8,256]{3,2,1,0:T(8,128)(2,1)}, u32[]{:S(2)}, u32[]{:S(2)}) async-start(bf16[16,4,8,256]{3,2,1,0:T(8,128)(2,1)} %bitcast.131), calls=%async_computation.8 | async-start | bytes 524288 | tf_op jit(solution)/shard_map/all_to_all | solution.py:99
  117.9 14.1 %copy-start.12 = (bf16[16,4,8,256]{3,2,1,0:T(8,128)(2,1)S(1)}, bf16[16,4,8,256]{3,2,1,0:T(8,128)(2,1)}, u32[]{:S(2)}) copy-start(bf16[16,4,8,256]{3,2,1,0:T(8,128)(2,1)} %copy-done.11) | copy-start | bytes 786436
  117.9 20.4 %collective-permute-start.3 = (bf16[1024,256]{1,0:T(8,128)(2,1)S(1)}, bf16[1024,256]{1,0:T(8,128)(2,1)S(1)}, u32[]{:S(2)}, u32[]{:S(2)}) collective-permute-start(bf16[1024,256]{1,0:T(8,128)(2,1)S(1)} %collective-permute-done.1), channel_id=1, source_target_pairs={{0,496},{16,0},{32,16},{48,32},{64,48},{80,64},{96,80},{112,96},{1... | collective-permute-start | bytes 1572872 | tf_op jit(solution)/shard_map/ppermute | solution.py:10
  125.6 14.7 %all-to-all-start.5 = ((bf16[16,4,8,256]{3,2,1,0:T(8,128)(2,1)}), bf16[16,4,8,256]{3,2,1,0:T(8,128)(2,1)S(1)}, u32[]{:S(2)}, u32[]{:S(2)}) async-start(bf16[16,4,8,256]{3,2,1,0:T(8,128)(2,1)} %copy.73), calls=%async_computation.5 | async-start | bytes 524288 | tf_op jit(solution)/shard_map/all_to_all | solution.py:80
  140.3 11.4 %copy-start.14 = (bf16[512,256]{1,0:T(8,128)(2,1)}, bf16[512,256]{1,0:T(8,128)(2,1)S(1)}, u32[]{:S(2)}) copy-start(bf16[512,256]{1,0:T(8,128)(2,1)S(1)} %gather_fusion.7) | copy-start | bytes 786436
  140.3 14.4 %all-to-all-start.6 = ((bf16[16,4,8,256]{3,2,1,0:T(8,128)(2,1)}), bf16[16,4,8,256]{3,2,1,0:T(8,128)(2,1)}, u32[]{:S(2)}, u32[]{:S(2)}) async-start(bf16[16,4,8,256]{3,2,1,0:T(8,128)(2,1)} %bitcast.36), calls=%async_computation.6 | async-start | bytes 524288 | tf_op jit(solution)/shard_map/all_to_all | solution.py:99
  151.7 1.9 copy-start.15
  151.7 1.9 copy-start.19
  153.6 7.1 copy-start.4
  153.6 7.1 copy-start.8
  154.8 28.0 %all-to-all-start.10 = ((bf16[16,4,8,256]{3,2,1,0:T(8,128)(2,1)}), bf16[16,4,8,256]{3,2,1,0:T(8,128)(2,1)}, u32[]{:S(2)}, u32[]{:S(2)}) async-start(bf16[16,4,8,256]{3,2,1,0:T(8,128)(2,1)} %bitcast.130), calls=%async_computation.10 | async-start | bytes 524288 | tf_op jit(solution)/shard_map/all_to_all | solution.py:99
  160.5 688.2 %reduce-scatter.5.cloned.1.call-start = ((), (), s32[]{:S(2)}) async-start(), calls=%async_computation.15 | async-start | bytes 1081344 | tf_op jit(solution)/shard_map/reduce_scatter | solution.py:120
  163.4 5.4 copy-start.2
  168.8 14.0 %copy-start.10 = (bf16[16,4,8,256]{3,2,1,0:T(8,128)(2,1)S(1)}, bf16[16,4,8,256]{3,2,1,0:T(8,128)(2,1)}, u32[]{:S(2)}) copy-start(bf16[16,4,8,256]{3,2,1,0:T(8,128)(2,1)} %copy-done.9) | copy-start | bytes 786436
  177.0 29.7 %collective-permute-start.2 = (f32[1024,256]{1,0:T(8,128)}, f32[1024,256]{1,0:T(8,128)S(1)}, u32[]{:S(2)}, u32[]{:S(2)}) collective-permute-start(f32[1024,256]{1,0:T(8,128)} %scatter_fusion.1), channel_id=1, source_target_pairs={{0,496},{16,0},{32,16},{48,32},{64,48},{80,64},{96,80},{112,96},{1... | collective-permute-start | bytes 3145736 | tf_op jit(solution)/shard_map/ppermute | solution.py:10
  217.1 34.3 %collective-permute-start.4 = (f32[1024,256]{1,0:T(8,128)S(1)}, f32[1024,256]{1,0:T(8,128)S(1)}, u32[]{:S(2)}, u32[]{:S(2)}) collective-permute-start(f32[1024,256]{1,0:T(8,128)S(1)} %scatter_fusion.2), channel_id=1, source_target_pairs={{0,32},{16,48},{32,64},{48,80},{64,96},{80,112},{96,128},{112,144}... | collective-permute-start | bytes 3145736 | tf_op jit(solution)/shard_map/ppermute | solution.py:10
  222.2 12.2 %all-to-all-start.7 = ((bf16[16,4,8,256]{3,2,1,0:T(8,128)(2,1)}), bf16[16,4,8,256]{3,2,1,0:T(8,128)(2,1)S(1)}, u32[]{:S(2)}, u32[]{:S(2)}) async-start(bf16[16,4,8,256]{3,2,1,0:T(8,128)(2,1)} %copy.78), calls=%async_computation.7 | async-start | bytes 524288 | tf_op jit(solution)/shard_map/all_to_all | solution.py:102
  234.4 11.4 %all-to-all-start.9 = ((bf16[16,4,8,256]{3,2,1,0:T(8,128)(2,1)}), bf16[16,4,8,256]{3,2,1,0:T(8,128)(2,1)S(1)}, u32[]{:S(2)}, u32[]{:S(2)}) async-start(bf16[16,4,8,256]{3,2,1,0:T(8,128)(2,1)} %copy.80), calls=%async_computation.9 | async-start | bytes 524288 | tf_op jit(solution)/shard_map/all_to_all | solution.py:102
  245.8 13.1 %all-to-all-start.11 = ((bf16[16,4,8,256]{3,2,1,0:T(8,128)(2,1)}), bf16[16,4,8,256]{3,2,1,0:T(8,128)(2,1)S(1)}, u32[]{:S(2)}, u32[]{:S(2)}) async-start(bf16[16,4,8,256]{3,2,1,0:T(8,128)(2,1)} %copy.82), calls=%async_computation.11 | async-start | bytes 524288 | tf_op jit(solution)/shard_map/all_to_all | solution.py:102
  250.5 665.3 %reduce-scatter.3.cloned.1.call-start = ((), (), s32[]{:S(2)}) async-start(), calls=%async_computation.14 | async-start | bytes 1114112 | tf_op jit(solution)/shard_map/reduce_scatter | solution.py:119
  262.7 1.0 copy-start.5
Sparse Core Ops, SparseCore 0:
  185.6 663.0 reduce-scatter.4
  852.3 63.3 reduce-scatter.2
where the time goes:
time: 936 us; the launch traced here: 923 us
  waiting for transfers between devices  704 us (75%)
  starting transfers between devices  93.3 us (10%)
  other arithmetic  47.4 us (5%)
  local copies, waits for them, and re-layouts  34.7 us (4%)
  matrix products  28.4 us (3%)
  between operations  14.9 us (2%)
    reduce_scatter x1, waiting for transfers between devices, shards(): lax.psum_scatter(relation_acc, 'dom', scatter_dimension=1, tiled=True)  585 us
    reduce_scatter x1, waiting for transfers between devices, shards(): lax.psum_scatter(left_grad + home_grad, 'span', scatter_dimension=0, tile...  67 us
    ppermute x5, starting transfers between devices, passed_along(): return lax.ppermute(value, axis, pairs)  25.7 us
    ppermute x5, waiting for transfers between devices, passed_along(): return lax.ppermute(value, axis, pairs)  24.6 us
    scatter-add x3, other arithmetic, score_bucket(): slab_grad = slab_grad.at[negative_index].add(negative_rows)  21.6 us
    all_to_all x3, starting transfers between devices, shards(): lax.all_to_all(owner_block, 'span', split_axis=0, concat_axis=0, tiled=True)  19 us
  transfers between devices with their start and end apart: 19, of which 11 were waited for; matrix products, arithmetic and copies ran while one was open for 12% of the time, Pallas kernels for 0%

commit v1 on v0

v1 whole, which is shorter than its diff:
```python
import functools

import jax
import jax.numpy as jnp
from jax import lax
from jax.experimental import pallas as pl
from jax.experimental.pallas import tpu as pltpu
from jax.sharding import PartitionSpec as P

BF = jnp.bfloat16
F32 = jnp.float32
NT = (((1,), (1,)), ((), ()))
TN = (((0,), (0,)), ((), ()))
VMEM = pl.BlockSpec(memory_space=pltpu.VMEM)
SMEM = pl.BlockSpec(memory_space=pltpu.SMEM)


def dot(a, b, dims=(((1,), (0,)), ((), ()))):
    return lax.dot_general(a, b, dims, preferred_element_type=F32)


def passed_along(value, axis, steps):
    count = lax.axis_size(axis)
    pairs = [(source, (source + steps) % count) for source in range(count)]
    return lax.ppermute(value, axis, pairs)


def exchanged(value, axis):
    return lax.all_to_all(value, axis, split_axis=0, concat_axis=0, tiled=True)


def iota(shape, axis):
    return lax.broadcasted_iota(jnp.int32, shape, axis)


def pack_kernel(buckets, groups, neg_ref, pair_ref, count_ref, out_ref):
    neg_count = neg_ref.shape[1]
    hist_rows = 8 * buckets
    for s in range(buckets):
        row = neg_ref[s : s + 1, :]
        high = (iota((16, neg_count), 0) == (row >> 7)).astype(F32).astype(BF)
        low = (iota((128, neg_count), 0) == (row & 127)).astype(F32).astype(BF)
        hist = dot(high, low, NT)[:8].astype(jnp.int32)
        for d in range(groups):
            out_ref[d, 8 * s : 8 * s + 8, :] = hist
    lines = pair_ref.shape[0] // buckets
    rest = jnp.zeros((8 - 2 * buckets, 128), jnp.int32)
    counts = count_ref[...]
    counts = jnp.concatenate([counts, jnp.zeros((buckets, 128 - counts.shape[1]), jnp.int32)], 1)
    for line in range(lines):
        pairs = [pair_ref[lines * s + line : lines * s + line + 1, :] for s in range(buckets)]
        block = jnp.concatenate(pairs + [counts, rest], 0)
        for d in range(line * groups // lines, (line + 1) * groups // lines):
            out_ref[d, hist_rows : hist_rows + 8, :] = block


def bucket_kernel(
    buckets, neg_scale, me_ref, x_ref, *refs
):
    slab_refs = refs[:buckets]
    ops_ref = refs[buckets]
    ent_ref, rel_ref = refs[buckets + 1 : buckets + 3]
    left_acc, rel_acc, ohl_ref, ng_ref, whi_ref, wlo_ref, mult_ref, rows_ref = refs[buckets + 3 :]
    rel_own, width, _ = ops_ref.shape
    groups = x_ref.shape[0]
    part_rows = slab_refs[0].shape[0]
    slots = rel_own * 128
    chunk = 128
    chunks = part_rows // chunk
    hist_rows = 8 * buckets
    share = part_rows // groups
    me = me_ref[0]

    lane_row = iota((128, slots), 0)
    lane = iota((128, slots), 1)
    relation, slot = lane >> 7, lane & 7
    per_line = 128 // (8 * rel_own)
    pick_slot = (lane_row == (me % per_line) * (8 * rel_own) + relation * 8 + slot)
    pick_slot = pick_slot.astype(F32).astype(BF)
    pick_count = (lane_row == me * rel_own + relation).astype(F32).astype(BF)
    lane = iota((groups, slots), 1)
    own_group = iota((groups, slots), 0) == ((lane >> 3) & (groups - 1))
    slot_row = iota((1, slots), 1) & 7

    def own(values):
        return jnp.sum(jnp.where(own_group, values, 0.0), axis=0, keepdims=True)

    def narrow(values):
        return values.astype(F32).astype(BF)

    for step, s in enumerate(list(range(1, buckets)) + [0]):
        slab = slab_refs[s]
        pair = x_ref[:, hist_rows + s, :]
        left, right = pair & 65535, pair >> 16
        parts = [left >> 5, left & 31, right >> 5, right & 31]
        parts = dot(narrow(jnp.concatenate(parts, 0)), pick_slot)
        parts = [own(parts[groups * q : groups * (q + 1)]) for q in range(4)]
        left_row = (parts[0] * 32.0 + parts[1]).astype(jnp.int32)
        right_row = (parts[2] * 32.0 + parts[3]).astype(jnp.int32)
        count_row = own(dot(narrow(x_ref[:, hist_rows + buckets + s, :]), pick_count))
        live = (count_row.astype(jnp.int32) > slot_row).astype(F32)

        for a in range(8):
            hist = x_ref[:, 8 * s + a, :].astype(F32)
            hist = jnp.broadcast_to(hist[:, None, :], (groups, 8, 128)).reshape(128, 128)
            mult_ref[128 * a : 128 * (a + 1), :] = hist.T

        def left_hot(n, carry):
            at = pl.multiple_of(n * chunk, chunk)
            rows = iota((chunk, slots), 0) + n * chunk
            ohl_ref[pl.ds(at, chunk), :] = (rows == left_row).astype(F32).astype(BF)
            return carry

        lax.fori_loop(0, chunks, left_hot, 0)
        left_t = dot(slab_refs[0][...], ohl_ref[...], TN).astype(BF)
        query_t = jnp.concatenate(
            [dot(ops_ref[i], left_t[:, 128 * i : 128 * (i + 1)], TN) for i in range(rel_own)], 1
        ).astype(BF)

        def score(n, positive):
            at = pl.multiple_of(n * chunk, chunk)
            scores = dot(slab[pl.ds(at, chunk), :], query_t)
            sig = 0.5 * jnp.tanh(0.5 * scores) + 0.5
            ng_ref[pl.ds(at, chunk), :] = (live * sig * neg_scale).astype(BF)
            hit = (iota((chunk, slots), 0) + n * chunk) == right_row
            return positive + jnp.sum(jnp.where(hit, scores, 0.0), axis=0, keepdims=True)

        positive = lax.fori_loop(0, chunks, score, jnp.zeros((1, slots), F32))
        pos_grad = -live * jax.nn.sigmoid(-positive)

        def weigh(n, carry):
            at = pl.multiple_of(n * chunk, chunk)
            mult = mult_ref[pl.ds(at, chunk), :]
            mult = jnp.concatenate([mult] * rel_own, 1)
            hit = (iota((chunk, slots), 0) + n * chunk) == right_row
            weight = ng_ref[pl.ds(at, chunk), :].astype(F32) * mult
            weight = weight + jnp.where(hit, pos_grad, 0.0)
            high = weight.astype(BF)
            whi_ref[pl.ds(at, chunk), :] = high
            wlo_ref[pl.ds(at, chunk), :] = (weight - high.astype(F32)).astype(BF)
            return carry

        lax.fori_loop(0, chunks, weigh, 0)
        whole = slab[...]
        qgrad_t = (dot(whole, whi_ref[...], TN) + dot(whole, wlo_ref[...], TN)).astype(BF)
        rows_ref[...] = dot(whi_ref[...], query_t, NT) + dot(wlo_ref[...], query_t, NT)
        lgrad_t = jnp.concatenate(
            [dot(ops_ref[i], qgrad_t[:, 128 * i : 128 * (i + 1)]) for i in range(rel_own)], 1
        ).astype(BF)
        left_rows = dot(ohl_ref[...], lgrad_t, NT)
        left_acc[...] = left_rows if step == 0 else left_acc[...] + left_rows
        for i in range(rel_own):
            cols = slice(128 * i, 128 * (i + 1))
            outer = dot(left_t[:, cols], qgrad_t[:, cols], NT)
            rel_acc[i] = outer if step == 0 else rel_acc[i] + outer
        for d in range(groups):
            block = rows_ref[share * d : share * (d + 1), :]
            if s == 0:
                block = block + left_acc[share * d : share * (d + 1), :]
            ent_ref[d, share * s : share * (s + 1), :] = block.astype(BF)

    doms, held, _ = rel_ref.shape
    held = held // rel_own
    for d in range(doms):
        block = [rel_acc[i, held * d : held * (d + 1), :] for i in range(rel_own)]
        rel_ref[d] = jnp.concatenate(block, 0).astype(BF)


def shards(entities, operators, left_rows, right_rows, negatives, counts):
    buckets = left_rows.shape[0]
    slot_count = left_rows.shape[-1]
    neg_count = negatives.shape[-1]
    groups = lax.axis_size("span")
    doms = lax.axis_size("dom")
    rel_own = operators.shape[0]
    relations = rel_own * groups
    part_rows, width = entities.shape
    neg_scale = float(neg_count) ** (-0.5)
    share = part_rows // groups
    slots = rel_own * 128

    pair = (left_rows + (right_rows << 16)).reshape(buckets * slot_count // 128, 128)
    packed = pl.pallas_call(
        functools.partial(pack_kernel, buckets, groups),
        out_shape=jax.ShapeDtypeStruct((groups, 8 * buckets + 8, 128), jnp.int32),
        in_specs=[VMEM] * 3,
        out_specs=VMEM,
        name="pack_lists",
    )(negatives.reshape(buckets, neg_count), pair, counts.reshape(buckets, relations))
    received = exchanged(packed, "span")
    slabs = [entities] + [passed_along(entities, "dom", -s) for s in range(1, buckets)]

    me = lax.axis_index("span").astype(jnp.int32).reshape(1)
    ent_parts, rel_parts = pl.pallas_call(
        functools.partial(bucket_kernel, buckets, neg_scale),
        out_shape=(
            jax.ShapeDtypeStruct((groups, buckets * share, width), BF),
            jax.ShapeDtypeStruct((doms, rel_own * width // doms, width), BF),
        ),
        in_specs=[SMEM] + [VMEM] * (buckets + 2),
        out_specs=(VMEM, VMEM),
        scratch_shapes=[
            pltpu.VMEM((part_rows, width), F32),
            pltpu.VMEM((rel_own, width, width), F32),
            pltpu.VMEM((part_rows, slots), BF),
            pltpu.VMEM((part_rows, slots), BF),
            pltpu.VMEM((part_rows, slots), BF),
            pltpu.VMEM((part_rows, slots), BF),
            pltpu.VMEM((part_rows, 128), F32),
            pltpu.VMEM((part_rows, width), F32),
        ],
        compiler_params=pltpu.CompilerParams(vmem_limit_bytes=40 * 1024 * 1024),
        cost_estimate=pl.CostEstimate(
            flops=6_200_000_000, bytes_accessed=6_000_000, transcendentals=1_600_000
        ),
        name="buckets",
    )(me, received, *slabs, operators)

    ent_shares = jnp.sum(exchanged(ent_parts, "span").astype(F32), axis=0)
    entity_share = ent_shares[:share]
    for s in range(1, buckets):
        entity_share = entity_share + passed_along(ent_shares[share * s : share * (s + 1)], "dom", s)
    rel_share = jnp.sum(exchanged(rel_parts, "dom").astype(F32), axis=0)
    return (entity_share, rel_share.reshape(rel_own, width // doms, width))


def solution(mesh):
    in_specs = (
        P("dom", None),
        P("span", None, None),
        P(None, "dom", "span", None),
        P(None, "dom", "span", None),
        P(None, "dom", "span", None),
        P(None, "dom", "span", None),
    )
    out_specs = (P(("dom", "span"), None), P("span", "dom", None))
    return jax.shard_map(shards, mesh=mesh, in_specs=in_specs, out_specs=out_specs, check_vma=False)
```

time: 936 us -> 126 us (0.13); the launches traced: 923 us -> 125 us
  waiting for transfers between devices: 704 us -> 31.7 us
  starting transfers between devices: 93.3 us -> 41.5 us
  other arithmetic: 47.4 us -> 2.29 us
  local copies, waits for them, and re-layouts: 34.7 us -> 5.29 us
  matrix products: 28.4 us -> 0 us
  blocking collectives: 0 us -> 24.3 us
  Pallas kernels: 0 us -> 19.3 us
  between operations: 14.9 us -> 0.69 us
    reduce_scatter x2 -> x0, waiting for transfers between devices: 652 us -> none  [the longest x1 585 us: shards(): lax.psum_scatter(relation_acc, 'dom', scatter_dimension=1, tiled=True)]
    all_to_all x12 -> x2, starting transfers between devices: 67.3 us -> 20.2 us  [exchanged(): return lax.all_to_all(value, axis, split_axis=0, concat_axis=0, tiled=True)]
    scatter-add x9 -> x0, other arithmetic: 45.8 us -> none  [the longest x3 21.6 us: score_bucket(): slab_grad = slab_grad.at[negative_index].add(negative_rows)]
    dot_general x18 -> x0, matrix products: 28.4 us -> none  [the longest x3 7.54 us: shards(): jnp.einsum('srkd,srke->rde', forward_received, backward_received, preferr...]
    gather x9 -> x0, local copies, waits for them, and re-layouts: 28.1 us -> none  [the longest x3 13.8 us: score_bucket(): negative_vecs = right_slab[negative_index]]
    all_to_all x0 -> x1, blocking collectives: none -> 24.3 us  [exchanged(): return lax.all_to_all(value, axis, split_axis=0, concat_axis=0, tiled=True)]
    pallas_call x0 -> x2, Pallas kernels: none -> 19.3 us  [the longest x1 17.6 us: shards(): pl.pallas_call(functools.partial(bucket_kernel, buckets, neg_scale), out_...]
    all_to_all x12 -> x2, waiting for transfers between devices: 27.4 us -> 10.7 us  [exchanged(): return lax.all_to_all(value, axis, split_axis=0, concat_axis=0, tiled=True)]
  transfers between devices with their start and end apart: 19 -> 6, of which waited for: 11 -> 4; matrix products, arithmetic and copies ran while one was open for 12% -> 4% of each run, Pallas kernels for 0% -> 1%
where the time goes in v1:
time: 126 us; the launch traced here: 125 us
  starting transfers between devices  41.5 us (33%)
  waiting for transfers between devices  31.7 us (25%)
  blocking collectives  24.3 us (19%)
  Pallas kernels  19.3 us (15%)
  local copies, waits for them, and re-layouts  5.29 us (4%)
  other arithmetic  2.29 us (2%)
    all_to_all x1, blocking collectives, exchanged(): return lax.all_to_all(value, axis, split_axis=0, concat_axis=0, tiled=True)  24.3 us
    ppermute x4, starting transfers between devices, passed_along(): return lax.ppermute(value, axis, pairs)  21.3 us
    ppermute x4, waiting for transfers between devices, passed_along(): return lax.ppermute(value, axis, pairs)  21 us
    all_to_all x2, starting transfers between devices, exchanged(): return lax.all_to_all(value, axis, split_axis=0, concat_axis=0, tiled=True)  20.2 us
    pallas_call x1, Pallas kernels, shards(): pl.pallas_call(functools.partial(bucket_kernel, buckets, neg_scale), out_...  17.6 us
    all_to_all x2, waiting for transfers between devices, exchanged(): return lax.all_to_all(value, axis, split_axis=0, concat_axis=0, tiled=True)  10.7 us
    unnamed x6, local copies, waits for them, and re-layouts  4.67 us
  transfers between devices with their start and end apart: 6, of which 4 were waited for; matrix products, arithmetic and copies ran while one was open for 4% of the time, Pallas kernels for 1%

profile of v1, /device:TPU:24, one launch (start us, length us, event | category | flops | bytes accessed | tf_op | source)
XLA Modules:
  0.0 125.2 jit_solution(12834875136733178445)
XLA Ops:
  0.6 3.1 %collective-permute-start = (bf16[1024,256]{1,0:T(8,128)(2,1)}, bf16[1024,256]{1,0:T(8,128)(2,1)S(1)}, u32[]{:S(2)}, u32[]{:S(2)}) collective-permute-start(bf16[1024,256]{1,0:T(8,128)(2,1)} %refs_0_.1), channel_id=1, source_target_pairs={{0,496},{16,0},{32,16},{48,32},{64,48},{80,64},{96,80},{112,96},{1... | collective-permute-start | bytes 1572872 | tf_op jit(solution)/shard_map/ppermute | solution.py:25
  3.8 11.4 %collective-permute-start.1 = (bf16[1024,256]{1,0:T(8,128)(2,1)}, bf16[1024,256]{1,0:T(8,128)(2,1)S(1)}, u32[]{:S(2)}, u32[]{:S(2)}) collective-permute-start(bf16[1024,256]{1,0:T(8,128)(2,1)} %refs_0_.1), channel_id=1, source_target_pairs={{0,480},{16,496},{32,0},{48,16},{64,32},{80,48},{96,64},{112,80},{... | collective-permute-start | bytes 1572872 | tf_op jit(solution)/shard_map/ppermute | solution.py:25
  15.2 1.3 %copy.13 = s32[3,1,1,64]{3,0,1,2:T(4,128)} copy(s32[3,1,1,64]{3,2,1,0:T(1,128)} %param.11) | data formatting | bytes 1536
  16.5 0.7 add_reduce_fusion
  17.2 0.6 reshape.21.pair_ref
  17.8 1.3 %copy.12 = s32[3,1,1,1024]{3,0,1,2:T(4,128)} copy(s32[3,1,1,1024]{3,2,1,0:T(1,128)} %param.10) | data formatting | bytes 24576
  19.1 1.8 %pack_lists.1 = s32[16,32,128]{2,1,0:T(8,128)} custom-call(s32[3,1024]{1,0:T(4,128)} %bitcast.8, s32[12,128]{1,0:T(8,128)} %reshape.21.pair_ref, s32[3,64]{1,0:T(4,128)} %bitcast.10), custom_call_target="tpu_custom_call" | custom-call | tf_op jit(solution)/shard_map/pack_lists/pallas_call | solution.py:183
  20.9 5.8 %all-to-all-start = ((s32[16,32,128]{2,1,0:T(8,128)}), s32[16,32,128]{2,1,0:T(8,128)S(1)}, u32[]{:S(2)}, u32[]{:S(2)}) async-start(s32[16,32,128]{2,1,0:T(8,128)} %pack_lists.1), calls=%async_computation | async-start | bytes 524288 | tf_op jit(solution)/shard_map/all_to_all | solution.py:29
  26.7 6.5 %all-to-all-done.x_ref = s32[16,32,128]{2,1,0:T(8,128)S(1)} async-done(((s32[16,32,128]{2,1,0:T(8,128)}), s32[16,32,128]{2,1,0:T(8,128)S(1)}, u32[]{:S(2)}, u32[]{:S(2)}) %all-to-all-start) | async-done | bytes 262176 | tf_op jit(solution)/shard_map/all_to_all | solution.py:29
  33.2 0.0 collective-permute-done.refs_1_
  33.2 0.0 collective-permute-done.1.refs_2_
  33.2 0.0 copy-start
  33.2 1.0 copy-done
  34.2 0.0 copy-start.1
  34.2 1.0 copy-done.1
  35.3 17.6 %buckets.1 = (bf16[16,192,256]{2,1,0:T(8,128)(2,1)S(1)}, bf16[32,32,256]{2,1,0:T(8,128)(2,1)}) custom-call(s32[1]{0:T(128)} %bitcast.me_ref, s32[16,32,128]{2,1,0:T(8,128)S(1)} %all-to-all-done.x_ref, bf16[1024,256]{1,0:T(8,128)(2,1)S(1)} %copy-done, bf16[1024,256]{1,0:T(8,128)(2,1)S(1)} %collective-permute-done.refs_1_, ...), custom_call_target="tpu_custom_call" | custom-call | flops 6200000000 | bytes 6000000 | tf_op jit(solution)/shard_map/buckets/pallas_call | solution.py:194
  52.8 24.3 %all_to_all.15 = bf16[16,192,256]{2,1,0:T(8,128)(2,1)S(1)} all-to-all(bf16[16,192,256]{2,1,0:T(8,128)(2,1)S(1)} %get-tuple-element.4), channel_id=1, replica_groups=mesh['dom'=32,'span'=16] {'span'}, dimensions={0} | all-to-all | bytes 3145728 | tf_op jit(solution)/shard_map/all_to_all | solution.py:29
  77.2 14.5 %all-to-all-start.2 = ((bf16[32,32,256]{2,1,0:T(8,128)(2,1)}), bf16[32,32,256]{2,1,0:T(8,128)(2,1)S(1)}, u32[]{:S(2)}, u32[]{:S(2)}) async-start(bf16[32,32,256]{2,1,0:T(8,128)(2,1)} %get-tuple-element.5), calls=%async_computation.2 | async-start | bytes 1048576 | tf_op jit(solution)/shard_map/all_to_all | solution.py:29
  91.6 0.2 convert_reduce_fusion
  91.9 3.4 %collective-permute-start.2 = (f32[64,256]{1,0:T(8,128)S(1)}, f32[64,256]{1,0:T(8,128)S(1)}, u32[]{:S(2)}, u32[]{:S(2)}) collective-permute-start(f32[64,256]{1,0:T(8,128)S(1)} %get-tuple-element.6), channel_id=1, source_target_pairs={{0,16},{16,32},{32,48},{48,64},{64,80},{80,96},{96,112},{112,128},... | collective-permute-start | bytes 196616 | tf_op jit(solution)/shard_map/ppermute | solution.py:25
  95.2 3.4 %collective-permute-start.3 = (f32[64,256]{1,0:T(8,128)S(1)}, f32[64,256]{1,0:T(8,128)S(1)}, u32[]{:S(2)}, u32[]{:S(2)}) collective-permute-start(f32[64,256]{1,0:T(8,128)S(1)} %get-tuple-element.7), channel_id=1, source_target_pairs={{0,32},{16,48},{32,64},{48,80},{64,96},{80,112},{96,128},{112,144}... | collective-permute-start | bytes 196616 | tf_op jit(solution)/shard_map/ppermute | solution.py:25
  98.6 16.0 %collective-permute-done.2 = f32[64,256]{1,0:T(8,128)S(1)} collective-permute-done((f32[64,256]{1,0:T(8,128)S(1)}, f32[64,256]{1,0:T(8,128)S(1)}, u32[]{:S(2)}, u32[]{:S(2)}) %collective-permute-start.2) | collective-permute-done | bytes 65568 | tf_op jit(solution)/shard_map/ppermute | solution.py:25
  114.6 5.1 %collective-permute-done.3 = f32[64,256]{1,0:T(8,128)S(1)} collective-permute-done((f32[64,256]{1,0:T(8,128)S(1)}, f32[64,256]{1,0:T(8,128)S(1)}, u32[]{:S(2)}, u32[]{:S(2)}) %collective-permute-start.3) | collective-permute-done | bytes 65568 | tf_op jit(solution)/shard_map/ppermute | solution.py:25
  119.6 0.6 fusion
  120.3 4.2 %all-to-all-done.2 = bf16[32,32,256]{2,1,0:T(8,128)(2,1)S(1)} async-done(((bf16[32,32,256]{2,1,0:T(8,128)(2,1)}), bf16[32,32,256]{2,1,0:T(8,128)(2,1)S(1)}, u32[]{:S(2)}, u32[]{:S(2)}) %all-to-all-start.2) | async-done | bytes 524320 | tf_op jit(solution)/shard_map/all_to_all | solution.py:29
  124.5 0.7 convert_reduce_fusion.1
  (1 shorter events, 0.0 us)
Async XLA Ops:
  0.6 32.5 %collective-permute-start = (bf16[1024,256]{1,0:T(8,128)(2,1)}, bf16[1024,256]{1,0:T(8,128)(2,1)S(1)}, u32[]{:S(2)}, u32[]{:S(2)}) collective-permute-start(bf16[1024,256]{1,0:T(8,128)(2,1)} %refs_0_.1), channel_id=1, source_target_pairs={{0,496},{16,0},{32,16},{48,32},{64,48},{80,64},{96,80},{112,96},{1... | collective-permute-start | bytes 1572872 | tf_op jit(solution)/shard_map/ppermute | solution.py:25
  3.8 29.4 %collective-permute-start.1 = (bf16[1024,256]{1,0:T(8,128)(2,1)}, bf16[1024,256]{1,0:T(8,128)(2,1)S(1)}, u32[]{:S(2)}, u32[]{:S(2)}) collective-permute-start(bf16[1024,256]{1,0:T(8,128)(2,1)} %refs_0_.1), channel_id=1, source_target_pairs={{0,480},{16,496},{32,0},{48,16},{64,32},{80,48},{96,64},{112,80},{... | collective-permute-start | bytes 1572872 | tf_op jit(solution)/shard_map/ppermute | solution.py:25
  20.9 12.3 %all-to-all-start = ((s32[16,32,128]{2,1,0:T(8,128)}), s32[16,32,128]{2,1,0:T(8,128)S(1)}, u32[]{:S(2)}, u32[]{:S(2)}) async-start(s32[16,32,128]{2,1,0:T(8,128)} %pack_lists.1), calls=%async_computation | async-start | bytes 524288 | tf_op jit(solution)/shard_map/all_to_all | solution.py:29
  33.2 1.0 copy-start
  34.2 1.0 copy-start.1
  77.2 47.4 %all-to-all-start.2 = ((bf16[32,32,256]{2,1,0:T(8,128)(2,1)}), bf16[32,32,256]{2,1,0:T(8,128)(2,1)S(1)}, u32[]{:S(2)}, u32[]{:S(2)}) async-start(bf16[32,32,256]{2,1,0:T(8,128)(2,1)} %get-tuple-element.5), calls=%async_computation.2 | async-start | bytes 1048576 | tf_op jit(solution)/shard_map/all_to_all | solution.py:29
  91.9 22.7 %collective-permute-start.2 = (f32[64,256]{1,0:T(8,128)S(1)}, f32[64,256]{1,0:T(8,128)S(1)}, u32[]{:S(2)}, u32[]{:S(2)}) collective-permute-start(f32[64,256]{1,0:T(8,128)S(1)} %get-tuple-element.6), channel_id=1, source_target_pairs={{0,16},{16,32},{32,48},{48,64},{64,80},{80,96},{96,112},{112,128},... | collective-permute-start | bytes 196616 | tf_op jit(solution)/shard_map/ppermute | solution.py:25
  95.2 24.4 %collective-permute-start.3 = (f32[64,256]{1,0:T(8,128)S(1)}, f32[64,256]{1,0:T(8,128)S(1)}, u32[]{:S(2)}, u32[]{:S(2)}) collective-permute-start(f32[64,256]{1,0:T(8,128)S(1)} %get-tuple-element.7), channel_id=1, source_target_pairs={{0,32},{16,48},{32,64},{48,80},{64,96},{80,112},{96,128},{112,144}... | collective-permute-start | bytes 196616 | tf_op jit(solution)/shard_map/ppermute | solution.py:25

commit v2 on v1

v2 whole, which is shorter than its diff:
```python
import functools

import jax
import jax.numpy as jnp
from jax import lax
from jax.experimental import pallas as pl
from jax.experimental.pallas import tpu as pltpu
from jax.sharding import PartitionSpec as P

BF = jnp.bfloat16
F32 = jnp.float32
NT = (((1,), (1,)), ((), ()))
TN = (((0,), (0,)), ((), ()))
VMEM = pl.BlockSpec(memory_space=pltpu.VMEM)
SMEM = pl.BlockSpec(memory_space=pltpu.SMEM)


def dot(a, b, dims=(((1,), (0,)), ((), ()))):
    return lax.dot_general(a, b, dims, preferred_element_type=F32)


def passed_along(value, axis, steps):
    count = lax.axis_size(axis)
    pairs = [(source, (source + steps) % count) for source in range(count)]
    return lax.ppermute(value, axis, pairs)


def exchanged(value, axis):
    return lax.all_to_all(value, axis, split_axis=0, concat_axis=0, tiled=True)


def iota(shape, axis):
    return lax.broadcasted_iota(jnp.int32, shape, axis)


def pack_kernel(buckets, groups, neg_ref, left_ref, right_ref, count_ref, out_ref):
    hist_rows = 8 * buckets
    for s in range(buckets):
        high, low = [], []
        for q in range(neg_ref.shape[1]):
            row = neg_ref[s, q : q + 1, :]
            high.append((iota((16, 128), 0) == (row >> 7)).astype(F32).astype(BF))
            low.append((iota((128, 128), 0) == (row & 127)).astype(F32).astype(BF))
        hist = dot(jnp.concatenate(high, 1), jnp.concatenate(low, 1), NT)[:8].astype(jnp.int32)
        for d in range(groups):
            out_ref[d, 8 * s : 8 * s + 8, :] = hist
    lines = left_ref.shape[1]
    rest = jnp.zeros((8 - 2 * buckets, 128), jnp.int32)
    counts = [count_ref[s] for s in range(buckets)]
    counts = jnp.concatenate(counts, 0)
    counts = jnp.concatenate([counts, jnp.zeros((buckets, 128 - counts.shape[1]), jnp.int32)], 1)
    for line in range(lines):
        pairs = [
            left_ref[s, line : line + 1, :] + (right_ref[s, line : line + 1, :] << 16)
            for s in range(buckets)
        ]
        block = jnp.concatenate(pairs + [counts, rest], 0)
        for d in range(line * groups // lines, (line + 1) * groups // lines):
            out_ref[d, hist_rows : hist_rows + 8, :] = block


def one_hot(rows, at, shape):
    return ((iota(shape, 0) + at) == rows).astype(F32).astype(BF)


def spread_counts(hist, groups, mult_ref, a):
    hist = jnp.broadcast_to(hist[:, None, :], (groups, 8, 128)).reshape(128, 128)
    mult_ref[128 * a : 128 * (a + 1), :] = hist.T


def forward_kernel(buckets, neg_scale, me_ref, x_ref, *refs):
    slab_refs = refs[:buckets]
    ops_ref = refs[buckets]
    rel_ref, qg_ref, lrow_ref = refs[buckets + 1 : buckets + 4]
    pk_refs = refs[buckets + 4 : 2 * buckets + 4]
    rel_acc, et0_ref, et_ref, oh_ref, whi_ref, wlo_ref, mult_ref = refs[2 * buckets + 4 :]
    rel_own, width, _ = ops_ref.shape
    groups = x_ref.shape[0]
    part_rows = slab_refs[0].shape[0]
    slots = rel_own * 128
    chunk = 256
    chunks = part_rows // chunk
    hist_rows = 8 * buckets
    me = me_ref[0]

    lane_row = iota((128, slots), 0)
    lane = iota((128, slots), 1)
    relation, slot = lane >> 7, lane & 7
    per_line = 128 // (8 * rel_own)
    pick_slot = (lane_row == (me % per_line) * (8 * rel_own) + relation * 8 + slot)
    pick_slot = pick_slot.astype(F32).astype(BF)
    pick_count = (lane_row == me * rel_own + relation).astype(F32).astype(BF)
    lane = iota((groups, slots), 1)
    own_group = iota((groups, slots), 0) == ((lane >> 3) & (groups - 1))
    slot_row = iota((1, slots), 1) & 7

    def own(values):
        return jnp.sum(jnp.where(own_group, values, 0.0), axis=0, keepdims=True)

    def narrow(values):
        return values.astype(F32).astype(BF)

    et0_ref[...] = slab_refs[0][...].T
    for s in range(buckets):
        slab, pk = slab_refs[s], pk_refs[s]
        pair = x_ref[:, hist_rows + s, :]
        left, right = pair & 65535, pair >> 16
        parts = [left >> 5, left & 31, right >> 5, right & 31]
        parts = dot(narrow(jnp.concatenate(parts, 0)), pick_slot)
        parts = [own(parts[groups * q : groups * (q + 1)]) for q in range(4)]
        left_row = (parts[0] * 32.0 + parts[1]).astype(jnp.int32)
        right_row = (parts[2] * 32.0 + parts[3]).astype(jnp.int32)
        count_row = own(dot(narrow(x_ref[:, hist_rows + buckets + s, :]), pick_count))
        live = (count_row.astype(jnp.int32) > slot_row).astype(F32)
        lrow_ref[s : s + 1, :] = left_row

        highs, lows = [], []
        for a in range(8):
            hist = x_ref[:, 8 * s + a, :]
            highs.append(hist >> 5)
            lows.append(hist & 31)
            spread_counts(hist.astype(F32), groups, mult_ref, a)
        for q, group in enumerate([highs[:4], highs[4:], lows[:4], lows[4:]]):
            at = width + 16 * q
            pk[at : at + 16, :] = narrow(jnp.concatenate(group, 1))

        if s == 0:
            slab_t = et0_ref
        else:
            et_ref[...] = slab[...].T
            slab_t = et_ref

        def left_hot(n, carry):
            at = pl.multiple_of(n * chunk, chunk)
            oh_ref[pl.ds(at, chunk), :] = one_hot(left_row, n * chunk, (chunk, slots))
            return carry

        def right_hot(n, carry):
            at = pl.multiple_of(n * chunk, chunk)
            oh_ref[pl.ds(at, chunk), :] = one_hot(right_row, n * chunk, (chunk, slots))
            return carry

        lax.fori_loop(0, chunks, left_hot, 0)
        left_t = dot(et0_ref[...], oh_ref[...]).astype(BF)
        query_t = jnp.concatenate(
            [dot(ops_ref[i], left_t[:, 128 * i : 128 * (i + 1)], TN) for i in range(rel_own)], 1
        ).astype(BF)
        pk[0:width, :] = query_t
        half_t = query_t * 0.5
        lax.fori_loop(0, chunks, right_hot, 0)
        right_t = dot(slab_t[...], oh_ref[...])
        positive = jnp.sum(query_t.astype(F32) * right_t, axis=0, keepdims=True)
        pos_grad = -live * jax.nn.sigmoid(-positive)
        pos_high = pos_grad.astype(BF)
        pos_low = (pos_grad - pos_high.astype(F32)).astype(BF)
        misc = [narrow(parts[2]), narrow(parts[3]), narrow(live), pos_high, pos_low]
        misc = [row.astype(F32) for row in misc] + [jnp.zeros((11, slots), F32)]
        pk[width + 64 : width + 80, :] = jnp.concatenate(misc, 0).astype(BF)
        factor = live * (0.5 * neg_scale)

        def weigh(n, carry):
            at = pl.multiple_of(n * chunk, chunk)
            level = jnp.tanh(dot(slab[pl.ds(at, chunk), :], half_t))
            ngrad = (level * factor + factor).astype(BF).astype(F32)
            mult = mult_ref[pl.ds(at, chunk), :]
            weight = ngrad * jnp.concatenate([mult] * rel_own, 1)
            high = weight.astype(BF)
            whi_ref[pl.ds(at, chunk), :] = high
            wlo_ref[pl.ds(at, chunk), :] = (weight - high.astype(F32)).astype(BF)
            return carry

        lax.fori_loop(0, chunks, weigh, 0)
        qgrad_t = dot(slab_t[...], whi_ref[...]) + dot(slab_t[...], wlo_ref[...])
        qgrad_t = (qgrad_t + right_t * pos_grad).astype(BF)
        qg_ref[s] = qgrad_t
        for i in range(rel_own):
            cols = slice(128 * i, 128 * (i + 1))
            outer = dot(left_t[:, cols], qgrad_t[:, cols], NT)
            rel_acc[i] = outer if s == 0 else rel_acc[i] + outer

    doms, held, _ = rel_ref.shape
    held = held // rel_own
    for d in range(doms):
        block = [rel_acc[i, held * d : held * (d + 1), :] for i in range(rel_own)]
        rel_ref[d] = jnp.concatenate(block, 0).astype(BF)


def entity_kernel(buckets, neg_scale, groups, me_ref, slab_ref, ops_ref, qg_ref, lrow_ref, *refs):
    pk_refs = refs[:buckets]
    keep_ref, send_ref, rows_ref, mult_ref = refs[buckets:]
    me = me_ref[0]
    rel_own, width, _ = ops_ref.shape
    part_rows = slab_ref.shape[0]
    slots = rel_own * 128
    chunk = 256
    chunks = part_rows // chunk
    share = part_rows // groups
    for s in range(buckets):
        pk = pk_refs[s]
        left_row = lrow_ref[s : s + 1, :]
        qgrad_t = qg_ref[s]
        lgrad_t = jnp.concatenate(
            [dot(ops_ref[i], qgrad_t[:, 128 * i : 128 * (i + 1)]) for i in range(rel_own)], 1
        ).astype(BF)
        hist = pk[width : width + 64, :].astype(F32)
        hist = hist[:32] * 32.0 + hist[32:]
        for a in range(8):
            cols = slice(128 * (a % 4), 128 * (a % 4 + 1))
            spread_counts(hist[16 * (a // 4) : 16 * (a // 4 + 1), cols], groups, mult_ref, a)
        misc = pk[width + 64 : width + 80, :].astype(F32)
        right_row = (misc[0:1] * 32.0 + misc[1:2]).astype(jnp.int32)
        factor = misc[2:3] * (0.5 * neg_scale)
        pos_grad = misc[3:4] + misc[4:5]
        query_t = pk[0:width, :]
        half_t = query_t * 0.5

        def weigh(n, carry):
            at = pl.multiple_of(n * chunk, chunk)
            level = jnp.tanh(dot(slab_ref[pl.ds(at, chunk), :], half_t))
            ngrad = (level * factor + factor).astype(BF).astype(F32)
            mult = mult_ref[pl.ds(at, chunk), :]
            hit = (iota((chunk, slots), 0) + n * chunk) == right_row
            weight = ngrad * jnp.concatenate([mult] * rel_own, 1) + jnp.where(hit, pos_grad, 0.0)
            high = weight.astype(BF)
            low = (weight - high.astype(F32)).astype(BF)
            hot = one_hot(left_row, n * chunk, (chunk, slots))
            rows = dot(high, query_t, NT) + dot(low, query_t, NT) + dot(hot, lgrad_t, NT)
            rows_ref[pl.ds(at, chunk), :] = rows if s == 0 else rows_ref[pl.ds(at, chunk), :] + rows
            return carry

        lax.fori_loop(0, chunks, weigh, 0)
    core, y, x = me & 1, (me >> 1) & 1, me >> 2
    pair, mirror = (x ^ (x >> 1)) & 1, x >> 1
    for n in range(groups):
        to_pair, to_mirror = pair ^ ((n >> 2) & 1), mirror ^ ((n >> 1) & 1)
        to_x = to_pair + to_mirror * (3 - 2 * to_pair)
        to = 4 * to_x + 2 * (y ^ (n & 1)) + (core ^ (n >> 3))
        block = rows_ref[pl.ds(pl.multiple_of(to * share, share), share), :]
        half = groups // 2
        if n < half:
            keep_ref[n] = block
        else:
            send_ref[n - half] = block


def shards(entities, operators, left_rows, right_rows, negatives, counts):
    buckets = left_rows.shape[0]
    slot_count = left_rows.shape[-1]
    neg_count = negatives.shape[-1]
    groups = lax.axis_size("span")
    doms = lax.axis_size("dom")
    rel_own = operators.shape[0]
    relations = rel_own * groups
    part_rows, width = entities.shape
    neg_scale = float(neg_count) ** (-0.5)
    share = part_rows // groups
    slots = rel_own * 128
    limit = pltpu.CompilerParams(vmem_limit_bytes=40 * 1024 * 1024)

    packed = pl.pallas_call(
        functools.partial(pack_kernel, buckets, groups),
        out_shape=jax.ShapeDtypeStruct((groups, 8 * buckets + 8, 128), jnp.int32),
        in_specs=[VMEM] * 4,
        out_specs=VMEM,
        name="pack_lists",
    )(
        negatives.reshape(buckets, neg_count // 128, 128),
        left_rows.reshape(buckets, slot_count // 128, 128),
        right_rows.reshape(buckets, slot_count // 128, 128),
        counts.reshape(buckets, 1, relations),
    )
    received = exchanged(packed, "span")
    slabs = [entities] + [passed_along(entities, "dom", -s) for s in range(1, buckets)]

    me = lax.axis_index("span").astype(jnp.int32).reshape(1)
    pack = jax.ShapeDtypeStruct((width + 80, slots), BF)
    wide = pltpu.VMEM((part_rows, slots), BF)
    rel_parts, qgrads, lrows, *packs = pl.pallas_call(
        functools.partial(forward_kernel, buckets, neg_scale),
        out_shape=[
            jax.ShapeDtypeStruct((doms, rel_own * width // doms, width), BF),
            jax.ShapeDtypeStruct((buckets, width, slots), BF),
            jax.ShapeDtypeStruct((8, slots), jnp.int32),
        ]
        + [pack] * buckets,
        in_specs=[SMEM] + [VMEM] * (buckets + 2),
        out_specs=[VMEM] * (buckets + 3),
        scratch_shapes=[
            pltpu.VMEM((rel_own, width, width), F32),
            pltpu.VMEM((width, part_rows), BF),
            pltpu.VMEM((width, part_rows), BF),
            wide,
            wide,
            wide,
            pltpu.VMEM((part_rows, 128), F32),
        ],
        compiler_params=limit,
        cost_estimate=pl.CostEstimate(
            flops=4_400_000_000, bytes_accessed=4_000_000, transcendentals=1_600_000
        ),
        name="query_gradients",
    )(me, received, *slabs, operators)
    packs = [packs[0]] + [passed_along(packs[s], "dom", s) for s in range(1, buckets)]
    rel_arrived = exchanged(rel_parts, "dom")

    half_parts = jax.ShapeDtypeStruct((groups // 2, share, width), F32)
    keep, send = pl.pallas_call(
        functools.partial(entity_kernel, buckets, neg_scale, groups),
        out_shape=(half_parts, half_parts),
        in_specs=[SMEM] + [VMEM] * (buckets + 4),
        out_specs=(VMEM, VMEM),
        scratch_shapes=[
            pltpu.VMEM((part_rows, width), F32),
            pltpu.VMEM((part_rows, 128), F32),
        ],
        compiler_params=limit,
        cost_estimate=pl.CostEstimate(
            flops=4_000_000_000, bytes_accessed=3_000_000, transcendentals=1_600_000
        ),
        name="entity_gradients",
    )(me, entities, operators, qgrads, lrows, *packs)
    for partner in (1, 4, 12, 2):
        got = lax.ppermute(send, "span", [(i, i ^ partner) for i in range(groups)])
        half = keep.shape[0] // 2
        if half:
            send, keep = keep[half:] + got[half:], keep[:half] + got[:half]
        else:
            entity_share = (keep + got).reshape(share, width)
    rel_share = jnp.sum(rel_arrived.astype(F32), axis=0)
    return (entity_share, rel_share.reshape(rel_own, width // doms, width))


def solution(mesh):
    in_specs = (
        P("dom", None),
        P("span", None, None),
        P(None, "dom", "span", None),
        P(None, "dom", "span", None),
        P(None, "dom", "span", None),
        P(None, "dom", "span", None),
    )
    out_specs = (P(("dom", "span"), None), P("span", "dom", None))
    return jax.shard_map(shards, mesh=mesh, in_specs=in_specs, out_specs=out_specs, check_vma=False)
```

time: 126 us -> 114 us (0.905)
  blocking collectives: 24.3 us -> 0 us
  starting transfers between devices: 41.5 us -> 55 us
  Pallas kernels: 19.3 us -> 23.4 us
  waiting for transfers between devices: 31.7 us -> 28.5 us
  local copies, waits for them, and re-layouts: 5.29 us -> 3.08 us
    all_to_all x1 -> x0, blocking collectives: 24.3 us -> none  [exchanged(): return lax.all_to_all(value, axis, split_axis=0, concat_axis=0, tiled=True)]
    ppermute x0 -> x4, waiting for transfers between devices: none -> 17.3 us  [shards(): got = lax.ppermute(send, 'span', [(i, i ^ partner) for i in range(groups)])]
    ppermute x4, waiting for transfers between devices: 21 us -> 4.7 us  [passed_along(): return lax.ppermute(value, axis, pairs)]
    ppermute x0 -> x4, starting transfers between devices: none -> 10.9 us  [shards(): got = lax.ppermute(send, 'span', [(i, i ^ partner) for i in range(groups)])]
    all_to_all x2, waiting for transfers between devices: 10.7 us -> 6.5 us  [exchanged(): return lax.all_to_all(value, axis, split_axis=0, concat_axis=0, tiled=True)]
    pallas_call x1 -> x2, Pallas kernels: 17.6 us -> 21.6 us  [the longest x1 13.4 us: shards(): pl.pallas_call(functools.partial(forward_kernel, buckets, neg_scale), out...]
    all_to_all x2, starting transfers between devices: 20.2 us -> 24.1 us  [exchanged(): return lax.all_to_all(value, axis, split_axis=0, concat_axis=0, tiled=True)]
    unnamed x6 -> x10, local copies, waits for them, and re-layouts: 4.67 us -> 3.08 us
  transfers between devices with their start and end apart: 6 -> 10, of which waited for: 4 -> 7; matrix products, arithmetic and copies ran while one was open for 4% -> 1% of each run, Pallas kernels for 1% -> 9%
where the time goes in v2:
time: 114 us; the launch traced here: 113 us
  starting transfers between devices  55 us (48%)
  waiting for transfers between devices  28.5 us (25%)
  Pallas kernels  23.4 us (21%)
  local copies, waits for them, and re-layouts  3.08 us (3%)
  other arithmetic  2.5 us (2%)
    all_to_all x2, starting transfers between devices, exchanged(): return lax.all_to_all(value, axis, split_axis=0, concat_axis=0, tiled=True)  24.1 us
    ppermute x4, starting transfers between devices, passed_along(): return lax.ppermute(value, axis, pairs)  20 us
    ppermute x4, waiting for transfers between devices, shards(): got = lax.ppermute(send, 'span', [(i, i ^ partner) for i in range(groups)])  17.3 us
    pallas_call x1, Pallas kernels, shards(): pl.pallas_call(functools.partial(forward_kernel, buckets, neg_scale), out...  13.4 us
    ppermute x4, starting transfers between devices, shards(): got = lax.ppermute(send, 'span', [(i, i ^ partner) for i in range(groups)])  10.9 us
    pallas_call x1, Pallas kernels, shards(): pl.pallas_call(functools.partial(entity_kernel, buckets, neg_scale, group...  8.21 us
    all_to_all x2, waiting for transfers between devices, exchanged(): return lax.all_to_all(value, axis, split_axis=0, concat_axis=0, tiled=True)  6.5 us
    ppermute x4, waiting for transfers between devices, passed_along(): return lax.ppermute(value, axis, pairs)  4.7 us
  transfers between devices with their start and end apart: 10, of which 7 were waited for; matrix products, arithmetic and copies ran while one was open for 1% of the time, Pallas kernels for 9%

profile of v2, /device:TPU:24, one launch (start us, length us, event | category | flops | bytes accessed | tf_op | source)
XLA Modules:
  0.0 113.2 jit_solution(12030117205264987521)
XLA Ops:
  0.6 0.0 copy-start
  0.6 11.5 %collective-permute-start.1 = (bf16[1024,256]{1,0:T(8,128)(2,1)}, bf16[1024,256]{1,0:T(8,128)(2,1)S(1)}, u32[]{:S(2)}, u32[]{:S(2)}) collective-permute-start(bf16[1024,256]{1,0:T(8,128)(2,1)} %slab_ref.1), channel_id=1, source_target_pairs={{0,480},{16,496},{32,0},{48,16},{64,32},{80,48},{96,64},{112,80},{... | collective-permute-start | bytes 1572872 | tf_op jit(solution)/shard_map/ppermute | solution.py:25
  12.2 3.1 %collective-permute-start = (bf16[1024,256]{1,0:T(8,128)(2,1)}, bf16[1024,256]{1,0:T(8,128)(2,1)S(1)}, u32[]{:S(2)}, u32[]{:S(2)}) collective-permute-start(bf16[1024,256]{1,0:T(8,128)(2,1)} %slab_ref.1), channel_id=1, source_target_pairs={{0,496},{16,0},{32,16},{48,32},{64,48},{80,64},{96,80},{112,96},{1... | collective-permute-start | bytes 1572872 | tf_op jit(solution)/shard_map/ppermute | solution.py:25
  15.3 1.8 %pack_lists.1 = s32[16,32,128]{2,1,0:T(8,128)} custom-call(s32[3,8,128]{2,1,0:T(8,128)} %bitcast.9, s32[3,4,128]{2,1,0:T(4,128)} %bitcast.10, s32[3,4,128]{2,1,0:T(4,128)} %bitcast.11, s32[3,1,64]{2,1,0:T(1,128)} %bitcast.12), custom_call_target="tpu_custom_call" | custom-call | tf_op jit(solution)/shard_map/pack_lists/pallas_call | solution.py:260
  17.1 5.8 %all-to-all-start = ((s32[16,32,128]{2,1,0:T(8,128)}), s32[16,32,128]{2,1,0:T(8,128)S(1)}, u32[]{:S(2)}, u32[]{:S(2)}) async-start(s32[16,32,128]{2,1,0:T(8,128)} %pack_lists.1), calls=%async_computation | async-start | bytes 524288 | tf_op jit(solution)/shard_map/all_to_all | solution.py:29
  22.9 6.5 %all-to-all-done.x_ref = s32[16,32,128]{2,1,0:T(8,128)S(1)} async-done(((s32[16,32,128]{2,1,0:T(8,128)}), s32[16,32,128]{2,1,0:T(8,128)S(1)}, u32[]{:S(2)}, u32[]{:S(2)}) %all-to-all-start) | async-done | bytes 262176 | tf_op jit(solution)/shard_map/all_to_all | solution.py:29
  29.4 0.0 collective-permute-done.1.refs_2_
  29.4 2.4 %collective-permute-done.refs_1_ = bf16[1024,256]{1,0:T(8,128)(2,1)S(1)} collective-permute-done((bf16[1024,256]{1,0:T(8,128)(2,1)}, bf16[1024,256]{1,0:T(8,128)(2,1)S(1)}, u32[]{:S(2)}, u32[]{:S(2)}) %collective-permute-start) | collective-permute-done | bytes 524320 | tf_op jit(solution)/shard_map/ppermute | solution.py:25
  31.7 0.0 copy-done
  31.7 0.0 copy-start.1
  31.7 1.0 copy-done.1
  32.8 13.4 %query_gradients.1 = (bf16[32,32,256]{2,1,0:T(8,128)(2,1)}, bf16[3,256,512]{2,1,0:T(8,128)(2,1)S(1)}, s32[8,512]{1,0:T(8,128)S(1)}, bf16[336,512]{1,0:T(8,128)(2...) custom-call(s32[1]{0:T(128)} %bitcast.me_ref, s32[16,32,128]{2,1,0:T(8,128)S(1)} %all-to-all-done.x_ref, ...), custom_call_target="tpu_custom_call" | custom-call | flops 4400000000 | bytes 4000000 | tf_op jit(solution)/shard_map/query_gradients/pallas_call | solution.py:278
  46.2 0.0 copy-start.3
  46.2 0.9 copy-done.3
  47.0 3.4 %collective-permute-start.2 = (bf16[336,512]{1,0:T(8,128)(2,1)S(1)}, bf16[336,512]{1,0:T(8,128)(2,1)S(1)}, u32[]{:S(2)}, u32[]{:S(2)}) collective-permute-start(bf16[336,512]{1,0:T(8,128)(2,1)S(1)} %get-tuple-element.13), channel_id=1, source_target_pairs={{0,16},{16,32},{32,48},{48,64},{64,80},{80,96},{96,112},{112,128},... | collective-permute-start | bytes 1032200 | tf_op jit(solution)/shard_map/ppermute | solution.py:25
  50.5 1.9 %collective-permute-start.3 = (bf16[336,512]{1,0:T(8,128)(2,1)S(1)}, bf16[336,512]{1,0:T(8,128)(2,1)S(1)}, u32[]{:S(2)}, u32[]{:S(2)}) collective-permute-start(bf16[336,512]{1,0:T(8,128)(2,1)S(1)} %get-tuple-element.14), channel_id=1, source_target_pairs={{0,32},{16,48},{32,64},{48,80},{64,96},{80,112},{96,128},{112,144}... | collective-permute-start | bytes 1032200 | tf_op jit(solution)/shard_map/ppermute | solution.py:25
  52.4 0.0 copy-start.2
  52.4 18.3 %all-to-all-start.1 = ((bf16[32,32,256]{2,1,0:T(8,128)(2,1)}), bf16[32,32,256]{2,1,0:T(8,128)(2,1)}, u32[]{:S(2)}, u32[]{:S(2)}) async-start(bf16[32,32,256]{2,1,0:T(8,128)(2,1)} %get-tuple-element.17), calls=%async_computation.1 | async-start | bytes 1048576 | tf_op jit(solution)/shard_map/all_to_all | solution.py:29
  70.7 0.0 collective-permute-done.2.refs_1_
  70.7 2.3 %collective-permute-done.3.refs_2_ = bf16[336,512]{1,0:T(8,128)(2,1)S(1)} collective-permute-done((bf16[336,512]{1,0:T(8,128)(2,1)S(1)}, bf16[336,512]{1,0:T(8,128)(2,1)S(1)}, u32[]{:S(2)}, u32[]{:S(2)}) %collective-permute-start.3) | collective-permute-done | bytes 344096 | tf_op jit(solution)/shard_map/ppermute | solution.py:25
  73.0 0.0 copy-done.2
  73.0 0.0 copy-start.4
  73.0 1.1 %copy-done.4 = bf16[3,256,512]{2,1,0:T(8,128)(2,1)S(1)} copy-done((bf16[3,256,512]{2,1,0:T(8,128)(2,1)S(1)}, bf16[3,256,512]{2,1,0:T(8,128)(2,1)}, u32[]{:S(2)}) %copy-start.4) | copy-done | bytes 786456
  74.2 8.2 %entity_gradients.1 = (f32[8,64,256]{2,1,0:T(8,128)S(1)}, f32[8,64,256]{2,1,0:T(8,128)S(1)}) custom-call(s32[1]{0:T(128)} %bitcast.me_ref, bf16[1024,256]{1,0:T(8,128)(2,1)S(1)} %copy-done, bf16[4,256,256]{2,1,0:T(8,128)(2,1)S(1)} %copy-done.2, bf16[3,256,512]{2,1,0:T(8,128)(2,1)S(1)} %copy-done.4, s32[8,512]{1,0:T(8,128)S(1)} %get-tuple-element.11.lrow_ref, ...), custom_call_target="tpu_custom_call" | custom-call | flops 4000000000 | bytes 3000000 | tf_op jit(solution)/shard_map/entity_gradients/pallas_call | solution.py:307
  82.4 1.9 %collective-permute-start.4 = (f32[8,64,256]{2,1,0:T(8,128)S(1)}, f32[8,64,256]{2,1,0:T(8,128)S(1)}, u32[]{:S(2)}, u32[]{:S(2)}) collective-permute-start(f32[8,64,256]{2,1,0:T(8,128)S(1)} %get-tuple-element.16), channel_id=1, source_target_pairs={{0,1},{1,0},{2,3},{3,2},{4,5},{5,4},{6,7},{7,6},{8,9},{9,8},{10,11... | collective-permute-start | bytes 1572872 | tf_op jit(solution)/shard_map/ppermute | solution.py:323
  84.3 1.9 %collective-permute-done.4 = f32[8,64,256]{2,1,0:T(8,128)S(1)} collective-permute-done((f32[8,64,256]{2,1,0:T(8,128)S(1)}, f32[8,64,256]{2,1,0:T(8,128)S(1)}, u32[]{:S(2)}, u32[]{:S(2)}) %collective-permute-start.4) | collective-permute-done | bytes 524320 | tf_op jit(solution)/shard_map/ppermute | solution.py:323
  86.2 0.1 slice_add_fusion.1
  86.3 3.1 %collective-permute-start.5 = (f32[4,64,256]{2,1,0:T(8,128)S(1)}, f32[4,64,256]{2,1,0:T(8,128)S(1)}, u32[]{:S(2)}, u32[]{:S(2)}) collective-permute-start(f32[4,64,256]{2,1,0:T(8,128)S(1)} %get-tuple-element.19), channel_id=1, source_target_pairs={{0,4},{1,5},{2,6},{3,7},{4,0},{5,1},{6,2},{7,3},{8,12},{9,13},{10,... | collective-permute-start | bytes 786440 | tf_op jit(solution)/shard_map/ppermute | solution.py:323
  89.3 7.2 %collective-permute-done.5 = f32[4,64,256]{2,1,0:T(8,128)S(1)} collective-permute-done((f32[4,64,256]{2,1,0:T(8,128)S(1)}, f32[4,64,256]{2,1,0:T(8,128)S(1)}, u32[]{:S(2)}, u32[]{:S(2)}) %collective-permute-start.5) | collective-permute-done | bytes 262176 | tf_op jit(solution)/shard_map/ppermute | solution.py:323
  96.6 4.0 %collective-permute-start.6 = (f32[2,64,256]{2,1,0:T(8,128)S(1)}, f32[2,64,256]{2,1,0:T(8,128)S(1)}, u32[]{:S(2)}, u32[]{:S(2)}) collective-permute-start(f32[2,64,256]{2,1,0:T(8,128)S(1)} %get-tuple-element.21), channel_id=1, source_target_pairs={{0,12},{1,13},{2,14},{3,15},{4,8},{5,9},{6,10},{7,11},{8,4},{9,5},... | collective-permute-start | bytes 393224 | tf_op jit(solution)/shard_map/ppermute | solution.py:323
  100.6 4.0 %collective-permute-done.6 = f32[2,64,256]{2,1,0:T(8,128)S(1)} collective-permute-done((f32[2,64,256]{2,1,0:T(8,128)S(1)}, f32[2,64,256]{2,1,0:T(8,128)S(1)}, u32[]{:S(2)}, u32[]{:S(2)}) %collective-permute-start.6) | collective-permute-done | bytes 131104 | tf_op jit(solution)/shard_map/ppermute | solution.py:323
  104.6 1.9 %collective-permute-start.7 = (f32[1,64,256]{2,1,0:T(8,128)S(1)}, f32[1,64,256]{2,1,0:T(8,128)S(1)}, u32[]{:S(2)}, u32[]{:S(2)}) collective-permute-start(f32[1,64,256]{2,1,0:T(8,128)S(1)} %slice_add_fusion.4), channel_id=1, source_target_pairs={{0,2},{1,3},{2,0},{3,1},{4,6},{5,7},{6,4},{7,5},{8,10},{9,11},{10,... | collective-permute-start | bytes 196616 | tf_op jit(solution)/shard_map/ppermute | solution.py:323
  106.6 4.2 %collective-permute-done.7 = f32[1,64,256]{2,1,0:T(8,128)S(1)} collective-permute-done((f32[1,64,256]{2,1,0:T(8,128)S(1)}, f32[1,64,256]{2,1,0:T(8,128)S(1)}, u32[]{:S(2)}, u32[]{:S(2)}) %collective-permute-start.7) | collective-permute-done | bytes 65568 | tf_op jit(solution)/shard_map/ppermute | solution.py:323
  110.8 0.6 fusion.1
  111.4 0.0 all-to-all-done.1
  111.4 1.7 %convert_reduce_fusion = f32[32,256]{1,0:T(8,128)} fusion(bf16[32,32,256]{2,1,0:T(8,128)(2,1)} %all-to-all-done.1), kind=kLoop, calls=%fused_computation | loop fusion | flops 516096 | bytes 557056 | tf_op jit(solution)/shard_map/reduce_sum | solution.py:329
  (2 shorter events, 0.0 us)
Async XLA Ops:
  0.6 31.1 %copy-start = (bf16[1024,256]{1,0:T(8,128)(2,1)S(1)}, bf16[1024,256]{1,0:T(8,128)(2,1)}, u32[]{:S(2)}) copy-start(bf16[1024,256]{1,0:T(8,128)(2,1)} %slab_ref.1) | copy-start | bytes 1572868
  0.6 28.7 %collective-permute-start.1 = (bf16[1024,256]{1,0:T(8,128)(2,1)}, bf16[1024,256]{1,0:T(8,128)(2,1)S(1)}, u32[]{:S(2)}, u32[]{:S(2)}) collective-permute-start(bf16[1024,256]{1,0:T(8,128)(2,1)} %slab_ref.1), channel_id=1, source_target_pairs={{0,480},{16,496},{32,0},{48,16},{64,32},{80,48},{96,64},{112,80},{... | collective-permute-start | bytes 1572872 | tf_op jit(solution)/shard_map/ppermute | solution.py:25
  12.2 19.6 %collective-permute-start = (bf16[1024,256]{1,0:T(8,128)(2,1)}, bf16[1024,256]{1,0:T(8,128)(2,1)S(1)}, u32[]{:S(2)}, u32[]{:S(2)}) collective-permute-start(bf16[1024,256]{1,0:T(8,128)(2,1)} %slab_ref.1), channel_id=1, source_target_pairs={{0,496},{16,0},{32,16},{48,32},{64,48},{80,64},{96,80},{112,96},{1... | collective-permute-start | bytes 1572872 | tf_op jit(solution)/shard_map/ppermute | solution.py:25
  17.1 12.3 %all-to-all-start = ((s32[16,32,128]{2,1,0:T(8,128)}), s32[16,32,128]{2,1,0:T(8,128)S(1)}, u32[]{:S(2)}, u32[]{:S(2)}) async-start(s32[16,32,128]{2,1,0:T(8,128)} %pack_lists.1), calls=%async_computation | async-start | bytes 524288 | tf_op jit(solution)/shard_map/all_to_all | solution.py:29
  31.7 1.0 copy-start.1
  46.2 0.9 copy-start.3
  47.0 23.6 %collective-permute-start.2 = (bf16[336,512]{1,0:T(8,128)(2,1)S(1)}, bf16[336,512]{1,0:T(8,128)(2,1)S(1)}, u32[]{:S(2)}, u32[]{:S(2)}) collective-permute-start(bf16[336,512]{1,0:T(8,128)(2,1)S(1)} %get-tuple-element.13), channel_id=1, source_target_pairs={{0,16},{16,32},{32,48},{48,64},{64,80},{80,96},{96,112},{112,128},... | collective-permute-start | bytes 1032200 | tf_op jit(solution)/shard_map/ppermute | solution.py:25
  50.5 22.6 %collective-permute-start.3 = (bf16[336,512]{1,0:T(8,128)(2,1)S(1)}, bf16[336,512]{1,0:T(8,128)(2,1)S(1)}, u32[]{:S(2)}, u32[]{:S(2)}) collective-permute-start(bf16[336,512]{1,0:T(8,128)(2,1)S(1)} %get-tuple-element.14), channel_id=1, source_target_pairs={{0,32},{16,48},{32,64},{48,80},{64,96},{80,112},{96,128},{112,144}... | collective-permute-start | bytes 1032200 | tf_op jit(solution)/shard_map/ppermute | solution.py:25
  52.4 20.6 %copy-start.2 = (bf16[4,256,256]{2,1,0:T(8,128)(2,1)S(1)}, bf16[4,256,256]{2,1,0:T(8,128)(2,1)}, u32[]{:S(2)}) copy-start(bf16[4,256,256]{2,1,0:T(8,128)(2,1)} %ops_ref.1) | copy-start | bytes 1572868
  52.4 59.0 %all-to-all-start.1 = ((bf16[32,32,256]{2,1,0:T(8,128)(2,1)}), bf16[32,32,256]{2,1,0:T(8,128)(2,1)}, u32[]{:S(2)}, u32[]{:S(2)}) async-start(bf16[32,32,256]{2,1,0:T(8,128)(2,1)} %get-tuple-element.17), calls=%async_computation.1 | async-start | bytes 1048576 | tf_op jit(solution)/shard_map/all_to_all | solution.py:29
  73.0 1.1 %copy-start.4 = (bf16[3,256,512]{2,1,0:T(8,128)(2,1)S(1)}, bf16[3,256,512]{2,1,0:T(8,128)(2,1)}, u32[]{:S(2)}) copy-start(bf16[3,256,512]{2,1,0:T(8,128)(2,1)} %copy-done.3) | copy-start | bytes 2359300
  82.4 3.8 %collective-permute-start.4 = (f32[8,64,256]{2,1,0:T(8,128)S(1)}, f32[8,64,256]{2,1,0:T(8,128)S(1)}, u32[]{:S(2)}, u32[]{:S(2)}) collective-permute-start(f32[8,64,256]{2,1,0:T(8,128)S(1)} %get-tuple-element.16), channel_id=1, source_target_pairs={{0,1},{1,0},{2,3},{3,2},{4,5},{5,4},{6,7},{7,6},{8,9},{9,8},{10,11... | collective-permute-start | bytes 1572872 | tf_op jit(solution)/shard_map/ppermute | solution.py:323
  86.3 10.2 %collective-permute-start.5 = (f32[4,64,256]{2,1,0:T(8,128)S(1)}, f32[4,64,256]{2,1,0:T(8,128)S(1)}, u32[]{:S(2)}, u32[]{:S(2)}) collective-permute-start(f32[4,64,256]{2,1,0:T(8,128)S(1)} %get-tuple-element.19), channel_id=1, source_target_pairs={{0,4},{1,5},{2,6},{3,7},{4,0},{5,1},{6,2},{7,3},{8,12},{9,13},{10,... | collective-permute-start | bytes 786440 | tf_op jit(solution)/shard_map/ppermute | solution.py:323
  96.6 8.1 %collective-permute-start.6 = (f32[2,64,256]{2,1,0:T(8,128)S(1)}, f32[2,64,256]{2,1,0:T(8,128)S(1)}, u32[]{:S(2)}, u32[]{:S(2)}) collective-permute-start(f32[2,64,256]{2,1,0:T(8,128)S(1)} %get-tuple-element.21), channel_id=1, source_target_pairs={{0,12},{1,13},{2,14},{3,15},{4,8},{5,9},{6,10},{7,11},{8,4},{9,5},... | collective-permute-start | bytes 393224 | tf_op jit(solution)/shard_map/ppermute | solution.py:323
  104.6 6.2 %collective-permute-start.7 = (f32[1,64,256]{2,1,0:T(8,128)S(1)}, f32[1,64,256]{2,1,0:T(8,128)S(1)}, u32[]{:S(2)}, u32[]{:S(2)}) collective-permute-start(f32[1,64,256]{2,1,0:T(8,128)S(1)} %slice_add_fusion.4), channel_id=1, source_target_pairs={{0,2},{1,3},{2,0},{3,1},{4,6},{5,7},{6,4},{7,5},{8,10},{9,11},{10,... | collective-permute-start | bytes 196616 | tf_op jit(solution)/shard_map/ppermute | solution.py:323

commit v3 on v2

--- a/solution.py
+++ b/solution.py
@@ -59,6 +59,12 @@
             out_ref[d, hist_rows : hist_rows + 8, :] = block
 
 
+def loop(n, step, carry):
+    for i in range(n):
+        carry = step(i, carry)
+    return carry
+
+
 def one_hot(rows, at, shape):
     return ((iota(shape, 0) + at) == rows).astype(F32).astype(BF)
 
@@ -68,12 +74,22 @@
     mult_ref[128 * a : 128 * (a + 1), :] = hist.T
 
 
-def forward_kernel(buckets, neg_scale, me_ref, x_ref, *refs):
-    slab_refs = refs[:buckets]
-    ops_ref = refs[buckets]
-    rel_ref, qg_ref, lrow_ref = refs[buckets + 1 : buckets + 4]
-    pk_refs = refs[buckets + 4 : 2 * buckets + 4]
-    rel_acc, et0_ref, et_ref, oh_ref, whi_ref, wlo_ref, mult_ref = refs[2 * buckets + 4 :]
+def forward_kernel(buckets, which, neg_scale, me_ref, x_ref, *refs):
+    first = which[0] == 0
+    many = len(which)
+    slab_refs, ops_ref = refs[:many], refs[many]
+    refs = refs[many + 1 :]
+    if first:
+        rel_acc, et0_ref = refs[:2]
+        refs = refs[2:]
+    else:
+        et0_ref, sum_ref, rel_ref = refs[:3]
+        refs = refs[3:]
+    qg_ref, lrow_ref = refs[:2]
+    pk_refs, refs = refs[2 : many + 2], refs[many + 2 :]
+    oh_ref, whi_ref, wlo_ref, mult_ref = refs[:4]
+    if not first:
+        rel_acc, et_ref = refs[4:]
     rel_own, width, _ = ops_ref.shape
     groups = x_ref.shape[0]
     part_rows = slab_refs[0].shape[0]
@@ -100,9 +116,8 @@
     def narrow(values):
         return values.astype(F32).astype(BF)
 
-    et0_ref[...] = slab_refs[0][...].T
-    for s in range(buckets):
-        slab, pk = slab_refs[s], pk_refs[s]
+    for at_call, s in enumerate(which):
+        slab, pk = slab_refs[at_call], pk_refs[at_call]
         pair = x_ref[:, hist_rows + s, :]
         left, right = pair & 65535, pair >> 16
         parts = [left >> 5, left & 31, right >> 5, right & 31]
@@ -112,7 +127,7 @@
         right_row = (parts[2] * 32.0 + parts[3]).astype(jnp.int32)
         count_row = own(dot(narrow(x_ref[:, hist_rows + buckets + s, :]), pick_count))
         live = (count_row.astype(jnp.int32) > slot_row).astype(F32)
-        lrow_ref[s : s + 1, :] = left_row
+        lrow_ref[at_call : at_call + 1, :] = left_row
 
         highs, lows = [], []
         for a in range(8):
@@ -124,30 +139,27 @@
             at = width + 16 * q
             pk[at : at + 16, :] = narrow(jnp.concatenate(group, 1))
 
-        if s == 0:
-            slab_t = et0_ref
-        else:
-            et_ref[...] = slab[...].T
-            slab_t = et_ref
+        slab_t = et0_ref if first else et_ref
+        slab_t[...] = slab[...].T
 
         def left_hot(n, carry):
-            at = pl.multiple_of(n * chunk, chunk)
+            at = n * chunk
             oh_ref[pl.ds(at, chunk), :] = one_hot(left_row, n * chunk, (chunk, slots))
             return carry
 
         def right_hot(n, carry):
-            at = pl.multiple_of(n * chunk, chunk)
+            at = n * chunk
             oh_ref[pl.ds(at, chunk), :] = one_hot(right_row, n * chunk, (chunk, slots))
             return carry
 
-        lax.fori_loop(0, chunks, left_hot, 0)
+        loop(chunks, left_hot, 0)
         left_t = dot(et0_ref[...], oh_ref[...]).astype(BF)
         query_t = jnp.concatenate(
             [dot(ops_ref[i], left_t[:, 128 * i : 128 * (i + 1)], TN) for i in range(rel_own)], 1
         ).astype(BF)
         pk[0:width, :] = query_t
         half_t = query_t * 0.5
-        lax.fori_loop(0, chunks, right_hot, 0)
+        loop(chunks, right_hot, 0)
         right_t = dot(slab_t[...], oh_ref[...])
         positive = jnp.sum(query_t.astype(F32) * right_t, axis=0, keepdims=True)
         pos_grad = -live * jax.nn.sigmoid(-positive)
@@ -159,7 +171,7 @@
         factor = live * (0.5 * neg_scale)
 
         def weigh(n, carry):
-            at = pl.multiple_of(n * chunk, chunk)
+            at = n * chunk
             level = jnp.tanh(dot(slab[pl.ds(at, chunk), :], half_t))
             ngrad = (level * factor + factor).astype(BF).astype(F32)
             mult = mult_ref[pl.ds(at, chunk), :]
@@ -169,15 +181,22 @@
             wlo_ref[pl.ds(at, chunk), :] = (weight - high.astype(F32)).astype(BF)
             return carry
 
-        lax.fori_loop(0, chunks, weigh, 0)
+        loop(chunks, weigh, 0)
         qgrad_t = dot(slab_t[...], whi_ref[...]) + dot(slab_t[...], wlo_ref[...])
         qgrad_t = (qgrad_t + right_t * pos_grad).astype(BF)
-        qg_ref[s] = qgrad_t
+        qg_ref[at_call] = qgrad_t
         for i in range(rel_own):
             cols = slice(128 * i, 128 * (i + 1))
             outer = dot(left_t[:, cols], qgrad_t[:, cols], NT)
-            rel_acc[i] = outer if s == 0 else rel_acc[i] + outer
-
+            if first:
+                rel_acc[i] = outer
+            elif at_call == 0:
+                rel_acc[i] = sum_ref[i] + outer
+            else:
+                rel_acc[i] = rel_acc[i] + outer
+
+    if first:
+        return
     doms, held, _ = rel_ref.shape
     held = held // rel_own
     for d in range(doms):
@@ -185,9 +204,10 @@
         rel_ref[d] = jnp.concatenate(block, 0).astype(BF)
 
 
-def entity_kernel(buckets, neg_scale, groups, me_ref, slab_ref, ops_ref, qg_ref, lrow_ref, *refs):
-    pk_refs = refs[:buckets]
-    keep_ref, send_ref, rows_ref, mult_ref = refs[buckets:]
+def entity_kernel(buckets, neg_scale, groups, me_ref, slab_ref, ops_ref, *refs):
+    qg0_ref, lrow0_ref, qg_ref, lrow_ref = refs[:4]
+    pk_refs = refs[4 : 4 + buckets]
+    keep_ref, send_ref, rows_ref, mult_ref = refs[4 + buckets :]
     me = me_ref[0]
     rel_own, width, _ = ops_ref.shape
     part_rows = slab_ref.shape[0]
@@ -197,8 +217,8 @@
     share = part_rows // groups
     for s in range(buckets):
         pk = pk_refs[s]
-        left_row = lrow_ref[s : s + 1, :]
-        qgrad_t = qg_ref[s]
+        left_row = lrow_ref[s - 1 : s, :] if s else lrow0_ref[0:1, :]
+        qgrad_t = qg_ref[s - 1] if s else qg0_ref[0]
         lgrad_t = jnp.concatenate(
             [dot(ops_ref[i], qgrad_t[:, 128 * i : 128 * (i + 1)]) for i in range(rel_own)], 1
         ).astype(BF)
@@ -215,7 +235,7 @@
         half_t = query_t * 0.5
 
         def weigh(n, carry):
-            at = pl.multiple_of(n * chunk, chunk)
+            at = n * chunk
             level = jnp.tanh(dot(slab_ref[pl.ds(at, chunk), :], half_t))
             ngrad = (level * factor + factor).astype(BF).astype(F32)
             mult = mult_ref[pl.ds(at, chunk), :]
@@ -228,13 +248,9 @@
             rows_ref[pl.ds(at, chunk), :] = rows if s == 0 else rows_ref[pl.ds(at, chunk), :] + rows
             return carry
 
-        lax.fori_loop(0, chunks, weigh, 0)
-    core, y, x = me & 1, (me >> 1) & 1, me >> 2
-    pair, mirror = (x ^ (x >> 1)) & 1, x >> 1
+        loop(chunks, weigh, 0)
     for n in range(groups):
-        to_pair, to_mirror = pair ^ ((n >> 2) & 1), mirror ^ ((n >> 1) & 1)
-        to_x = to_pair + to_mirror * (3 - 2 * to_pair)
-        to = 4 * to_x + 2 * (y ^ (n & 1)) + (core ^ (n >> 3))
+        to = me ^ (((n >> 1) & 3) * 4 + (n & 1) * 2 + (n >> 3))
         block = rows_ref[pl.ds(pl.multiple_of(to * share, share), share), :]
         half = groups // 2
         if n < half:
@@ -255,7 +271,7 @@
     neg_scale = float(neg_count) ** (-0.5)
     share = part_rows // groups
     slots = rel_own * 128
-    limit = pltpu.CompilerParams(vmem_limit_bytes=40 * 1024 * 1024)
+    limit = pltpu.CompilerParams(vmem_limit_bytes=24 * 1024 * 1024)
 
     packed = pl.pallas_call(
         functools.partial(pack_kernel, buckets, groups),
@@ -273,41 +289,54 @@
     slabs = [entities] + [passed_along(entities, "dom", -s) for s in range(1, buckets)]
 
     me = lax.axis_index("span").astype(jnp.int32).reshape(1)
-    pack = jax.ShapeDtypeStruct((width + 80, slots), BF)
     wide = pltpu.VMEM((part_rows, slots), BF)
-    rel_parts, qgrads, lrows, *packs = pl.pallas_call(
-        functools.partial(forward_kernel, buckets, neg_scale),
+    scratch = [wide, wide, wide, pltpu.VMEM((part_rows, 128), F32)]
+
+    def packs_of(many):
+        return [
+            jax.ShapeDtypeStruct((many, width, slots), BF),
+            jax.ShapeDtypeStruct((8, slots), jnp.int32),
+        ] + [jax.ShapeDtypeStruct((width + 80, slots), BF)] * many
+
+    rel_sum, slab_t, qg_own, lrow_own, pack_own = pl.pallas_call(
+        functools.partial(forward_kernel, buckets, (0,), neg_scale),
         out_shape=[
-            jax.ShapeDtypeStruct((doms, rel_own * width // doms, width), BF),
-            jax.ShapeDtypeStruct((buckets, width, slots), BF),
-            jax.ShapeDtypeStruct((8, slots), jnp.int32),
+            jax.ShapeDtypeStruct((rel_own, width, width), F32),
+            jax.ShapeDtypeStruct((width, part_rows), BF),
         ]
-        + [pack] * buckets,
-        in_specs=[SMEM] + [VMEM] * (buckets + 2),
-        out_specs=[VMEM] * (buckets + 3),
-        scratch_shapes=[
-            pltpu.VMEM((rel_own, width, width), F32),
-            pltpu.VMEM((width, part_rows), BF),
-            pltpu.VMEM((width, part_rows), BF),
-            wide,
-            wide,
-            wide,
-            pltpu.VMEM((part_rows, 128), F32),
-        ],
+        + packs_of(1),
+        in_specs=[SMEM] + [VMEM] * 3,
+        out_specs=[VMEM] * 5,
+        scratch_shapes=scratch,
         compiler_params=limit,
         cost_estimate=pl.CostEstimate(
-            flops=4_400_000_000, bytes_accessed=4_000_000, transcendentals=1_600_000
+            flops=1_400_000_000, bytes_accessed=2_000_000, transcendentals=500_000
         ),
-        name="query_gradients",
-    )(me, received, *slabs, operators)
-    packs = [packs[0]] + [passed_along(packs[s], "dom", s) for s in range(1, buckets)]
+        name="own_bucket",
+    )(me, received, entities, operators)
+    others = tuple(range(1, buckets))
+    rel_parts, qg_other, lrow_other, *packs = pl.pallas_call(
+        functools.partial(forward_kernel, buckets, others, neg_scale),
+        out_shape=[jax.ShapeDtypeStruct((doms, rel_own * width // doms, width), BF)]
+        + packs_of(buckets - 1),
+        in_specs=[SMEM] + [VMEM] * (buckets + 3),
+        out_specs=[VMEM] * (buckets + 2),
+        scratch_shapes=scratch
+        + [pltpu.VMEM((rel_own, width, width), F32), pltpu.VMEM((width, part_rows), BF)],
+        compiler_params=limit,
+        cost_estimate=pl.CostEstimate(
+            flops=3_000_000_000, bytes_accessed=3_000_000, transcendentals=1_100_000
+        ),
+        name="other_buckets",
+    )(me, received, *slabs[1:], operators, slab_t, rel_sum)
+    packs = [pack_own] + [passed_along(packs[s - 1], "dom", s) for s in others]
     rel_arrived = exchanged(rel_parts, "dom")
 
     half_parts = jax.ShapeDtypeStruct((groups // 2, share, width), F32)
     keep, send = pl.pallas_call(
         functools.partial(entity_kernel, buckets, neg_scale, groups),
         out_shape=(half_parts, half_parts),
-        in_specs=[SMEM] + [VMEM] * (buckets + 4),
+        in_specs=[SMEM] + [VMEM] * (buckets + 6),
         out_specs=(VMEM, VMEM),
         scratch_shapes=[
             pltpu.VMEM((part_rows, width), F32),
@@ -318,14 +347,16 @@
             flops=4_000_000_000, bytes_accessed=3_000_000, transcendentals=1_600_000
         ),
         name="entity_gradients",
-    )(me, entities, operators, qgrads, lrows, *packs)
-    for partner in (1, 4, 12, 2):
-        got = lax.ppermute(send, "span", [(i, i ^ partner) for i in range(groups)])
-        half = keep.shape[0] // 2
-        if half:
-            send, keep = keep[half:] + got[half:], keep[:half] + got[:half]
-        else:
-            entity_share = (keep + got).reshape(share, width)
+    )(me, entities, operators, qg_own, lrow_own, qg_other, lrow_other, *packs)
+
+    def swapped(value, bits):
+        return lax.ppermute(value, "span", [(i, i ^ bits) for i in range(groups)])
+
+    total = keep + swapped(send, 1)
+    total = total.reshape(4, 2, share, width)
+    got = [swapped(total[x].astype(BF), 4 * x) for x in (1, 2, 3)]
+    total = total[0] + sum(part.astype(F32) for part in got)
+    entity_share = total[0] + swapped(total[1], 2)
     rel_share = jnp.sum(rel_arrived.astype(F32), axis=0)
     return (entity_share, rel_share.reshape(rel_own, width // doms, width))
 

time: 114 us -> 98.1 us (0.86)
  waiting for transfers between devices: 28.5 us -> 18.4 us
  Pallas kernels: 23.4 us -> 15.7 us
  starting transfers between devices: 55 us -> 57 us
    ppermute x4 -> x5, waiting for transfers between devices: 17.3 us -> 10.5 us  [swapped(): return lax.ppermute(value, 'span', [(i, i ^ bits) for i in range(groups)])]
    pallas_call x1 -> x2, Pallas kernels: 13.4 us -> 9.01 us  [the longest x1 6.23 us: shards(): pl.pallas_call(functools.partial(forward_kernel, buckets, others, neg_sca...]
    ppermute x4 -> x5, starting transfers between devices: 10.9 us -> 14.5 us  [swapped(): return lax.ppermute(value, 'span', [(i, i ^ bits) for i in range(groups)])]
    all_to_all x2, starting transfers between devices: 24.1 us -> 20.7 us  [exchanged(): return lax.all_to_all(value, axis, split_axis=0, concat_axis=0, tiled=True)]
    pallas_call x1, Pallas kernels: 8.21 us -> 4.94 us  [shards(): pl.pallas_call(functools.partial(entity_kernel, buckets, neg_scale, group...]
    ppermute x4, waiting for transfers between devices: 4.7 us -> 1.44 us  [passed_along(): return lax.ppermute(value, axis, pairs)]
    ppermute x4, starting transfers between devices: 20 us -> 21.7 us  [passed_along(): return lax.ppermute(value, axis, pairs)]
  transfers between devices with their start and end apart: 10 -> 11, of which waited for: 7 -> 6; matrix products, arithmetic and copies ran while one was open for 1% -> 1% of each run, Pallas kernels for 9% -> 10%
where the time goes in v3:
time: 98.1 us; the launch traced here: 97.3 us
  starting transfers between devices  57 us (58%)
  waiting for transfers between devices  18.4 us (19%)
  Pallas kernels  15.7 us (16%)
  local copies, waits for them, and re-layouts  2.93 us (3%)
  other arithmetic  2.49 us (3%)
    ppermute x4, starting transfers between devices, passed_along(): return lax.ppermute(value, axis, pairs)  21.7 us
    all_to_all x2, starting transfers between devices, exchanged(): return lax.all_to_all(value, axis, split_axis=0, concat_axis=0, tiled=True)  20.7 us
    ppermute x5, starting transfers between devices, swapped(): return lax.ppermute(value, 'span', [(i, i ^ bits) for i in range(groups)])  14.5 us
    ppermute x5, waiting for transfers between devices, swapped(): return lax.ppermute(value, 'span', [(i, i ^ bits) for i in range(groups)])  10.5 us
    all_to_all x2, waiting for transfers between devices, exchanged(): return lax.all_to_all(value, axis, split_axis=0, concat_axis=0, tiled=True)  6.5 us
    pallas_call x1, Pallas kernels, shards(): pl.pallas_call(functools.partial(forward_kernel, buckets, others, neg_sca...  6.23 us
    pallas_call x1, Pallas kernels, shards(): pl.pallas_call(functools.partial(entity_kernel, buckets, neg_scale, group...  4.94 us
    unnamed x10, local copies, waits for them, and re-layouts  2.91 us
  transfers between devices with their start and end apart: 11, of which 6 were waited for; matrix products, arithmetic and copies ran while one was open for 1% of the time, Pallas kernels for 10%

profile of v3, /device:TPU:24, one launch (start us, length us, event | category | flops | bytes accessed | tf_op | source)
XLA Modules:
  0.0 97.3 jit_solution(4259015929829695721)
XLA Ops:
  0.6 0.0 copy-start
  0.6 3.3 %collective-permute-start = (bf16[1024,256]{1,0:T(8,128)(2,1)}, bf16[1024,256]{1,0:T(8,128)(2,1)S(1)}, u32[]{:S(2)}, u32[]{:S(2)}) collective-permute-start(bf16[1024,256]{1,0:T(8,128)(2,1)} %slab_ref.1), channel_id=1, source_target_pairs={{0,496},{16,0},{32,16},{48,32},{64,48},{80,64},{96,80},{112,96},{1... | collective-permute-start | bytes 1572872 | tf_op jit(solution)/shard_map/ppermute | solution.py:25
  3.9 11.4 %collective-permute-start.1 = (bf16[1024,256]{1,0:T(8,128)(2,1)}, bf16[1024,256]{1,0:T(8,128)(2,1)S(1)}, u32[]{:S(2)}, u32[]{:S(2)}) collective-permute-start(bf16[1024,256]{1,0:T(8,128)(2,1)} %slab_ref.1), channel_id=1, source_target_pairs={{0,480},{16,496},{32,0},{48,16},{64,32},{80,48},{96,64},{112,80},{... | collective-permute-start | bytes 1572872 | tf_op jit(solution)/shard_map/ppermute | solution.py:25
  15.3 1.8 %pack_lists.1 = s32[16,32,128]{2,1,0:T(8,128)} custom-call(s32[3,8,128]{2,1,0:T(8,128)} %bitcast.13, s32[3,4,128]{2,1,0:T(4,128)} %bitcast.14, s32[3,4,128]{2,1,0:T(4,128)} %bitcast.15, s32[3,1,64]{2,1,0:T(1,128)} %bitcast.16), custom_call_target="tpu_custom_call" | custom-call | tf_op jit(solution)/shard_map/pack_lists/pallas_call | solution.py:276
  17.1 5.8 %all-to-all-start = ((s32[16,32,128]{2,1,0:T(8,128)}), s32[16,32,128]{2,1,0:T(8,128)S(1)}, u32[]{:S(2)}, u32[]{:S(2)}) async-start(s32[16,32,128]{2,1,0:T(8,128)} %pack_lists.1), calls=%async_computation | async-start | bytes 524288 | tf_op jit(solution)/shard_map/all_to_all | solution.py:29
  22.9 6.5 %all-to-all-done.x_ref = s32[16,32,128]{2,1,0:T(8,128)S(1)} async-done(((s32[16,32,128]{2,1,0:T(8,128)}), s32[16,32,128]{2,1,0:T(8,128)S(1)}, u32[]{:S(2)}, u32[]{:S(2)}) %all-to-all-start) | async-done | bytes 262176 | tf_op jit(solution)/shard_map/all_to_all | solution.py:29
  29.4 0.0 copy-done
  29.4 0.0 copy-start.1
  29.4 1.0 %copy-done.1 = bf16[4,256,256]{2,1,0:T(8,128)(2,1)S(1)} copy-done((bf16[4,256,256]{2,1,0:T(8,128)(2,1)S(1)}, bf16[4,256,256]{2,1,0:T(8,128)(2,1)}, u32[]{:S(2)}) %copy-start.1) | copy-done | bytes 524312
  30.4 2.8 %own_bucket.1 = (f32[4,256,256]{2,1,0:T(8,128)S(1)}, bf16[256,1024]{1,0:T(8,128)(2,1)S(1)}, bf16[1,256,512]{2,1,0:T(8,128)(2,1)S(1)}, s32[8,512]{1,0:T(8,128)S(1)}, bf16[336,512]{1,0:T(8,128)(2,1)S(1)}) custom-call(s32[1]{0:T(128)} %bitcast.me_ref, s32[16,32,128]{2,1,0:T(8,128)S(1)} %all-to-all-done.x_ref, bf16[1024,256]{1,0:T(8,128)(2,1)S(1)} %copy-done, ...), custom_call_target="tpu_custom_call" | custom-call | flops 1400000000 | bytes 2000000 | tf_op jit(solution)/shard_map/own_bucket/pallas_call | solution.py:301
  33.2 0.0 collective-permute-done.refs_0_
  33.2 0.0 collective-permute-done.1.refs_1_
  33.2 6.2 %other_buckets.1 = (bf16[32,32,256]{2,1,0:T(8,128)(2,1)}, bf16[2,256,512]{2,1,0:T(8,128)(2,1)S(1)}, s32[8,512]{1,0:T(8,128)S(1)}, bf16[336,512]{1,0:T(8,128)(2,1)S(1)}, bf16[336,512]{1,0:T(8,128)(2,1)S(1)}) custom-call(s32[1]{0:T(128)} %bitcast.me_ref, s32[16,32,128]{2,1,0:T(8,128)S(1)} %all-to-all-done.x_ref, ...), custom_call_target="tpu_custom_call" | custom-call | flops 3000000000 | bytes 3000000 | tf_op jit(solution)/shard_map/other_buckets/pallas_call | solution.py:318
  39.5 0.0 copy-start.3
  39.5 0.8 copy-done.3
  40.3 5.1 %collective-permute-start.2 = (bf16[336,512]{1,0:T(8,128)(2,1)S(1)}, bf16[336,512]{1,0:T(8,128)(2,1)S(1)}, u32[]{:S(2)}, u32[]{:S(2)}) collective-permute-start(bf16[336,512]{1,0:T(8,128)(2,1)S(1)} %get-tuple-element.21), channel_id=1, source_target_pairs={{0,16},{16,32},{32,48},{48,64},{64,80},{80,96},{96,112},{112,128},... | collective-permute-start | bytes 1032200 | tf_op jit(solution)/shard_map/ppermute | solution.py:25
  45.4 1.9 %collective-permute-start.3 = (bf16[336,512]{1,0:T(8,128)(2,1)S(1)}, bf16[336,512]{1,0:T(8,128)(2,1)S(1)}, u32[]{:S(2)}, u32[]{:S(2)}) collective-permute-start(bf16[336,512]{1,0:T(8,128)(2,1)S(1)} %get-tuple-element.22), channel_id=1, source_target_pairs={{0,32},{16,48},{32,64},{48,80},{64,96},{80,112},{96,128},{112,144}... | collective-permute-start | bytes 1032200 | tf_op jit(solution)/shard_map/ppermute | solution.py:25
  47.3 0.0 copy-start.2
  47.3 15.0 %all-to-all-start.1 = ((bf16[32,32,256]{2,1,0:T(8,128)(2,1)}), bf16[32,32,256]{2,1,0:T(8,128)(2,1)}, u32[]{:S(2)}, u32[]{:S(2)}) async-start(bf16[32,32,256]{2,1,0:T(8,128)(2,1)} %get-tuple-element.25), calls=%async_computation.1 | async-start | bytes 1048576 | tf_op jit(solution)/shard_map/all_to_all | solution.py:29
  62.3 0.0 collective-permute-done.2.refs_5_
  62.3 1.4 %collective-permute-done.3.refs_6_ = bf16[336,512]{1,0:T(8,128)(2,1)S(1)} collective-permute-done((bf16[336,512]{1,0:T(8,128)(2,1)S(1)}, bf16[336,512]{1,0:T(8,128)(2,1)S(1)}, u32[]{:S(2)}, u32[]{:S(2)}) %collective-permute-start.3) | collective-permute-done | bytes 344096 | tf_op jit(solution)/shard_map/ppermute | solution.py:25
  63.7 0.0 copy-done.2
  63.7 0.0 copy-start.4
  63.7 1.0 %copy-done.4 = bf16[2,256,512]{2,1,0:T(8,128)(2,1)S(1)} copy-done((bf16[2,256,512]{2,1,0:T(8,128)(2,1)S(1)}, bf16[2,256,512]{2,1,0:T(8,128)(2,1)}, u32[]{:S(2)}) %copy-start.4) | copy-done | bytes 524312
  64.8 4.9 %entity_gradients.1 = (f32[8,64,256]{2,1,0:T(8,128)S(1)}, f32[8,64,256]{2,1,0:T(8,128)S(1)}) custom-call(s32[1]{0:T(128)} %bitcast.me_ref, bf16[1024,256]{1,0:T(8,128)(2,1)S(1)} %copy-done, bf16[4,256,256]{2,1,0:T(8,128)(2,1)S(1)} %copy-done.2, bf16[1,256,512]{2,1,0:T(8,128)(2,1)S(1)} %get-tuple-element.14.refs_0_, s32[8,512]{1,0:T(8,128)S(1)} %get-tuple-element.15.refs_1_, ...), custom_call_target="tpu_custom_call" | custom-call | flops 4000000000 | bytes 3000000 | tf_op jit(solution)/shard_map/entity_gradients/pallas_call | solution.py:336
  69.7 1.9 %collective-permute-start.4 = (f32[8,64,256]{2,1,0:T(8,128)S(1)}, f32[8,64,256]{2,1,0:T(8,128)S(1)}, u32[]{:S(2)}, u32[]{:S(2)}) collective-permute-start(f32[8,64,256]{2,1,0:T(8,128)S(1)} %get-tuple-element.24), channel_id=1, source_target_pairs={{0,1},{1,0},{2,3},{3,2},{4,5},{5,4},{6,7},{7,6},{8,9},{9,8},{10,11... | collective-permute-start | bytes 1572872 | tf_op jit(solution)/shard_map/ppermute | solution.py:353
  71.7 1.9 %collective-permute-done.4 = f32[8,64,256]{2,1,0:T(8,128)S(1)} collective-permute-done((f32[8,64,256]{2,1,0:T(8,128)S(1)}, f32[8,64,256]{2,1,0:T(8,128)S(1)}, u32[]{:S(2)}, u32[]{:S(2)}) %collective-permute-start.4) | collective-permute-done | bytes 524320 | tf_op jit(solution)/shard_map/ppermute | solution.py:353
  73.5 0.1 fusion.1
  73.6 3.4 %collective-permute-start.5 = (bf16[2,64,256]{2,1,0:T(8,128)(2,1)S(1)}, bf16[2,64,256]{2,1,0:T(8,128)(2,1)S(1)}, u32[]{:S(2)}, u32[]{:S(2)}) collective-permute-start(bf16[2,64,256]{2,1,0:T(8,128)(2,1)S(1)} %get-tuple-element.28), channel_id=1, source_target_pairs={{0,4},{1,5},{2,6},{3,7},{4,0},{5,1},{6,2},{7,3},{8,12},{9,13},{10,... | collective-permute-start | bytes 196616 | tf_op jit(solution)/shard_map/ppermute | solution.py:353
  77.1 4.0 %collective-permute-start.7 = (bf16[2,64,256]{2,1,0:T(8,128)(2,1)S(1)}, bf16[2,64,256]{2,1,0:T(8,128)(2,1)S(1)}, u32[]{:S(2)}, u32[]{:S(2)}) collective-permute-start(bf16[2,64,256]{2,1,0:T(8,128)(2,1)S(1)} %get-tuple-element.29), channel_id=1, source_target_pairs={{0,12},{1,13},{2,14},{3,15},{4,8},{5,9},{6,10},{7,11},{8,4},{9,5},... | collective-permute-start | bytes 196616 | tf_op jit(solution)/shard_map/ppermute | solution.py:353
  81.1 2.6 %collective-permute-start.6 = (bf16[2,64,256]{2,1,0:T(8,128)(2,1)S(1)}, bf16[2,64,256]{2,1,0:T(8,128)(2,1)S(1)}, u32[]{:S(2)}, u32[]{:S(2)}) collective-permute-start(bf16[2,64,256]{2,1,0:T(8,128)(2,1)S(1)} %get-tuple-element.30), channel_id=1, source_target_pairs={{0,8},{1,9},{2,10},{3,11},{4,12},{5,13},{6,14},{7,15},{8,0},{9,1},... | collective-permute-start | bytes 196616 | tf_op jit(solution)/shard_map/ppermute | solution.py:353
  83.6 0.0 collective-permute-done.5
  83.6 0.8 collective-permute-done.7
  84.4 4.3 %collective-permute-done.6 = bf16[2,64,256]{2,1,0:T(8,128)(2,1)S(1)} collective-permute-done((bf16[2,64,256]{2,1,0:T(8,128)(2,1)S(1)}, bf16[2,64,256]{2,1,0:T(8,128)(2,1)S(1)}, u32[]{:S(2)}, u32[]{:S(2)}) %collective-permute-start.6) | collective-permute-done | bytes 65568 | tf_op jit(solution)/shard_map/ppermute | solution.py:353
  88.8 2.7 %collective-permute-start.8 = (f32[64,256]{1,0:T(8,128)S(1)}, f32[64,256]{1,0:T(8,128)S(1)}, u32[]{:S(2)}, u32[]{:S(2)}) collective-permute-start(f32[64,256]{1,0:T(8,128)S(1)} %slice_bitcast_fusion), channel_id=1, source_target_pairs={{0,2},{1,3},{2,0},{3,1},{4,6},{5,7},{6,4},{7,5},{8,10},{9,11},{10,... | collective-permute-start | bytes 196616 | tf_op jit(solution)/shard_map/ppermute | solution.py:353
  91.5 3.5 %collective-permute-done.8 = f32[64,256]{1,0:T(8,128)S(1)} collective-permute-done((f32[64,256]{1,0:T(8,128)S(1)}, f32[64,256]{1,0:T(8,128)S(1)}, u32[]{:S(2)}, u32[]{:S(2)}) %collective-permute-start.8) | collective-permute-done | bytes 65568 | tf_op jit(solution)/shard_map/ppermute | solution.py:353
  94.9 0.6 fusion
  95.6 0.0 all-to-all-done.1
  95.6 1.7 %convert_reduce_fusion = f32[32,256]{1,0:T(8,128)} fusion(bf16[32,32,256]{2,1,0:T(8,128)(2,1)} %all-to-all-done.1), kind=kLoop, calls=%fused_computation | loop fusion | flops 516096 | bytes 557056 | tf_op jit(solution)/shard_map/reduce_sum | solution.py:360
  (3 shorter events, 0.1 us)
Async XLA Ops:
  0.6 28.7 %copy-start = (bf16[1024,256]{1,0:T(8,128)(2,1)S(1)}, bf16[1024,256]{1,0:T(8,128)(2,1)}, u32[]{:S(2)}) copy-start(bf16[1024,256]{1,0:T(8,128)(2,1)} %slab_ref.1) | copy-start | bytes 1572868
  0.6 32.6 %collective-permute-start = (bf16[1024,256]{1,0:T(8,128)(2,1)}, bf16[1024,256]{1,0:T(8,128)(2,1)S(1)}, u32[]{:S(2)}, u32[]{:S(2)}) collective-permute-start(bf16[1024,256]{1,0:T(8,128)(2,1)} %slab_ref.1), channel_id=1, source_target_pairs={{0,496},{16,0},{32,16},{48,32},{64,48},{80,64},{96,80},{112,96},{1... | collective-permute-start | bytes 1572872 | tf_op jit(solution)/shard_map/ppermute | solution.py:25
  3.9 29.3 %collective-permute-start.1 = (bf16[1024,256]{1,0:T(8,128)(2,1)}, bf16[1024,256]{1,0:T(8,128)(2,1)S(1)}, u32[]{:S(2)}, u32[]{:S(2)}) collective-permute-start(bf16[1024,256]{1,0:T(8,128)(2,1)} %slab_ref.1), channel_id=1, source_target_pairs={{0,480},{16,496},{32,0},{48,16},{64,32},{80,48},{96,64},{112,80},{... | collective-permute-start | bytes 1572872 | tf_op jit(solution)/shard_map/ppermute | solution.py:25
  17.1 12.3 %all-to-all-start = ((s32[16,32,128]{2,1,0:T(8,128)}), s32[16,32,128]{2,1,0:T(8,128)S(1)}, u32[]{:S(2)}, u32[]{:S(2)}) async-start(s32[16,32,128]{2,1,0:T(8,128)} %pack_lists.1), calls=%async_computation | async-start | bytes 524288 | tf_op jit(solution)/shard_map/all_to_all | solution.py:29
  29.4 1.0 %copy-start.1 = (bf16[4,256,256]{2,1,0:T(8,128)(2,1)S(1)}, bf16[4,256,256]{2,1,0:T(8,128)(2,1)}, u32[]{:S(2)}) copy-start(bf16[4,256,256]{2,1,0:T(8,128)(2,1)} %ops_ref.1) | copy-start | bytes 1572868
  39.5 0.8 copy-start.3
  40.3 22.0 %collective-permute-start.2 = (bf16[336,512]{1,0:T(8,128)(2,1)S(1)}, bf16[336,512]{1,0:T(8,128)(2,1)S(1)}, u32[]{:S(2)}, u32[]{:S(2)}) collective-permute-start(bf16[336,512]{1,0:T(8,128)(2,1)S(1)} %get-tuple-element.21), channel_id=1, source_target_pairs={{0,16},{16,32},{32,48},{48,64},{64,80},{80,96},{96,112},{112,128},... | collective-permute-start | bytes 1032200 | tf_op jit(solution)/shard_map/ppermute | solution.py:25
  45.4 18.4 %collective-permute-start.3 = (bf16[336,512]{1,0:T(8,128)(2,1)S(1)}, bf16[336,512]{1,0:T(8,128)(2,1)S(1)}, u32[]{:S(2)}, u32[]{:S(2)}) collective-permute-start(bf16[336,512]{1,0:T(8,128)(2,1)S(1)} %get-tuple-element.22), channel_id=1, source_target_pairs={{0,32},{16,48},{32,64},{48,80},{64,96},{80,112},{96,128},{112,144}... | collective-permute-start | bytes 1032200 | tf_op jit(solution)/shard_map/ppermute | solution.py:25
  47.3 16.4 %copy-start.2 = (bf16[4,256,256]{2,1,0:T(8,128)(2,1)S(1)}, bf16[4,256,256]{2,1,0:T(8,128)(2,1)}, u32[]{:S(2)}) copy-start(bf16[4,256,256]{2,1,0:T(8,128)(2,1)} %ops_ref.1) | copy-start | bytes 1572868
  47.3 48.3 %all-to-all-start.1 = ((bf16[32,32,256]{2,1,0:T(8,128)(2,1)}), bf16[32,32,256]{2,1,0:T(8,128)(2,1)}, u32[]{:S(2)}, u32[]{:S(2)}) async-start(bf16[32,32,256]{2,1,0:T(8,128)(2,1)} %get-tuple-element.25), calls=%async_computation.1 | async-start | bytes 1048576 | tf_op jit(solution)/shard_map/all_to_all | solution.py:29
  63.7 1.0 %copy-start.4 = (bf16[2,256,512]{2,1,0:T(8,128)(2,1)S(1)}, bf16[2,256,512]{2,1,0:T(8,128)(2,1)}, u32[]{:S(2)}) copy-start(bf16[2,256,512]{2,1,0:T(8,128)(2,1)} %copy-done.3) | copy-start | bytes 1572868
  69.7 3.8 %collective-permute-start.4 = (f32[8,64,256]{2,1,0:T(8,128)S(1)}, f32[8,64,256]{2,1,0:T(8,128)S(1)}, u32[]{:S(2)}, u32[]{:S(2)}) collective-permute-start(f32[8,64,256]{2,1,0:T(8,128)S(1)} %get-tuple-element.24), channel_id=1, source_target_pairs={{0,1},{1,0},{2,3},{3,2},{4,5},{5,4},{6,7},{7,6},{8,9},{9,8},{10,11... | collective-permute-start | bytes 1572872 | tf_op jit(solution)/shard_map/ppermute | solution.py:353
  73.6 10.0 %collective-permute-start.5 = (bf16[2,64,256]{2,1,0:T(8,128)(2,1)S(1)}, bf16[2,64,256]{2,1,0:T(8,128)(2,1)S(1)}, u32[]{:S(2)}, u32[]{:S(2)}) collective-permute-start(bf16[2,64,256]{2,1,0:T(8,128)(2,1)S(1)} %get-tuple-element.28), channel_id=1, source_target_pairs={{0,4},{1,5},{2,6},{3,7},{4,0},{5,1},{6,2},{7,3},{8,12},{9,13},{10,... | collective-permute-start | bytes 196616 | tf_op jit(solution)/shard_map/ppermute | solution.py:353
  77.1 7.4 %collective-permute-start.7 = (bf16[2,64,256]{2,1,0:T(8,128)(2,1)S(1)}, bf16[2,64,256]{2,1,0:T(8,128)(2,1)S(1)}, u32[]{:S(2)}, u32[]{:S(2)}) collective-permute-start(bf16[2,64,256]{2,1,0:T(8,128)(2,1)S(1)} %get-tuple-element.29), channel_id=1, source_target_pairs={{0,12},{1,13},{2,14},{3,15},{4,8},{5,9},{6,10},{7,11},{8,4},{9,5},... | collective-permute-start | bytes 196616 | tf_op jit(solution)/shard_map/ppermute | solution.py:353
  81.1 7.7 %collective-permute-start.6 = (bf16[2,64,256]{2,1,0:T(8,128)(2,1)S(1)}, bf16[2,64,256]{2,1,0:T(8,128)(2,1)S(1)}, u32[]{:S(2)}, u32[]{:S(2)}) collective-permute-start(bf16[2,64,256]{2,1,0:T(8,128)(2,1)S(1)} %get-tuple-element.30), channel_id=1, source_target_pairs={{0,8},{1,9},{2,10},{3,11},{4,12},{5,13},{6,14},{7,15},{8,0},{9,1},... | collective-permute-start | bytes 196616 | tf_op jit(solution)/shard_map/ppermute | solution.py:353
  88.8 6.2 %collective-permute-start.8 = (f32[64,256]{1,0:T(8,128)S(1)}, f32[64,256]{1,0:T(8,128)S(1)}, u32[]{:S(2)}, u32[]{:S(2)}) collective-permute-start(f32[64,256]{1,0:T(8,128)S(1)} %slice_bitcast_fusion), channel_id=1, source_target_pairs={{0,2},{1,3},{2,0},{3,1},{4,6},{5,7},{6,4},{7,5},{8,10},{9,11},{10,... | collective-permute-start | bytes 196616 | tf_op jit(solution)/shard_map/ppermute | solution.py:353

commit v4 on v3

--- a/solution.py
+++ b/solution.py
@@ -13,16 +13,26 @@
 TN = (((0,), (0,)), ((), ()))
 VMEM = pl.BlockSpec(memory_space=pltpu.VMEM)
 SMEM = pl.BlockSpec(memory_space=pltpu.SMEM)
+HBM = pl.BlockSpec(memory_space=pltpu.HBM)
 
 
 def dot(a, b, dims=(((1,), (0,)), ((), ()))):
     return lax.dot_general(a, b, dims, preferred_element_type=F32)
 
 
-def passed_along(value, axis, steps):
-    count = lax.axis_size(axis)
-    pairs = [(source, (source + steps) % count) for source in range(count)]
-    return lax.ppermute(value, axis, pairs)
+def shifted(value, step, other):
+    doms, groups = lax.axis_size("dom"), lax.axis_size("span")
+    pairs = []
+    for p in range(doms):
+        for c in range(groups):
+            to = (p + (other if c & 1 else step)) % doms
+            pairs.append((p * groups + c, to * groups + c))
+    return lax.ppermute(value, ("dom", "span"), pairs)
+
+
+def swapped(value, bits):
+    groups = lax.axis_size("span")
+    return lax.ppermute(value, "span", [(i, i ^ bits) for i in range(groups)])
 
 
 def exchanged(value, axis):
@@ -65,6 +75,10 @@
     return carry
 
 
+def tie_kernel(held_ref, first_ref, out_ref):
+    out_ref[...] = held_ref[...]
+
+
 def one_hot(rows, at, shape):
     return ((iota(shape, 0) + at) == rows).astype(F32).astype(BF)
 
@@ -77,7 +91,7 @@
 def forward_kernel(buckets, which, neg_scale, me_ref, x_ref, *refs):
     first = which[0] == 0
     many = len(which)
-    slab_refs, ops_ref = refs[:many], refs[many]
+    slab_refs, ops_hbm = refs[:many], refs[many]
     refs = refs[many + 1 :]
     if first:
         rel_acc, et0_ref = refs[:2]
@@ -85,12 +99,14 @@
     else:
         et0_ref, sum_ref, rel_ref = refs[:3]
         refs = refs[3:]
-    qg_ref, lrow_ref = refs[:2]
-    pk_refs, refs = refs[2 : many + 2], refs[many + 2 :]
-    oh_ref, whi_ref, wlo_ref, mult_ref = refs[:4]
+    lrow_ref, qg_refs, pk_refs = refs[0], refs[1 : many + 1], refs[many + 1 : 2 * many + 1]
+    refs = refs[2 * many + 1 :]
+    oh_ref, whi_ref, wlo_ref, mult_ref, ops_ref, ops_sem = refs[:6]
     if not first:
-        rel_acc, et_ref = refs[4:]
-    rel_own, width, _ = ops_ref.shape
+        rel_acc, et_ref = refs[6:]
+    ops_copy = pltpu.make_async_copy(ops_hbm, ops_ref, ops_sem)
+    ops_copy.start()
+    rel_own, width, _ = ops_hbm.shape
     groups = x_ref.shape[0]
     part_rows = slab_refs[0].shape[0]
     slots = rel_own * 128
@@ -98,6 +114,7 @@
     chunks = part_rows // chunk
     hist_rows = 8 * buckets
     me = me_ref[0]
+    core = me & 1
 
     lane_row = iota((128, slots), 0)
     lane = iota((128, slots), 1)
@@ -118,6 +135,8 @@
 
     for at_call, s in enumerate(which):
         slab, pk = slab_refs[at_call], pk_refs[at_call]
+        if not first:
+            s = 1 + core if at_call == 0 else 2 - core
         pair = x_ref[:, hist_rows + s, :]
         left, right = pair & 65535, pair >> 16
         parts = [left >> 5, left & 31, right >> 5, right & 31]
@@ -154,6 +173,8 @@
 
         loop(chunks, left_hot, 0)
         left_t = dot(et0_ref[...], oh_ref[...]).astype(BF)
+        if at_call == 0:
+            ops_copy.wait()
         query_t = jnp.concatenate(
             [dot(ops_ref[i], left_t[:, 128 * i : 128 * (i + 1)], TN) for i in range(rel_own)], 1
         ).astype(BF)
@@ -184,7 +205,7 @@
         loop(chunks, weigh, 0)
         qgrad_t = dot(slab_t[...], whi_ref[...]) + dot(slab_t[...], wlo_ref[...])
         qgrad_t = (qgrad_t + right_t * pos_grad).astype(BF)
-        qg_ref[at_call] = qgrad_t
+        qg_refs[at_call][...] = qgrad_t
         for i in range(rel_own):
             cols = slice(128 * i, 128 * (i + 1))
             outer = dot(left_t[:, cols], qgrad_t[:, cols], NT)
@@ -204,12 +225,14 @@
         rel_ref[d] = jnp.concatenate(block, 0).astype(BF)
 
 
-def entity_kernel(buckets, neg_scale, groups, me_ref, slab_ref, ops_ref, *refs):
-    qg0_ref, lrow0_ref, qg_ref, lrow_ref = refs[:4]
-    pk_refs = refs[4 : 4 + buckets]
-    keep_ref, send_ref, rows_ref, mult_ref = refs[4 + buckets :]
+def entity_kernel(buckets, neg_scale, groups, me_ref, slab_ref, ops_hbm, *refs):
+    lrow0_ref, lrow_ref = refs[:2]
+    qg_refs, pk_refs = refs[2 : 2 + buckets], refs[2 + buckets : 2 + 2 * buckets]
+    keep_ref, send_ref, rows_ref, mult_ref, ops_ref, ops_sem = refs[2 + 2 * buckets :]
+    ops_copy = pltpu.make_async_copy(ops_hbm, ops_ref, ops_sem)
+    ops_copy.start()
     me = me_ref[0]
-    rel_own, width, _ = ops_ref.shape
+    rel_own, width, _ = ops_hbm.shape
     part_rows = slab_ref.shape[0]
     slots = rel_own * 128
     chunk = 256
@@ -218,7 +241,9 @@
     for s in range(buckets):
         pk = pk_refs[s]
         left_row = lrow_ref[s - 1 : s, :] if s else lrow0_ref[0:1, :]
-        qgrad_t = qg_ref[s - 1] if s else qg0_ref[0]
+        if s == 0:
+            ops_copy.wait()
+        qgrad_t = qg_refs[s][...]
         lgrad_t = jnp.concatenate(
             [dot(ops_ref[i], qgrad_t[:, 128 * i : 128 * (i + 1)]) for i in range(rel_own)], 1
         ).astype(BF)
@@ -271,7 +296,8 @@
     neg_scale = float(neg_count) ** (-0.5)
     share = part_rows // groups
     slots = rel_own * 128
-    limit = pltpu.CompilerParams(vmem_limit_bytes=24 * 1024 * 1024)
+    limit = pltpu.CompilerParams(vmem_limit_bytes=12 * 1024 * 1024)
+    small = pltpu.CompilerParams(vmem_limit_bytes=2 * 1024 * 1024)
 
     packed = pl.pallas_call(
         functools.partial(pack_kernel, buckets, groups),
@@ -286,28 +312,47 @@
         counts.reshape(buckets, 1, relations),
     )
     received = exchanged(packed, "span")
-    slabs = [entities] + [passed_along(entities, "dom", -s) for s in range(1, buckets)]
+    near = shifted(entities, -1, -2)
+    near = pl.pallas_call(
+        tie_kernel,
+        out_shape=jax.ShapeDtypeStruct(entities.shape, BF),
+        in_specs=[VMEM, VMEM],
+        out_specs=VMEM,
+        compiler_params=small,
+        name="after_lists",
+    )(near, received)
+    slabs = [near, swapped(near, 1)]
 
     me = lax.axis_index("span").astype(jnp.int32).reshape(1)
     wide = pltpu.VMEM((part_rows, slots), BF)
-    scratch = [wide, wide, wide, pltpu.VMEM((part_rows, 128), F32)]
+
+    def scratch_of():
+        return [
+            wide,
+            wide,
+            wide,
+            pltpu.VMEM((part_rows, 128), F32),
+            pltpu.VMEM(operators.shape, BF),
+            pltpu.SemaphoreType.DMA,
+        ]
 
     def packs_of(many):
-        return [
-            jax.ShapeDtypeStruct((many, width, slots), BF),
-            jax.ShapeDtypeStruct((8, slots), jnp.int32),
-        ] + [jax.ShapeDtypeStruct((width + 80, slots), BF)] * many
-
-    rel_sum, slab_t, qg_own, lrow_own, pack_own = pl.pallas_call(
+        return (
+            [jax.ShapeDtypeStruct((8, slots), jnp.int32)]
+            + [jax.ShapeDtypeStruct((width, slots), BF)] * many
+            + [jax.ShapeDtypeStruct((width + 80, slots), BF)] * many
+        )
+
+    rel_sum, slab_t, lrow_own, qg_own, pack_own = pl.pallas_call(
         functools.partial(forward_kernel, buckets, (0,), neg_scale),
         out_shape=[
             jax.ShapeDtypeStruct((rel_own, width, width), F32),
             jax.ShapeDtypeStruct((width, part_rows), BF),
         ]
         + packs_of(1),
-        in_specs=[SMEM] + [VMEM] * 3,
+        in_specs=[SMEM, VMEM, VMEM, HBM],
         out_specs=[VMEM] * 5,
-        scratch_shapes=scratch,
+        scratch_shapes=scratch_of(),
         compiler_params=limit,
         cost_estimate=pl.CostEstimate(
             flops=1_400_000_000, bytes_accessed=2_000_000, transcendentals=500_000
@@ -315,42 +360,42 @@
         name="own_bucket",
     )(me, received, entities, operators)
     others = tuple(range(1, buckets))
-    rel_parts, qg_other, lrow_other, *packs = pl.pallas_call(
+    rel_parts, lrow_other, *packs = pl.pallas_call(
         functools.partial(forward_kernel, buckets, others, neg_scale),
         out_shape=[jax.ShapeDtypeStruct((doms, rel_own * width // doms, width), BF)]
         + packs_of(buckets - 1),
-        in_specs=[SMEM] + [VMEM] * (buckets + 3),
-        out_specs=[VMEM] * (buckets + 2),
-        scratch_shapes=scratch
+        in_specs=[SMEM] + [VMEM] * buckets + [HBM, VMEM, VMEM],
+        out_specs=[VMEM] * (2 * buckets),
+        scratch_shapes=scratch_of()
         + [pltpu.VMEM((rel_own, width, width), F32), pltpu.VMEM((width, part_rows), BF)],
         compiler_params=limit,
         cost_estimate=pl.CostEstimate(
             flops=3_000_000_000, bytes_accessed=3_000_000, transcendentals=1_100_000
         ),
         name="other_buckets",
-    )(me, received, *slabs[1:], operators, slab_t, rel_sum)
-    packs = [pack_own] + [passed_along(packs[s - 1], "dom", s) for s in others]
+    )(me, received, *slabs, operators, slab_t, rel_sum)
+    grads = [qg_own] + packs[:2]
+    packs = [pack_own, shifted(packs[2], 1, 2), shifted(packs[3], 2, 1)]
     rel_arrived = exchanged(rel_parts, "dom")
 
     half_parts = jax.ShapeDtypeStruct((groups // 2, share, width), F32)
     keep, send = pl.pallas_call(
         functools.partial(entity_kernel, buckets, neg_scale, groups),
         out_shape=(half_parts, half_parts),
-        in_specs=[SMEM] + [VMEM] * (buckets + 6),
+        in_specs=[SMEM, VMEM, HBM] + [VMEM] * (2 + 2 * buckets),
         out_specs=(VMEM, VMEM),
         scratch_shapes=[
             pltpu.VMEM((part_rows, width), F32),
             pltpu.VMEM((part_rows, 128), F32),
+            pltpu.VMEM(operators.shape, BF),
+            pltpu.SemaphoreType.DMA,
         ],
         compiler_params=limit,
         cost_estimate=pl.CostEstimate(
             flops=4_000_000_000, bytes_accessed=3_000_000, transcendentals=1_600_000
         ),
         name="entity_gradients",
-    )(me, entities, operators, qg_own, lrow_own, qg_other, lrow_other, *packs)
-
-    def swapped(value, bits):
-        return lax.ppermute(value, "span", [(i, i ^ bits) for i in range(groups)])
+    )(me, entities, operators, lrow_own, lrow_other, *grads, *packs)
 
     total = keep + swapped(send, 1)
     total = total.reshape(4, 2, share, width)

time: 98.1 us -> 96.1 us (0.980)
  blocking collectives: 0 us -> 19.7 us
  starting transfers between devices: 57 us -> 39.8 us
  waiting for transfers between devices: 18.4 us -> 13 us
    all_to_all x0 -> x1, blocking collectives: none -> 19.7 us  [exchanged(): return lax.all_to_all(value, axis, split_axis=0, concat_axis=0, tiled=True)]
    ppermute x4 -> x3, starting transfers between devices: 21.7 us -> 6.97 us  [shifted(): return lax.ppermute(value, ('dom', 'span'), pairs)]
    all_to_all x2 -> x1, waiting for transfers between devices: 6.5 us -> 0.01 us  [exchanged(): return lax.all_to_all(value, axis, split_axis=0, concat_axis=0, tiled=True)]
    all_to_all x2 -> x1, starting transfers between devices: 20.7 us -> 15.5 us  [exchanged(): return lax.all_to_all(value, axis, split_axis=0, concat_axis=0, tiled=True)]
    ppermute x5 -> x6, starting transfers between devices: 14.5 us -> 17.3 us  [swapped(): return lax.ppermute(value, 'span', [(i, i ^ bits) for i in range(groups)])]
    ppermute x5 -> x6, waiting for transfers between devices: 10.5 us -> 11.3 us  [swapped(): return lax.ppermute(value, 'span', [(i, i ^ bits) for i in range(groups)])]
    unnamed x10 -> x16, local copies, waits for them, and re-layouts: 2.91 us -> 3.04 us
  transfers between devices with their start and end apart: 11 -> 10, of which waited for: 6 -> 5; matrix products, arithmetic and copies ran while one was open for 1% -> 1% of each run, Pallas kernels for 10% -> 10%
where the time goes in v4:
time: 96.1 us; the launch traced here: 94.7 us
  starting transfers between devices  39.8 us (41%)
  blocking collectives  19.7 us (20%)
  Pallas kernels  15.8 us (16%)
  waiting for transfers between devices  13 us (14%)
  local copies, waits for them, and re-layouts  3.06 us (3%)
  other arithmetic  2.49 us (3%)
    all_to_all x1, blocking collectives, exchanged(): return lax.all_to_all(value, axis, split_axis=0, concat_axis=0, tiled=True)  19.7 us
    ppermute x6, starting transfers between devices, swapped(): return lax.ppermute(value, 'span', [(i, i ^ bits) for i in range(groups)])  17.3 us
    all_to_all x1, starting transfers between devices, exchanged(): return lax.all_to_all(value, axis, split_axis=0, concat_axis=0, tiled=True)  15.5 us
    ppermute x6, waiting for transfers between devices, swapped(): return lax.ppermute(value, 'span', [(i, i ^ bits) for i in range(groups)])  11.3 us
    ppermute x3, starting transfers between devices, shifted(): return lax.ppermute(value, ('dom', 'span'), pairs)  6.97 us
    pallas_call x1, Pallas kernels, shards(): pl.pallas_call(functools.partial(forward_kernel, buckets, others, neg_sca...  6.23 us
    pallas_call x1, Pallas kernels, shards(): pl.pallas_call(functools.partial(entity_kernel, buckets, neg_scale, group...  4.99 us
    unnamed x16, local copies, waits for them, and re-layouts  3.04 us
  transfers between devices with their start and end apart: 10, of which 5 were waited for; matrix products, arithmetic and copies ran while one was open for 1% of the time, Pallas kernels for 10%

profile of v4, /device:TPU:24, one launch (start us, length us, event | category | flops | bytes accessed | tf_op | source)
XLA Modules:
  0.0 94.7 jit_solution(11944510844393938929)
XLA Ops:
  0.6 3.1 %collective-permute-start = (bf16[1024,256]{1,0:T(8,128)(2,1)}, bf16[1024,256]{1,0:T(8,128)(2,1)S(1)}, u32[]{:S(2)}, u32[]{:S(2)}) collective-permute-start(bf16[1024,256]{1,0:T(8,128)(2,1)} %slab_ref.1), channel_id=1, source_target_pairs={{0,496},{1,481},{2,498},{3,483},{4,500},{5,485},{6,502},{7,487},{8... | collective-permute-start | bytes 1572872 | tf_op jit(solution)/shard_map/ppermute | solution.py:30
  3.8 1.8 %pack_lists.1 = s32[16,32,128]{2,1,0:T(8,128)} custom-call(s32[3,8,128]{2,1,0:T(8,128)} %bitcast.13, s32[3,4,128]{2,1,0:T(4,128)} %bitcast.14, s32[3,4,128]{2,1,0:T(4,128)} %bitcast.15, s32[3,1,64]{2,1,0:T(1,128)} %bitcast.16), custom_call_target="tpu_custom_call" | custom-call | tf_op jit(solution)/shard_map/pack_lists/pallas_call | solution.py:302
  5.5 19.7 %all_to_all.10.x_ref.first_ref = s32[16,32,128]{2,1,0:T(8,128)S(1)} all-to-all(s32[16,32,128]{2,1,0:T(8,128)} %pack_lists.1), channel_id=1, replica_groups=mesh['dom'=32,'span'=16] {'span'}, dimensions={0} | all-to-all | bytes 524288 | tf_op jit(solution)/shard_map/all_to_all | solution.py:39
  25.2 0.0 copy-start
  25.2 0.0 copy-start.1
  25.2 0.0 collective-permute-done.held_ref
  25.3 2.3 %collective-permute-start.1 = (bf16[1024,256]{1,0:T(8,128)(2,1)S(1)}, bf16[1024,256]{1,0:T(8,128)(2,1)S(1)}, u32[]{:S(2)}, u32[]{:S(2)}) collective-permute-start(bf16[1024,256]{1,0:T(8,128)(2,1)S(1)} %after_lists.1.refs_0_), channel_id=1, source_target_pairs={{0,1},{1,0},{2,3},{3,2},{4,5},{5,4},{6,7},{7,6},{8,9},{9,8},{10,11... | collective-permute-start | bytes 1572872 | tf_op jit(solution)/shard_map/ppermute | solution.py:35
  27.6 0.0 copy-done
  27.6 0.0 copy-done.1
  27.7 2.8 %own_bucket.1 = (f32[4,256,256]{2,1,0:T(8,128)S(1)}, bf16[256,1024]{1,0:T(8,128)(2,1)S(1)}, s32[8,512]{1,0:T(8,128)S(1)}, bf16[256,512]{1,0:T(8,128)(2,1)S(1)}, bf16[336,512]{1,0:T(8,128)(2,1)S(1)}) custom-call(s32[1]{0:T(128)} %bitcast.me_ref, s32[16,32,128]{2,1,0:T(8,128)S(1)} %all_to_all.10.x_ref.first_ref, bf16[1024,256]{1,0:T(8,128)(2,1)S(1)} %copy-done, ...), custom_call_target="tpu_custom_call" | custom-call | flops 1400000000 | bytes 2000000 | tf_op jit(solution)/shard_map/own_bucket/pallas_call | solution.py:346
  30.5 0.0 copy-start.2
  30.5 0.7 copy-done.2
  31.2 0.0 collective-permute-done.1.refs_1_
  31.2 6.2 %other_buckets.1 = (bf16[32,32,256]{2,1,0:T(8,128)(2,1)}, s32[8,512]{1,0:T(8,128)S(1)}, bf16[256,512]{1,0:T(8,128)(2,1)S(1)}, bf16[256,512]{1,0:T(8,128)(2,1)S(1...) custom-call(s32[1]{0:T(128)} %bitcast.me_ref, s32[16,32,128]{2,1,0:T(8,128)S(1)} %all_to_all.10.x_ref.first_ref, ...), custom_call_target="tpu_custom_call" | custom-call | flops 3000000000 | bytes 3000000 | tf_op jit(solution)/shard_map/other_buckets/pallas_call | solution.py:363
  37.4 0.0 copy-start.4
  37.4 0.7 copy-done.4
  38.1 0.0 copy-start.6
  38.1 0.7 copy-done.6
  38.8 1.9 %collective-permute-start.2 = (bf16[336,512]{1,0:T(8,128)(2,1)S(1)}, bf16[336,512]{1,0:T(8,128)(2,1)S(1)}, u32[]{:S(2)}, u32[]{:S(2)}) collective-permute-start(bf16[336,512]{1,0:T(8,128)(2,1)S(1)} %get-tuple-element.23), channel_id=1, source_target_pairs={{0,16},{1,33},{2,18},{3,35},{4,20},{5,37},{6,22},{7,39},{8,24},{9,... | collective-permute-start | bytes 1032200 | tf_op jit(solution)/shard_map/ppermute | solution.py:30
  40.7 1.9 %collective-permute-start.3 = (bf16[336,512]{1,0:T(8,128)(2,1)S(1)}, bf16[336,512]{1,0:T(8,128)(2,1)S(1)}, u32[]{:S(2)}, u32[]{:S(2)}) collective-permute-start(bf16[336,512]{1,0:T(8,128)(2,1)S(1)} %get-tuple-element.24), channel_id=1, source_target_pairs={{0,32},{1,17},{2,34},{3,19},{4,36},{5,21},{6,38},{7,23},{8,40},{9,... | collective-permute-start | bytes 1032200 | tf_op jit(solution)/shard_map/ppermute | solution.py:30
  42.7 0.0 copy-start.3
  42.7 0.0 copy-start.5
  42.7 15.5 %all-to-all-start.1 = ((bf16[32,32,256]{2,1,0:T(8,128)(2,1)}), bf16[32,32,256]{2,1,0:T(8,128)(2,1)}, u32[]{:S(2)}, u32[]{:S(2)}) async-start(bf16[32,32,256]{2,1,0:T(8,128)(2,1)} %get-tuple-element.27), calls=%async_computation.1 | async-start | bytes 1048576 | tf_op jit(solution)/shard_map/all_to_all | solution.py:39
  58.2 0.0 collective-permute-done.2.refs_6_
  58.2 1.7 %collective-permute-done.3.refs_7_ = bf16[336,512]{1,0:T(8,128)(2,1)S(1)} collective-permute-done((bf16[336,512]{1,0:T(8,128)(2,1)S(1)}, bf16[336,512]{1,0:T(8,128)(2,1)S(1)}, u32[]{:S(2)}, u32[]{:S(2)}) %collective-permute-start.3) | collective-permute-done | bytes 344096 | tf_op jit(solution)/shard_map/ppermute | solution.py:30
  59.9 0.0 copy-done.3
  59.9 0.0 copy-done.5
  59.9 0.0 copy-start.7
  59.9 0.9 %copy-done.7 = bf16[256,512]{1,0:T(8,128)(2,1)S(1)} copy-done((bf16[256,512]{1,0:T(8,128)(2,1)S(1)}, bf16[256,512]{1,0:T(8,128)(2,1)}, u32[]{:S(2)}) %copy-start.7) | copy-done | bytes 262168
  60.9 5.0 %entity_gradients.1 = (f32[8,64,256]{2,1,0:T(8,128)S(1)}, f32[8,64,256]{2,1,0:T(8,128)S(1)}) custom-call(s32[1]{0:T(128)} %bitcast.me_ref, bf16[1024,256]{1,0:T(8,128)(2,1)S(1)} %copy-done, bf16[4,256,256]{2,1,0:T(8,128)(2,1)S(1)} %copy-done.1, s32[8,512]{1,0:T(8,128)S(1)} %get-tuple-element.15.refs_0_, s32[8,512]{1,0:T(8,128)S(1)} %get-tuple-element.18.refs_1_, ...), custom_call_target="tpu_custom_call" | custom-call | flops 4000000000 | bytes 3000000 | tf_op jit(solution)/shard_map/entity_gradients/pallas_call | solution.py:382
  65.9 1.9 %collective-permute-start.4 = (f32[8,64,256]{2,1,0:T(8,128)S(1)}, f32[8,64,256]{2,1,0:T(8,128)S(1)}, u32[]{:S(2)}, u32[]{:S(2)}) collective-permute-start(f32[8,64,256]{2,1,0:T(8,128)S(1)} %get-tuple-element.26), channel_id=1, source_target_pairs={{0,1},{1,0},{2,3},{3,2},{4,5},{5,4},{6,7},{7,6},{8,9},{9,8},{10,11... | collective-permute-start | bytes 1572872 | tf_op jit(solution)/shard_map/ppermute | solution.py:35
  67.8 1.9 %collective-permute-done.4 = f32[8,64,256]{2,1,0:T(8,128)S(1)} collective-permute-done((f32[8,64,256]{2,1,0:T(8,128)S(1)}, f32[8,64,256]{2,1,0:T(8,128)S(1)}, u32[]{:S(2)}, u32[]{:S(2)}) %collective-permute-start.4) | collective-permute-done | bytes 524320 | tf_op jit(solution)/shard_map/ppermute | solution.py:35
  69.7 0.1 fusion.1
  69.8 4.4 %collective-permute-start.5 = (bf16[2,64,256]{2,1,0:T(8,128)(2,1)S(1)}, bf16[2,64,256]{2,1,0:T(8,128)(2,1)S(1)}, u32[]{:S(2)}, u32[]{:S(2)}) collective-permute-start(bf16[2,64,256]{2,1,0:T(8,128)(2,1)S(1)} %get-tuple-element.30), channel_id=1, source_target_pairs={{0,4},{1,5},{2,6},{3,7},{4,0},{5,1},{6,2},{7,3},{8,12},{9,13},{10,... | collective-permute-start | bytes 196616 | tf_op jit(solution)/shard_map/ppermute | solution.py:35
  74.2 4.2 %collective-permute-start.7 = (bf16[2,64,256]{2,1,0:T(8,128)(2,1)S(1)}, bf16[2,64,256]{2,1,0:T(8,128)(2,1)S(1)}, u32[]{:S(2)}, u32[]{:S(2)}) collective-permute-start(bf16[2,64,256]{2,1,0:T(8,128)(2,1)S(1)} %get-tuple-element.31), channel_id=1, source_target_pairs={{0,12},{1,13},{2,14},{3,15},{4,8},{5,9},{6,10},{7,11},{8,4},{9,5},... | collective-permute-start | bytes 196616 | tf_op jit(solution)/shard_map/ppermute | solution.py:35
  78.4 2.5 %collective-permute-start.6 = (bf16[2,64,256]{2,1,0:T(8,128)(2,1)S(1)}, bf16[2,64,256]{2,1,0:T(8,128)(2,1)S(1)}, u32[]{:S(2)}, u32[]{:S(2)}) collective-permute-start(bf16[2,64,256]{2,1,0:T(8,128)(2,1)S(1)} %get-tuple-element.32), channel_id=1, source_target_pairs={{0,8},{1,9},{2,10},{3,11},{4,12},{5,13},{6,14},{7,15},{8,0},{9,1},... | collective-permute-start | bytes 196616 | tf_op jit(solution)/shard_map/ppermute | solution.py:35
  80.9 0.0 collective-permute-done.5
  80.9 0.7 collective-permute-done.7
  81.6 4.5 %collective-permute-done.6 = bf16[2,64,256]{2,1,0:T(8,128)(2,1)S(1)} collective-permute-done((bf16[2,64,256]{2,1,0:T(8,128)(2,1)S(1)}, bf16[2,64,256]{2,1,0:T(8,128)(2,1)S(1)}, u32[]{:S(2)}, u32[]{:S(2)}) %collective-permute-start.6) | collective-permute-done | bytes 65568 | tf_op jit(solution)/shard_map/ppermute | solution.py:35
  86.1 1.9 %collective-permute-start.8 = (f32[64,256]{1,0:T(8,128)S(1)}, f32[64,256]{1,0:T(8,128)S(1)}, u32[]{:S(2)}, u32[]{:S(2)}) collective-permute-start(f32[64,256]{1,0:T(8,128)S(1)} %slice_bitcast_fusion), channel_id=1, source_target_pairs={{0,2},{1,3},{2,0},{3,1},{4,6},{5,7},{6,4},{7,5},{8,10},{9,11},{10,... | collective-permute-start | bytes 196616 | tf_op jit(solution)/shard_map/ppermute | solution.py:35
  88.1 4.2 %collective-permute-done.8 = f32[64,256]{1,0:T(8,128)S(1)} collective-permute-done((f32[64,256]{1,0:T(8,128)S(1)}, f32[64,256]{1,0:T(8,128)S(1)}, u32[]{:S(2)}, u32[]{:S(2)}) %collective-permute-start.8) | collective-permute-done | bytes 65568 | tf_op jit(solution)/shard_map/ppermute | solution.py:35
  92.3 0.6 fusion
  92.9 0.0 all-to-all-done.1
  92.9 1.7 %convert_reduce_fusion = f32[32,256]{1,0:T(8,128)} fusion(bf16[32,32,256]{2,1,0:T(8,128)(2,1)} %all-to-all-done.1), kind=kLoop, calls=%fused_computation | loop fusion | flops 516096 | bytes 557056 | tf_op jit(solution)/shard_map/reduce_sum | solution.py:405
  (4 shorter events, 0.1 us)
Async XLA Ops:
  0.6 24.6 %collective-permute-start = (bf16[1024,256]{1,0:T(8,128)(2,1)}, bf16[1024,256]{1,0:T(8,128)(2,1)S(1)}, u32[]{:S(2)}, u32[]{:S(2)}) collective-permute-start(bf16[1024,256]{1,0:T(8,128)(2,1)} %slab_ref.1), channel_id=1, source_target_pairs={{0,496},{1,481},{2,498},{3,483},{4,500},{5,485},{6,502},{7,487},{8... | collective-permute-start | bytes 1572872 | tf_op jit(solution)/shard_map/ppermute | solution.py:30
  25.2 2.4 %copy-start = (bf16[1024,256]{1,0:T(8,128)(2,1)S(1)}, bf16[1024,256]{1,0:T(8,128)(2,1)}, u32[]{:S(2)}) copy-start(bf16[1024,256]{1,0:T(8,128)(2,1)} %slab_ref.1) | copy-start | bytes 1572868
  25.2 2.4 %copy-start.1 = (bf16[4,256,256]{2,1,0:T(8,128)(2,1)S(1)}, bf16[4,256,256]{2,1,0:T(8,128)(2,1)}, u32[]{:S(2)}) copy-start(bf16[4,256,256]{2,1,0:T(8,128)(2,1)} %ops_hbm.1) | copy-start | bytes 1572868
  25.3 5.9 %collective-permute-start.1 = (bf16[1024,256]{1,0:T(8,128)(2,1)S(1)}, bf16[1024,256]{1,0:T(8,128)(2,1)S(1)}, u32[]{:S(2)}, u32[]{:S(2)}) collective-permute-start(bf16[1024,256]{1,0:T(8,128)(2,1)S(1)} %after_lists.1.refs_0_), channel_id=1, source_target_pairs={{0,1},{1,0},{2,3},{3,2},{4,5},{5,4},{6,7},{7,6},{8,9},{9,8},{10,11... | collective-permute-start | bytes 1572872 | tf_op jit(solution)/shard_map/ppermute | solution.py:35
  30.5 0.7 copy-start.2
  37.4 0.7 copy-start.4
  38.1 0.7 copy-start.6
  38.8 19.4 %collective-permute-start.2 = (bf16[336,512]{1,0:T(8,128)(2,1)S(1)}, bf16[336,512]{1,0:T(8,128)(2,1)S(1)}, u32[]{:S(2)}, u32[]{:S(2)}) collective-permute-start(bf16[336,512]{1,0:T(8,128)(2,1)S(1)} %get-tuple-element.23), channel_id=1, source_target_pairs={{0,16},{1,33},{2,18},{3,35},{4,20},{5,37},{6,22},{7,39},{8,24},{9,... | collective-permute-start | bytes 1032200 | tf_op jit(solution)/shard_map/ppermute | solution.py:30
  40.7 19.2 %collective-permute-start.3 = (bf16[336,512]{1,0:T(8,128)(2,1)S(1)}, bf16[336,512]{1,0:T(8,128)(2,1)S(1)}, u32[]{:S(2)}, u32[]{:S(2)}) collective-permute-start(bf16[336,512]{1,0:T(8,128)(2,1)S(1)} %get-tuple-element.24), channel_id=1, source_target_pairs={{0,32},{1,17},{2,34},{3,19},{4,36},{5,21},{6,38},{7,23},{8,40},{9,... | collective-permute-start | bytes 1032200 | tf_op jit(solution)/shard_map/ppermute | solution.py:30
  42.7 17.2 %copy-start.3 = (bf16[256,512]{1,0:T(8,128)(2,1)S(1)}, bf16[256,512]{1,0:T(8,128)(2,1)}, u32[]{:S(2)}) copy-start(bf16[256,512]{1,0:T(8,128)(2,1)} %copy-done.2) | copy-start | bytes 786436
  42.7 17.2 %copy-start.5 = (bf16[256,512]{1,0:T(8,128)(2,1)S(1)}, bf16[256,512]{1,0:T(8,128)(2,1)}, u32[]{:S(2)}) copy-start(bf16[256,512]{1,0:T(8,128)(2,1)} %copy-done.4) | copy-start | bytes 786436
  42.7 50.3 %all-to-all-start.1 = ((bf16[32,32,256]{2,1,0:T(8,128)(2,1)}), bf16[32,32,256]{2,1,0:T(8,128)(2,1)}, u32[]{:S(2)}, u32[]{:S(2)}) async-start(bf16[32,32,256]{2,1,0:T(8,128)(2,1)} %get-tuple-element.27), calls=%async_computation.1 | async-start | bytes 1048576 | tf_op jit(solution)/shard_map/all_to_all | solution.py:39
  59.9 1.0 %copy-start.7 = (bf16[256,512]{1,0:T(8,128)(2,1)S(1)}, bf16[256,512]{1,0:T(8,128)(2,1)}, u32[]{:S(2)}) copy-start(bf16[256,512]{1,0:T(8,128)(2,1)} %copy-done.6) | copy-start | bytes 786436
  65.9 3.8 %collective-permute-start.4 = (f32[8,64,256]{2,1,0:T(8,128)S(1)}, f32[8,64,256]{2,1,0:T(8,128)S(1)}, u32[]{:S(2)}, u32[]{:S(2)}) collective-permute-start(f32[8,64,256]{2,1,0:T(8,128)S(1)} %get-tuple-element.26), channel_id=1, source_target_pairs={{0,1},{1,0},{2,3},{3,2},{4,5},{5,4},{6,7},{7,6},{8,9},{9,8},{10,11... | collective-permute-start | bytes 1572872 | tf_op jit(solution)/shard_map/ppermute | solution.py:35
  69.8 11.1 %collective-permute-start.5 = (bf16[2,64,256]{2,1,0:T(8,128)(2,1)S(1)}, bf16[2,64,256]{2,1,0:T(8,128)(2,1)S(1)}, u32[]{:S(2)}, u32[]{:S(2)}) collective-permute-start(bf16[2,64,256]{2,1,0:T(8,128)(2,1)S(1)} %get-tuple-element.30), channel_id=1, source_target_pairs={{0,4},{1,5},{2,6},{3,7},{4,0},{5,1},{6,2},{7,3},{8,12},{9,13},{10,... | collective-permute-start | bytes 196616 | tf_op jit(solution)/shard_map/ppermute | solution.py:35
  74.2 7.4 %collective-permute-start.7 = (bf16[2,64,256]{2,1,0:T(8,128)(2,1)S(1)}, bf16[2,64,256]{2,1,0:T(8,128)(2,1)S(1)}, u32[]{:S(2)}, u32[]{:S(2)}) collective-permute-start(bf16[2,64,256]{2,1,0:T(8,128)(2,1)S(1)} %get-tuple-element.31), channel_id=1, source_target_pairs={{0,12},{1,13},{2,14},{3,15},{4,8},{5,9},{6,10},{7,11},{8,4},{9,5},... | collective-permute-start | bytes 196616 | tf_op jit(solution)/shard_map/ppermute | solution.py:35
  78.4 7.7 %collective-permute-start.6 = (bf16[2,64,256]{2,1,0:T(8,128)(2,1)S(1)}, bf16[2,64,256]{2,1,0:T(8,128)(2,1)S(1)}, u32[]{:S(2)}, u32[]{:S(2)}) collective-permute-start(bf16[2,64,256]{2,1,0:T(8,128)(2,1)S(1)} %get-tuple-element.32), channel_id=1, source_target_pairs={{0,8},{1,9},{2,10},{3,11},{4,12},{5,13},{6,14},{7,15},{8,0},{9,1},... | collective-permute-start | bytes 196616 | tf_op jit(solution)/shard_map/ppermute | solution.py:35
  86.1 6.2 %collective-permute-start.8 = (f32[64,256]{1,0:T(8,128)S(1)}, f32[64,256]{1,0:T(8,128)S(1)}, u32[]{:S(2)}, u32[]{:S(2)}) collective-permute-start(f32[64,256]{1,0:T(8,128)S(1)} %slice_bitcast_fusion), channel_id=1, source_target_pairs={{0,2},{1,3},{2,0},{3,1},{4,6},{5,7},{6,4},{7,5},{8,10},{9,11},{10,... | collective-permute-start | bytes 196616 | tf_op jit(solution)/shard_map/ppermute | solution.py:35

commit v5 on v4

--- a/solution.py
+++ b/solution.py
@@ -43,30 +43,33 @@
     return lax.broadcasted_iota(jnp.int32, shape, axis)
 
 
-def pack_kernel(buckets, groups, neg_ref, left_ref, right_ref, count_ref, out_ref):
-    hist_rows = 8 * buckets
-    for s in range(buckets):
+def pack_kernel(
+    groups, neg_ref, left_ref, right_ref, count_ref, ent_ref, out_ref, slab_ref, sem
+):
+    slab_copy = pltpu.make_async_copy(ent_ref, slab_ref, sem)
+    slab_copy.start()
+    hists = []
+    for s in range(3):
         high, low = [], []
         for q in range(neg_ref.shape[1]):
             row = neg_ref[s, q : q + 1, :]
             high.append((iota((16, 128), 0) == (row >> 7)).astype(F32).astype(BF))
             low.append((iota((128, 128), 0) == (row & 127)).astype(F32).astype(BF))
-        hist = dot(jnp.concatenate(high, 1), jnp.concatenate(low, 1), NT)[:8].astype(jnp.int32)
-        for d in range(groups):
-            out_ref[d, 8 * s : 8 * s + 8, :] = hist
+        hist = dot(jnp.concatenate(high, 1), jnp.concatenate(low, 1), NT)[:8]
+        hists.append(hist.astype(jnp.int32))
+    words = hists[0] + (hists[1] << 16)
+    for d in range(groups):
+        out_ref[d, 0:8, :] = words
     lines = left_ref.shape[1]
-    rest = jnp.zeros((8 - 2 * buckets, 128), jnp.int32)
-    counts = [count_ref[s] for s in range(buckets)]
-    counts = jnp.concatenate(counts, 0)
-    counts = jnp.concatenate([counts, jnp.zeros((buckets, 128 - counts.shape[1]), jnp.int32)], 1)
+    counts = [count_ref[s] for s in range(3)]
+    counts = counts + [jnp.zeros(counts[0].shape, jnp.int32)]
+    counts = [jnp.concatenate(counts[:2], 1), jnp.concatenate(counts[2:], 1)]
     for line in range(lines):
-        pairs = [
-            left_ref[s, line : line + 1, :] + (right_ref[s, line : line + 1, :] << 16)
-            for s in range(buckets)
-        ]
-        block = jnp.concatenate(pairs + [counts, rest], 0)
+        rows = [ref[s, line : line + 1, :] for ref in (left_ref, right_ref) for s in range(3)]
+        words = hists[2] + (jnp.concatenate(rows + counts, 0) << 16)
         for d in range(line * groups // lines, (line + 1) * groups // lines):
-            out_ref[d, hist_rows : hist_rows + 8, :] = block
+            out_ref[d, 8:16, :] = words
+    slab_copy.wait()
 
 
 def loop(n, step, carry):
@@ -99,11 +102,17 @@
     else:
         et0_ref, sum_ref, rel_ref = refs[:3]
         refs = refs[3:]
-    lrow_ref, qg_refs, pk_refs = refs[0], refs[1 : many + 1], refs[many + 1 : 2 * many + 1]
+    lrow_ref, qg_hbms, pk_refs = refs[0], refs[1 : many + 1], refs[many + 1 : 2 * many + 1]
     refs = refs[2 * many + 1 :]
-    oh_ref, whi_ref, wlo_ref, mult_ref, ops_ref, ops_sem = refs[:6]
-    if not first:
-        rel_acc, et_ref = refs[6:]
+    oh_ref, whi_ref, wlo_ref, mult_ref, ops_ref, qg_ref, ops_sem, qg_sems = refs[:8]
+    qg_copies = [
+        pltpu.make_async_copy(qg_ref.at[n], qg_hbms[n], qg_sems.at[n]) for n in range(many)
+    ]
+    if first:
+        pk_hbm, pk_refs = pk_refs[0], refs[8:9]
+        pk_copy = pltpu.make_async_copy(pk_refs[0], pk_hbm, refs[9])
+    else:
+        rel_acc, et_ref = refs[8:]
     ops_copy = pltpu.make_async_copy(ops_hbm, ops_ref, ops_sem)
     ops_copy.start()
     rel_own, width, _ = ops_hbm.shape
@@ -112,7 +121,6 @@
     slots = rel_own * 128
     chunk = 256
     chunks = part_rows // chunk
-    hist_rows = 8 * buckets
     me = me_ref[0]
     core = me & 1
 
@@ -122,7 +130,7 @@
     per_line = 128 // (8 * rel_own)
     pick_slot = (lane_row == (me % per_line) * (8 * rel_own) + relation * 8 + slot)
     pick_slot = pick_slot.astype(F32).astype(BF)
-    pick_count = (lane_row == me * rel_own + relation).astype(F32).astype(BF)
+    count_lane = me * rel_own + relation
     lane = iota((groups, slots), 1)
     own_group = iota((groups, slots), 0) == ((lane >> 3) & (groups - 1))
     slot_row = iota((1, slots), 1) & 7
@@ -137,20 +145,20 @@
         slab, pk = slab_refs[at_call], pk_refs[at_call]
         if not first:
             s = 1 + core if at_call == 0 else 2 - core
-        pair = x_ref[:, hist_rows + s, :]
-        left, right = pair & 65535, pair >> 16
+        left, right = x_ref[:, 8 + s, :] >> 16, x_ref[:, 11 + s, :] >> 16
         parts = [left >> 5, left & 31, right >> 5, right & 31]
         parts = dot(narrow(jnp.concatenate(parts, 0)), pick_slot)
         parts = [own(parts[groups * q : groups * (q + 1)]) for q in range(4)]
         left_row = (parts[0] * 32.0 + parts[1]).astype(jnp.int32)
         right_row = (parts[2] * 32.0 + parts[3]).astype(jnp.int32)
-        count_row = own(dot(narrow(x_ref[:, hist_rows + buckets + s, :]), pick_count))
+        pick_count = narrow(lane_row == count_lane + (s % 2) * (groups * rel_own))
+        count_row = own(dot(narrow(x_ref[:, 14 + s // 2, :] >> 16), pick_count))
         live = (count_row.astype(jnp.int32) > slot_row).astype(F32)
         lrow_ref[at_call : at_call + 1, :] = left_row
 
         highs, lows = [], []
         for a in range(8):
-            hist = x_ref[:, 8 * s + a, :]
+            hist = (x_ref[:, (s // 2) * 8 + a, :] >> (16 * (s % 2))) & 65535
             highs.append(hist >> 5)
             lows.append(hist & 31)
             spread_counts(hist.astype(F32), groups, mult_ref, a)
@@ -189,6 +197,8 @@
         misc = [narrow(parts[2]), narrow(parts[3]), narrow(live), pos_high, pos_low]
         misc = [row.astype(F32) for row in misc] + [jnp.zeros((11, slots), F32)]
         pk[width + 64 : width + 80, :] = jnp.concatenate(misc, 0).astype(BF)
+        if first:
+            pk_copy.start()
         factor = live * (0.5 * neg_scale)
 
         def weigh(n, carry):
@@ -205,7 +215,8 @@
         loop(chunks, weigh, 0)
         qgrad_t = dot(slab_t[...], whi_ref[...]) + dot(slab_t[...], wlo_ref[...])
         qgrad_t = (qgrad_t + right_t * pos_grad).astype(BF)
-        qg_refs[at_call][...] = qgrad_t
+        qg_ref[at_call] = qgrad_t
+        qg_copies[at_call].start()
         for i in range(rel_own):
             cols = slice(128 * i, 128 * (i + 1))
             outer = dot(left_t[:, cols], qgrad_t[:, cols], NT)
@@ -217,20 +228,31 @@
                 rel_acc[i] = rel_acc[i] + outer
 
     if first:
+        pk_copy.wait()
+        qg_copies[0].wait()
         return
     doms, held, _ = rel_ref.shape
     held = held // rel_own
     for d in range(doms):
         block = [rel_acc[i, held * d : held * (d + 1), :] for i in range(rel_own)]
         rel_ref[d] = jnp.concatenate(block, 0).astype(BF)
+    for copy in qg_copies:
+        copy.wait()
 
 
 def entity_kernel(buckets, neg_scale, groups, me_ref, slab_ref, ops_hbm, *refs):
     lrow0_ref, lrow_ref = refs[:2]
-    qg_refs, pk_refs = refs[2 : 2 + buckets], refs[2 + buckets : 2 + 2 * buckets]
-    keep_ref, send_ref, rows_ref, mult_ref, ops_ref, ops_sem = refs[2 + 2 * buckets :]
-    ops_copy = pltpu.make_async_copy(ops_hbm, ops_ref, ops_sem)
-    ops_copy.start()
+    qg_hbms, pk_refs = refs[2 : 2 + buckets], list(refs[2 + buckets : 2 + 2 * buckets])
+    keep_ref, send_ref, rows_ref, mult_ref, ops_ref, qg_ref, pk_ref, sems = refs[2 + 2 * buckets :]
+    copies = [
+        pltpu.make_async_copy(ops_hbm, ops_ref, sems.at[0]),
+        pltpu.make_async_copy(pk_refs[0], pk_ref, sems.at[1]),
+    ]
+    for s in range(buckets):
+        copies.append(pltpu.make_async_copy(qg_hbms[s], qg_ref.at[s], sems.at[2 + s]))
+    for copy in copies:
+        copy.start()
+    pk_refs[0] = pk_ref
     me = me_ref[0]
     rel_own, width, _ = ops_hbm.shape
     part_rows = slab_ref.shape[0]
@@ -238,15 +260,9 @@
     chunk = 256
     chunks = part_rows // chunk
     share = part_rows // groups
-    for s in range(buckets):
+    for step, s in enumerate(list(range(1, buckets)) + [0]):
         pk = pk_refs[s]
         left_row = lrow_ref[s - 1 : s, :] if s else lrow0_ref[0:1, :]
-        if s == 0:
-            ops_copy.wait()
-        qgrad_t = qg_refs[s][...]
-        lgrad_t = jnp.concatenate(
-            [dot(ops_ref[i], qgrad_t[:, 128 * i : 128 * (i + 1)]) for i in range(rel_own)], 1
-        ).astype(BF)
         hist = pk[width : width + 64, :].astype(F32)
         hist = hist[:32] * 32.0 + hist[32:]
         for a in range(8):
@@ -258,6 +274,13 @@
         pos_grad = misc[3:4] + misc[4:5]
         query_t = pk[0:width, :]
         half_t = query_t * 0.5
+        if step == 0:
+            for copy in copies:
+                copy.wait()
+        qgrad_t = qg_ref[s]
+        lgrad_t = jnp.concatenate(
+            [dot(ops_ref[i], qgrad_t[:, 128 * i : 128 * (i + 1)]) for i in range(rel_own)], 1
+        ).astype(BF)
 
         def weigh(n, carry):
             at = n * chunk
@@ -270,7 +293,7 @@
             low = (weight - high.astype(F32)).astype(BF)
             hot = one_hot(left_row, n * chunk, (chunk, slots))
             rows = dot(high, query_t, NT) + dot(low, query_t, NT) + dot(hot, lgrad_t, NT)
-            rows_ref[pl.ds(at, chunk), :] = rows if s == 0 else rows_ref[pl.ds(at, chunk), :] + rows
+            rows_ref[pl.ds(at, chunk), :] = rows if step == 0 else rows_ref[pl.ds(at, chunk), :] + rows
             return carry
 
         loop(chunks, weigh, 0)
@@ -282,6 +305,20 @@
             keep_ref[n] = block
         else:
             send_ref[n - half] = block
+
+
+def finish_kernel(keep_ref, got_ref, parts_hbm, ent_ref, rel_ref, parts_ref, sems):
+    cuts = parts_ref.shape[0]
+    copies = [pltpu.make_async_copy(parts_hbm.at[n], parts_ref.at[n], sems.at[n]) for n in range(cuts)]
+    for copy in copies:
+        copy.start()
+    ent_ref[...] = keep_ref[...] + got_ref[...]
+    total = None
+    for n in range(cuts):
+        copies[n].wait()
+        part = jnp.sum(parts_ref[n].astype(F32), axis=0)
+        total = part if total is None else total + part
+    rel_ref[...] = total
 
 
 def shards(entities, operators, left_rows, right_rows, negatives, counts):
@@ -299,20 +336,25 @@
     limit = pltpu.CompilerParams(vmem_limit_bytes=12 * 1024 * 1024)
     small = pltpu.CompilerParams(vmem_limit_bytes=2 * 1024 * 1024)
 
-    packed = pl.pallas_call(
-        functools.partial(pack_kernel, buckets, groups),
-        out_shape=jax.ShapeDtypeStruct((groups, 8 * buckets + 8, 128), jnp.int32),
-        in_specs=[VMEM] * 4,
-        out_specs=VMEM,
+    packed, slab = pl.pallas_call(
+        functools.partial(pack_kernel, groups),
+        out_shape=(
+            jax.ShapeDtypeStruct((groups, 16, 128), jnp.int32),
+            jax.ShapeDtypeStruct(entities.shape, BF),
+        ),
+        in_specs=[VMEM] * 4 + [HBM],
+        out_specs=(VMEM, VMEM),
+        scratch_shapes=[pltpu.SemaphoreType.DMA],
         name="pack_lists",
     )(
         negatives.reshape(buckets, neg_count // 128, 128),
         left_rows.reshape(buckets, slot_count // 128, 128),
         right_rows.reshape(buckets, slot_count // 128, 128),
         counts.reshape(buckets, 1, relations),
+        entities,
     )
     received = exchanged(packed, "span")
-    near = shifted(entities, -1, -2)
+    near = shifted(slab, -1, -2)
     near = pl.pallas_call(
         tie_kernel,
         out_shape=jax.ShapeDtypeStruct(entities.shape, BF),
@@ -326,21 +368,23 @@
     me = lax.axis_index("span").astype(jnp.int32).reshape(1)
     wide = pltpu.VMEM((part_rows, slots), BF)
 
-    def scratch_of():
+    def scratch_of(many):
         return [
             wide,
             wide,
             wide,
             pltpu.VMEM((part_rows, 128), F32),
             pltpu.VMEM(operators.shape, BF),
+            pltpu.VMEM((many, width, slots), BF),
             pltpu.SemaphoreType.DMA,
+            pltpu.SemaphoreType.DMA((many,)),
         ]
 
-    def packs_of(many):
+    def packs_of(many, pack):
         return (
             [jax.ShapeDtypeStruct((8, slots), jnp.int32)]
-            + [jax.ShapeDtypeStruct((width, slots), BF)] * many
-            + [jax.ShapeDtypeStruct((width + 80, slots), BF)] * many
+            + [pltpu.HBM((width, slots), BF)] * many
+            + [pack((width + 80, slots), BF)] * many
         )
 
     rel_sum, slab_t, lrow_own, qg_own, pack_own = pl.pallas_call(
@@ -349,24 +393,25 @@
             jax.ShapeDtypeStruct((rel_own, width, width), F32),
             jax.ShapeDtypeStruct((width, part_rows), BF),
         ]
-        + packs_of(1),
+        + packs_of(1, pltpu.HBM),
         in_specs=[SMEM, VMEM, VMEM, HBM],
-        out_specs=[VMEM] * 5,
-        scratch_shapes=scratch_of(),
+        out_specs=[VMEM] * 3 + [HBM] * 2,
+        scratch_shapes=scratch_of(1)
+        + [pltpu.VMEM((width + 80, slots), BF), pltpu.SemaphoreType.DMA],
         compiler_params=limit,
         cost_estimate=pl.CostEstimate(
             flops=1_400_000_000, bytes_accessed=2_000_000, transcendentals=500_000
         ),
         name="own_bucket",
-    )(me, received, entities, operators)
+    )(me, received, slab, operators)
     others = tuple(range(1, buckets))
     rel_parts, lrow_other, *packs = pl.pallas_call(
         functools.partial(forward_kernel, buckets, others, neg_scale),
         out_shape=[jax.ShapeDtypeStruct((doms, rel_own * width // doms, width), BF)]
-        + packs_of(buckets - 1),
+        + packs_of(buckets - 1, jax.ShapeDtypeStruct),
         in_specs=[SMEM] + [VMEM] * buckets + [HBM, VMEM, VMEM],
-        out_specs=[VMEM] * (2 * buckets),
-        scratch_shapes=scratch_of()
+        out_specs=[VMEM] * 2 + [HBM] * (buckets - 1) + [VMEM] * (buckets - 1),
+        scratch_shapes=scratch_of(buckets - 1)
         + [pltpu.VMEM((rel_own, width, width), F32), pltpu.VMEM((width, part_rows), BF)],
         compiler_params=limit,
         cost_estimate=pl.CostEstimate(
@@ -374,7 +419,8 @@
         ),
         name="other_buckets",
     )(me, received, *slabs, operators, slab_t, rel_sum)
-    grads = [qg_own] + packs[:2]
+    pack_own = pltpu.with_memory_space_constraint(pack_own, pltpu.HBM)
+    grads = [pltpu.with_memory_space_constraint(grad, pltpu.HBM) for grad in [qg_own] + packs[:2]]
     packs = [pack_own, shifted(packs[2], 1, 2), shifted(packs[3], 2, 1)]
     rel_arrived = exchanged(rel_parts, "dom")
 
@@ -382,27 +428,44 @@
     keep, send = pl.pallas_call(
         functools.partial(entity_kernel, buckets, neg_scale, groups),
         out_shape=(half_parts, half_parts),
-        in_specs=[SMEM, VMEM, HBM] + [VMEM] * (2 + 2 * buckets),
+        in_specs=[SMEM, VMEM, HBM, VMEM, VMEM] + [HBM] * (buckets + 1) + [VMEM] * (buckets - 1),
         out_specs=(VMEM, VMEM),
         scratch_shapes=[
             pltpu.VMEM((part_rows, width), F32),
             pltpu.VMEM((part_rows, 128), F32),
             pltpu.VMEM(operators.shape, BF),
-            pltpu.SemaphoreType.DMA,
+            pltpu.VMEM((buckets, width, slots), BF),
+            pltpu.VMEM((width + 80, slots), BF),
+            pltpu.SemaphoreType.DMA((buckets + 2,)),
         ],
         compiler_params=limit,
         cost_estimate=pl.CostEstimate(
             flops=4_000_000_000, bytes_accessed=3_000_000, transcendentals=1_600_000
         ),
         name="entity_gradients",
-    )(me, entities, operators, lrow_own, lrow_other, *grads, *packs)
+    )(me, slab, operators, lrow_own, lrow_other, *grads, *packs)
 
     total = keep + swapped(send, 1)
     total = total.reshape(4, 2, share, width)
     got = [swapped(total[x].astype(BF), 4 * x) for x in (1, 2, 3)]
     total = total[0] + sum(part.astype(F32) for part in got)
-    entity_share = total[0] + swapped(total[1], 2)
-    rel_share = jnp.sum(rel_arrived.astype(F32), axis=0)
+    held = rel_own * width // doms
+    rel_arrived = rel_arrived.reshape(4, doms // 4, held, width)
+    entity_share, rel_share = pl.pallas_call(
+        finish_kernel,
+        out_shape=(
+            jax.ShapeDtypeStruct((share, width), F32),
+            jax.ShapeDtypeStruct((held, width), F32),
+        ),
+        in_specs=[VMEM, VMEM, HBM],
+        out_specs=(VMEM, VMEM),
+        scratch_shapes=[
+            pltpu.VMEM(rel_arrived.shape, BF),
+            pltpu.SemaphoreType.DMA((4,)),
+        ],
+        compiler_params=small,
+        name="last_sums",
+    )(total[0], swapped(total[1], 2), rel_arrived)
     return (entity_share, rel_share.reshape(rel_own, width // doms, width))
 
 

time: 96.1 us -> 95.5 us (level)
  Pallas kernels: 15.8 us -> 20.5 us
  local copies, waits for them, and re-layouts: 3.06 us -> 0.03 us
  other arithmetic: 2.49 us -> 0.11 us
  blocking collectives: 19.7 us -> 18.4 us
  waiting for transfers between devices: 13 us -> 14.3 us
    unnamed x16 -> x4, local copies, waits for them, and re-layouts: 3.04 us -> 0.01 us
    ppermute x3, waiting for transfers between devices: 1.68 us -> 4.4 us  [shifted(): return lax.ppermute(value, ('dom', 'span'), pairs)]
    pallas_call x1 -> x2, Pallas kernels: 1.76 us -> 4.03 us  [the longest x1 2.62 us: shards(): pl.pallas_call(functools.partial(pack_kernel, groups), out_shape=(jax.Sha...]
    reduce_sum x1 -> x0, other arithmetic: 1.74 us -> none  [shards(): rel_share = jnp.sum(rel_arrived.astype(F32), axis=0)]
    ppermute x6, waiting for transfers between devices: 11.3 us -> 9.92 us  [swapped(): return lax.ppermute(value, 'span', [(i, i ^ bits) for i in range(groups)])]
    all_to_all x1, blocking collectives: 19.7 us -> 18.4 us  [exchanged(): return lax.all_to_all(value, axis, split_axis=0, concat_axis=0, tiled=True)]
    pallas_call x1, Pallas kernels: 4.99 us -> 6.18 us  [shards(): pl.pallas_call(functools.partial(entity_kernel, buckets, neg_scale, group...]
    ppermute x6, starting transfers between devices: 17.3 us -> 16.2 us  [swapped(): return lax.ppermute(value, 'span', [(i, i ^ bits) for i in range(groups)])]
  transfers between devices with their start and end apart: 10 -> 10, of which waited for: 5 -> 5; matrix products, arithmetic and copies ran while one was open for 1% -> 0% of each run, Pallas kernels for 10% -> 10%
where the time goes in v5:
time: 95.5 us; the launch traced here: 93.8 us
  starting transfers between devices  39.5 us (41%)
  Pallas kernels  20.5 us (21%)
  blocking collectives  18.4 us (19%)
  waiting for transfers between devices  14.3 us (15%)
  between operations  0.98 us (1%)
    all_to_all x1, blocking collectives, exchanged(): return lax.all_to_all(value, axis, split_axis=0, concat_axis=0, tiled=True)  18.4 us
    all_to_all x1, starting transfers between devices, exchanged(): return lax.all_to_all(value, axis, split_axis=0, concat_axis=0, tiled=True)  16.3 us
    ppermute x6, starting transfers between devices, swapped(): return lax.ppermute(value, 'span', [(i, i ^ bits) for i in range(groups)])  16.2 us
    ppermute x6, waiting for transfers between devices, swapped(): return lax.ppermute(value, 'span', [(i, i ^ bits) for i in range(groups)])  9.92 us
    ppermute x3, starting transfers between devices, shifted(): return lax.ppermute(value, ('dom', 'span'), pairs)  6.98 us
    pallas_call x1, Pallas kernels, shards(): pl.pallas_call(functools.partial(forward_kernel, buckets, others, neg_sca...  6.73 us
    pallas_call x1, Pallas kernels, shards(): pl.pallas_call(functools.partial(entity_kernel, buckets, neg_scale, group...  6.18 us
    ppermute x3, waiting for transfers between devices, shifted(): return lax.ppermute(value, ('dom', 'span'), pairs)  4.4 us
  transfers between devices with their start and end apart: 10, of which 5 were waited for; matrix products, arithmetic and copies ran while one was open for 0% of the time, Pallas kernels for 10%

profile of v5, /device:TPU:24, one launch (start us, length us, event | category | flops | bytes accessed | tf_op | source)
XLA Modules:
  0.0 93.8 jit_solution(10864081976808942374)
XLA Ops:
  0.6 2.6 %pack_lists.1 = (s32[16,16,128]{2,1,0:T(8,128)}, bf16[1024,256]{1,0:T(8,128)(2,1)}) custom-call(s32[3,8,128]{2,1,0:T(8,128)} %bitcast.12, s32[3,4,128]{2,1,0:T(4,128)} %bitcast.13, s32[3,4,128]{2,1,0:T(4,128)} %bitcast.14, s32[3,1,64]{2,1,0:T(1,128)} %bitcast.15, bf16[1024,256]{1,0:T(8,128)(2,1)} %ent_ref.1), custom_call_target="tpu_custom_call" | custom-call | tf_op jit(solution)/shard_map/pack_lists/pallas_call | solution.py:339
  3.3 3.1 %collective-permute-start = (bf16[1024,256]{1,0:T(8,128)(2,1)}, bf16[1024,256]{1,0:T(8,128)(2,1)S(1)}, u32[]{:S(2)}, u32[]{:S(2)}) collective-permute-start(bf16[1024,256]{1,0:T(8,128)(2,1)} %get-tuple-element.19.refs_0_.slab_ref), channel_id=1, source_target_pairs={{0,496},{1,481},{2,498},{3,483},{4,500},{5,485},{6,502},{7,487},{8... | collective-permute-start | bytes 1572872 | tf_op jit(solution)/shard_map/ppermute | solution.py:30
  6.4 18.4 %all_to_all.10.x_ref.first_ref = s32[16,16,128]{2,1,0:T(8,128)S(1)} all-to-all(s32[16,16,128]{2,1,0:T(8,128)} %get-tuple-element.20), channel_id=1, replica_groups=mesh['dom'=32,'span'=16] {'span'}, dimensions={0} | all-to-all | bytes 262144 | tf_op jit(solution)/shard_map/all_to_all | solution.py:39
  24.8 0.0 copy-start
  24.8 0.0 copy-start.1
  24.8 0.0 collective-permute-done.held_ref
  24.9 2.2 %collective-permute-start.1 = (bf16[1024,256]{1,0:T(8,128)(2,1)S(1)}, bf16[1024,256]{1,0:T(8,128)(2,1)S(1)}, u32[]{:S(2)}, u32[]{:S(2)}) collective-permute-start(bf16[1024,256]{1,0:T(8,128)(2,1)S(1)} %after_lists.1.refs_0_), channel_id=1, source_target_pairs={{0,1},{1,0},{2,3},{3,2},{4,5},{5,4},{6,7},{7,6},{8,9},{9,8},{10,11... | collective-permute-start | bytes 1572872 | tf_op jit(solution)/shard_map/ppermute | solution.py:35
  27.1 0.0 copy-done
  27.1 0.0 copy-done.1
  27.1 3.5 %own_bucket.1 = (f32[4,256,256]{2,1,0:T(8,128)S(1)}, bf16[256,1024]{1,0:T(8,128)(2,1)S(1)}, s32[8,512]{1,0:T(8,128)S(1)}, bf16[256,512]{1,0:T(8,128)(2,1)}, bf16[336,512]{1,0:T(8,128)(2,1)}) custom-call(s32[1]{0:T(128)} %bitcast.me_ref, s32[16,16,128]{2,1,0:T(8,128)S(1)} %all_to_all.10.x_ref.first_ref, bf16[1024,256]{1,0:T(8,128)(2,1)S(1)} %copy-done.1, ...), custom_call_target="tpu_custom_call" | custom-call | flops 1400000000 | bytes 2000000 | tf_op jit(solution)/shard_map/own_bucket/pallas_call | solution.py:390
  30.6 0.0 collective-permute-done.1.refs_1_
  30.6 6.7 %other_buckets.1 = (bf16[32,32,256]{2,1,0:T(8,128)(2,1)}, s32[8,512]{1,0:T(8,128)S(1)}, bf16[256,512]{1,0:T(8,128)(2,1)}, bf16[256,512]{1,0:T(8,128)(2,1)}, bf16...) custom-call(s32[1]{0:T(128)} %bitcast.me_ref, s32[16,16,128]{2,1,0:T(8,128)S(1)} %all_to_all.10.x_ref.first_ref, ...), custom_call_target="tpu_custom_call" | custom-call | flops 3000000000 | bytes 3000000 | tf_op jit(solution)/shard_map/other_buckets/pallas_call | solution.py:408
  37.4 1.9 %collective-permute-start.2 = (bf16[336,512]{1,0:T(8,128)(2,1)S(1)}, bf16[336,512]{1,0:T(8,128)(2,1)S(1)}, u32[]{:S(2)}, u32[]{:S(2)}) collective-permute-start(bf16[336,512]{1,0:T(8,128)(2,1)S(1)} %get-tuple-element.29), channel_id=1, source_target_pairs={{0,16},{1,33},{2,18},{3,35},{4,20},{5,37},{6,22},{7,39},{8,24},{9,... | collective-permute-start | bytes 1032200 | tf_op jit(solution)/shard_map/ppermute | solution.py:30
  39.3 1.9 %collective-permute-start.3 = (bf16[336,512]{1,0:T(8,128)(2,1)S(1)}, bf16[336,512]{1,0:T(8,128)(2,1)S(1)}, u32[]{:S(2)}, u32[]{:S(2)}) collective-permute-start(bf16[336,512]{1,0:T(8,128)(2,1)S(1)} %get-tuple-element.30), channel_id=1, source_target_pairs={{0,32},{1,17},{2,34},{3,19},{4,36},{5,21},{6,38},{7,23},{8,40},{9,... | collective-permute-start | bytes 1032200 | tf_op jit(solution)/shard_map/ppermute | solution.py:30
  41.2 16.3 %all-to-all-start.1 = ((bf16[32,32,256]{2,1,0:T(8,128)(2,1)}), bf16[32,32,256]{2,1,0:T(8,128)(2,1)S(1)}, u32[]{:S(2)}, u32[]{:S(2)}) async-start(bf16[32,32,256]{2,1,0:T(8,128)(2,1)} %get-tuple-element.33), calls=%async_computation.1 | async-start | bytes 1048576 | tf_op jit(solution)/shard_map/all_to_all | solution.py:39
  57.6 0.0 collective-permute-done.2.refs_6_
  57.6 4.4 %collective-permute-done.3.refs_7_ = bf16[336,512]{1,0:T(8,128)(2,1)S(1)} collective-permute-done((bf16[336,512]{1,0:T(8,128)(2,1)S(1)}, bf16[336,512]{1,0:T(8,128)(2,1)S(1)}, u32[]{:S(2)}, u32[]{:S(2)}) %collective-permute-start.3) | collective-permute-done | bytes 344096 | tf_op jit(solution)/shard_map/ppermute | solution.py:30
  62.0 6.2 %entity_gradients.1 = (f32[8,64,256]{2,1,0:T(8,128)S(1)}, f32[8,64,256]{2,1,0:T(8,128)S(1)}) custom-call(s32[1]{0:T(128)} %bitcast.me_ref, bf16[1024,256]{1,0:T(8,128)(2,1)S(1)} %copy-done.1, bf16[4,256,256]{2,1,0:T(8,128)(2,1)S(1)} %copy-done, s32[8,512]{1,0:T(8,128)S(1)} %get-tuple-element.21.refs_0_, s32[8,512]{1,0:T(8,128)S(1)} %get-tuple-element.24.refs_1_, ...), custom_call_target="tpu_custom_call" | custom-call | flops 4000000000 | bytes 3000000 | tf_op jit(solution)/shard_map/entity_gradients/pallas_call | solution.py:428
  68.1 1.9 %collective-permute-start.4 = (f32[8,64,256]{2,1,0:T(8,128)S(1)}, f32[8,64,256]{2,1,0:T(8,128)S(1)}, u32[]{:S(2)}, u32[]{:S(2)}) collective-permute-start(f32[8,64,256]{2,1,0:T(8,128)S(1)} %get-tuple-element.32), channel_id=1, source_target_pairs={{0,1},{1,0},{2,3},{3,2},{4,5},{5,4},{6,7},{7,6},{8,9},{9,8},{10,11... | collective-permute-start | bytes 1572872 | tf_op jit(solution)/shard_map/ppermute | solution.py:35
  70.1 1.9 %collective-permute-done.4 = f32[8,64,256]{2,1,0:T(8,128)S(1)} collective-permute-done((f32[8,64,256]{2,1,0:T(8,128)S(1)}, f32[8,64,256]{2,1,0:T(8,128)S(1)}, u32[]{:S(2)}, u32[]{:S(2)}) %collective-permute-start.4) | collective-permute-done | bytes 524320 | tf_op jit(solution)/shard_map/ppermute | solution.py:35
  71.9 0.1 fusion
  72.1 2.7 %collective-permute-start.5 = (bf16[2,64,256]{2,1,0:T(8,128)(2,1)S(1)}, bf16[2,64,256]{2,1,0:T(8,128)(2,1)S(1)}, u32[]{:S(2)}, u32[]{:S(2)}) collective-permute-start(bf16[2,64,256]{2,1,0:T(8,128)(2,1)S(1)} %get-tuple-element.38), channel_id=1, source_target_pairs={{0,4},{1,5},{2,6},{3,7},{4,0},{5,1},{6,2},{7,3},{8,12},{9,13},{10,... | collective-permute-start | bytes 196616 | tf_op jit(solution)/shard_map/ppermute | solution.py:35
  74.8 3.6 %collective-permute-start.7 = (bf16[2,64,256]{2,1,0:T(8,128)(2,1)S(1)}, bf16[2,64,256]{2,1,0:T(8,128)(2,1)S(1)}, u32[]{:S(2)}, u32[]{:S(2)}) collective-permute-start(bf16[2,64,256]{2,1,0:T(8,128)(2,1)S(1)} %get-tuple-element.39), channel_id=1, source_target_pairs={{0,12},{1,13},{2,14},{3,15},{4,8},{5,9},{6,10},{7,11},{8,4},{9,5},... | collective-permute-start | bytes 196616 | tf_op jit(solution)/shard_map/ppermute | solution.py:35
  78.4 3.5 %collective-permute-start.6 = (bf16[2,64,256]{2,1,0:T(8,128)(2,1)S(1)}, bf16[2,64,256]{2,1,0:T(8,128)(2,1)S(1)}, u32[]{:S(2)}, u32[]{:S(2)}) collective-permute-start(bf16[2,64,256]{2,1,0:T(8,128)(2,1)S(1)} %get-tuple-element.40), channel_id=1, source_target_pairs={{0,8},{1,9},{2,10},{3,11},{4,12},{5,13},{6,14},{7,15},{8,0},{9,1},... | collective-permute-start | bytes 196616 | tf_op jit(solution)/shard_map/ppermute | solution.py:35
  81.9 0.0 collective-permute-done.5
  81.9 0.2 collective-permute-done.7
  82.1 3.9 %collective-permute-done.6 = bf16[2,64,256]{2,1,0:T(8,128)(2,1)S(1)} collective-permute-done((bf16[2,64,256]{2,1,0:T(8,128)(2,1)S(1)}, bf16[2,64,256]{2,1,0:T(8,128)(2,1)S(1)}, u32[]{:S(2)}, u32[]{:S(2)}) %collective-permute-start.6) | collective-permute-done | bytes 65568 | tf_op jit(solution)/shard_map/ppermute | solution.py:35
  86.1 2.3 %collective-permute-start.8 = (f32[64,256]{1,0:T(8,128)S(1)}, f32[64,256]{1,0:T(8,128)S(1)}, u32[]{:S(2)}, u32[]{:S(2)}) collective-permute-start(f32[64,256]{1,0:T(8,128)S(1)} %get-tuple-element.41), channel_id=1, source_target_pairs={{0,2},{1,3},{2,0},{3,1},{4,6},{5,7},{6,4},{7,5},{8,10},{9,11},{10,... | collective-permute-start | bytes 196616 | tf_op jit(solution)/shard_map/ppermute | solution.py:35
  88.4 3.9 %collective-permute-done.8.got_ref = f32[64,256]{1,0:T(8,128)S(1)} collective-permute-done((f32[64,256]{1,0:T(8,128)S(1)}, f32[64,256]{1,0:T(8,128)S(1)}, u32[]{:S(2)}, u32[]{:S(2)}) %collective-permute-start.8) | collective-permute-done | bytes 65568 | tf_op jit(solution)/shard_map/ppermute | solution.py:35
  92.3 0.0 all-to-all-done.1
  92.3 1.4 %last_sums.1 = (f32[64,256]{1,0:T(8,128)}, f32[32,256]{1,0:T(8,128)}) custom-call(f32[64,256]{1,0:T(8,128)S(1)} %get-tuple-element.42.keep_ref, f32[64,256]{1,0:T(8,128)S(1)} %collective-permute-done.8.got_ref, bf16[4,8,32,256]{3,2,1,0:T(8,128)(2,1)S(1)} %bitcast.11), custom_call_target="tpu_custom_call" | custom-call | tf_op jit(solution)/shard_map/last_sums/pallas_call | solution.py:454
  (4 shorter events, 0.1 us)
Async XLA Ops:
  3.3 21.6 %collective-permute-start = (bf16[1024,256]{1,0:T(8,128)(2,1)}, bf16[1024,256]{1,0:T(8,128)(2,1)S(1)}, u32[]{:S(2)}, u32[]{:S(2)}) collective-permute-start(bf16[1024,256]{1,0:T(8,128)(2,1)} %get-tuple-element.19.refs_0_.slab_ref), channel_id=1, source_target_pairs={{0,496},{1,481},{2,498},{3,483},{4,500},{5,485},{6,502},{7,487},{8... | collective-permute-start | bytes 1572872 | tf_op jit(solution)/shard_map/ppermute | solution.py:30
  24.8 2.3 %copy-start = (bf16[4,256,256]{2,1,0:T(8,128)(2,1)S(1)}, bf16[4,256,256]{2,1,0:T(8,128)(2,1)}, u32[]{:S(2)}) copy-start(bf16[4,256,256]{2,1,0:T(8,128)(2,1)} %ops_hbm.1) | copy-start | bytes 1572868
  24.8 2.3 %copy-start.1 = (bf16[1024,256]{1,0:T(8,128)(2,1)S(1)}, bf16[1024,256]{1,0:T(8,128)(2,1)}, u32[]{:S(2)}) copy-start(bf16[1024,256]{1,0:T(8,128)(2,1)} %get-tuple-element.19.refs_0_.slab_ref) | copy-start | bytes 1572868
  24.9 5.7 %collective-permute-start.1 = (bf16[1024,256]{1,0:T(8,128)(2,1)S(1)}, bf16[1024,256]{1,0:T(8,128)(2,1)S(1)}, u32[]{:S(2)}, u32[]{:S(2)}) collective-permute-start(bf16[1024,256]{1,0:T(8,128)(2,1)S(1)} %after_lists.1.refs_0_), channel_id=1, source_target_pairs={{0,1},{1,0},{2,3},{3,2},{4,5},{5,4},{6,7},{7,6},{8,9},{9,8},{10,11... | collective-permute-start | bytes 1572872 | tf_op jit(solution)/shard_map/ppermute | solution.py:35
  37.4 20.2 %collective-permute-start.2 = (bf16[336,512]{1,0:T(8,128)(2,1)S(1)}, bf16[336,512]{1,0:T(8,128)(2,1)S(1)}, u32[]{:S(2)}, u32[]{:S(2)}) collective-permute-start(bf16[336,512]{1,0:T(8,128)(2,1)S(1)} %get-tuple-element.29), channel_id=1, source_target_pairs={{0,16},{1,33},{2,18},{3,35},{4,20},{5,37},{6,22},{7,39},{8,24},{9,... | collective-permute-start | bytes 1032200 | tf_op jit(solution)/shard_map/ppermute | solution.py:30
  39.3 22.7 %collective-permute-start.3 = (bf16[336,512]{1,0:T(8,128)(2,1)S(1)}, bf16[336,512]{1,0:T(8,128)(2,1)S(1)}, u32[]{:S(2)}, u32[]{:S(2)}) collective-permute-start(bf16[336,512]{1,0:T(8,128)(2,1)S(1)} %get-tuple-element.30), channel_id=1, source_target_pairs={{0,32},{1,17},{2,34},{3,19},{4,36},{5,21},{6,38},{7,23},{8,40},{9,... | collective-permute-start | bytes 1032200 | tf_op jit(solution)/shard_map/ppermute | solution.py:30
  41.2 51.1 %all-to-all-start.1 = ((bf16[32,32,256]{2,1,0:T(8,128)(2,1)}), bf16[32,32,256]{2,1,0:T(8,128)(2,1)S(1)}, u32[]{:S(2)}, u32[]{:S(2)}) async-start(bf16[32,32,256]{2,1,0:T(8,128)(2,1)} %get-tuple-element.33), calls=%async_computation.1 | async-start | bytes 1048576 | tf_op jit(solution)/shard_map/all_to_all | solution.py:39
  68.1 3.8 %collective-permute-start.4 = (f32[8,64,256]{2,1,0:T(8,128)S(1)}, f32[8,64,256]{2,1,0:T(8,128)S(1)}, u32[]{:S(2)}, u32[]{:S(2)}) collective-permute-start(f32[8,64,256]{2,1,0:T(8,128)S(1)} %get-tuple-element.32), channel_id=1, source_target_pairs={{0,1},{1,0},{2,3},{3,2},{4,5},{5,4},{6,7},{7,6},{8,9},{9,8},{10,11... | collective-permute-start | bytes 1572872 | tf_op jit(solution)/shard_map/ppermute | solution.py:35
  72.1 9.8 %collective-permute-start.5 = (bf16[2,64,256]{2,1,0:T(8,128)(2,1)S(1)}, bf16[2,64,256]{2,1,0:T(8,128)(2,1)S(1)}, u32[]{:S(2)}, u32[]{:S(2)}) collective-permute-start(bf16[2,64,256]{2,1,0:T(8,128)(2,1)S(1)} %get-tuple-element.38), channel_id=1, source_target_pairs={{0,4},{1,5},{2,6},{3,7},{4,0},{5,1},{6,2},{7,3},{8,12},{9,13},{10,... | collective-permute-start | bytes 196616 | tf_op jit(solution)/shard_map/ppermute | solution.py:35
  74.8 7.4 %collective-permute-start.7 = (bf16[2,64,256]{2,1,0:T(8,128)(2,1)S(1)}, bf16[2,64,256]{2,1,0:T(8,128)(2,1)S(1)}, u32[]{:S(2)}, u32[]{:S(2)}) collective-permute-start(bf16[2,64,256]{2,1,0:T(8,128)(2,1)S(1)} %get-tuple-element.39), channel_id=1, source_target_pairs={{0,12},{1,13},{2,14},{3,15},{4,8},{5,9},{6,10},{7,11},{8,4},{9,5},... | collective-permute-start | bytes 196616 | tf_op jit(solution)/shard_map/ppermute | solution.py:35
  78.4 7.7 %collective-permute-start.6 = (bf16[2,64,256]{2,1,0:T(8,128)(2,1)S(1)}, bf16[2,64,256]{2,1,0:T(8,128)(2,1)S(1)}, u32[]{:S(2)}, u32[]{:S(2)}) collective-permute-start(bf16[2,64,256]{2,1,0:T(8,128)(2,1)S(1)} %get-tuple-element.40), channel_id=1, source_target_pairs={{0,8},{1,9},{2,10},{3,11},{4,12},{5,13},{6,14},{7,15},{8,0},{9,1},... | collective-permute-start | bytes 196616 | tf_op jit(solution)/shard_map/ppermute | solution.py:35
  86.1 6.2 %collective-permute-start.8 = (f32[64,256]{1,0:T(8,128)S(1)}, f32[64,256]{1,0:T(8,128)S(1)}, u32[]{:S(2)}, u32[]{:S(2)}) collective-permute-start(f32[64,256]{1,0:T(8,128)S(1)} %get-tuple-element.41), channel_id=1, source_target_pairs={{0,2},{1,3},{2,0},{3,1},{4,6},{5,7},{6,4},{7,5},{8,10},{9,11},{10,... | collective-permute-start | bytes 196616 | tf_op jit(solution)/shard_map/ppermute | solution.py:35

commit v6 on v5

--- a/solution.py
+++ b/solution.py
@@ -43,11 +43,7 @@
     return lax.broadcasted_iota(jnp.int32, shape, axis)
 
 
-def pack_kernel(
-    groups, neg_ref, left_ref, right_ref, count_ref, ent_ref, out_ref, slab_ref, sem
-):
-    slab_copy = pltpu.make_async_copy(ent_ref, slab_ref, sem)
-    slab_copy.start()
+def pack_kernel(groups, neg_ref, left_ref, right_ref, count_ref, out_ref):
     hists = []
     for s in range(3):
         high, low = [], []
@@ -69,7 +65,6 @@
         words = hists[2] + (jnp.concatenate(rows + counts, 0) << 16)
         for d in range(line * groups // lines, (line + 1) * groups // lines):
             out_ref[d, 8:16, :] = words
-    slab_copy.wait()
 
 
 def loop(n, step, carry):
@@ -245,8 +240,8 @@
     qg_hbms, pk_refs = refs[2 : 2 + buckets], list(refs[2 + buckets : 2 + 2 * buckets])
     keep_ref, send_ref, rows_ref, mult_ref, ops_ref, qg_ref, pk_ref, sems = refs[2 + 2 * buckets :]
     copies = [
-        pltpu.make_async_copy(ops_hbm, ops_ref, sems.at[0]),
-        pltpu.make_async_copy(pk_refs[0], pk_ref, sems.at[1]),
+        pltpu.make_async_copy(pk_refs[0], pk_ref, sems.at[0]),
+        pltpu.make_async_copy(ops_hbm, ops_ref, sems.at[1]),
     ]
     for s in range(buckets):
         copies.append(pltpu.make_async_copy(qg_hbms[s], qg_ref.at[s], sems.at[2 + s]))
@@ -262,7 +257,8 @@
     share = part_rows // groups
     for step, s in enumerate(list(range(1, buckets)) + [0]):
         pk = pk_refs[s]
-        left_row = lrow_ref[s - 1 : s, :] if s else lrow0_ref[0:1, :]
+        if s == 0:
+            copies[0].wait()
         hist = pk[width : width + 64, :].astype(F32)
         hist = hist[:32] * 32.0 + hist[32:]
         for a in range(8):
@@ -274,13 +270,6 @@
         pos_grad = misc[3:4] + misc[4:5]
         query_t = pk[0:width, :]
         half_t = query_t * 0.5
-        if step == 0:
-            for copy in copies:
-                copy.wait()
-        qgrad_t = qg_ref[s]
-        lgrad_t = jnp.concatenate(
-            [dot(ops_ref[i], qgrad_t[:, 128 * i : 128 * (i + 1)]) for i in range(rel_own)], 1
-        ).astype(BF)
 
         def weigh(n, carry):
             at = n * chunk
@@ -291,12 +280,23 @@
             weight = ngrad * jnp.concatenate([mult] * rel_own, 1) + jnp.where(hit, pos_grad, 0.0)
             high = weight.astype(BF)
             low = (weight - high.astype(F32)).astype(BF)
-            hot = one_hot(left_row, n * chunk, (chunk, slots))
-            rows = dot(high, query_t, NT) + dot(low, query_t, NT) + dot(hot, lgrad_t, NT)
+            rows = dot(high, query_t, NT) + dot(low, query_t, NT)
             rows_ref[pl.ds(at, chunk), :] = rows if step == 0 else rows_ref[pl.ds(at, chunk), :] + rows
             return carry
 
         loop(chunks, weigh, 0)
+    for copy in copies[1:]:
+        copy.wait()
+    lefts = [lrow0_ref[0:1, :]] + [lrow_ref[s - 1 : s, :] for s in range(1, buckets)]
+    grads = []
+    for s in range(buckets):
+        qgrad_t = qg_ref[s]
+        for i in range(rel_own):
+            grads.append(dot(ops_ref[i], qgrad_t[:, 128 * i : 128 * (i + 1)]).astype(BF))
+    lgrad_t = jnp.concatenate(grads, 1)
+    for n in range(chunks):
+        hot = [one_hot(left, n * chunk, (chunk, slots)) for left in lefts]
+        rows_ref[pl.ds(n * chunk, chunk), :] += dot(jnp.concatenate(hot, 1), lgrad_t, NT)
     for n in range(groups):
         to = me ^ (((n >> 1) & 3) * 4 + (n & 1) * 2 + (n >> 3))
         block = rows_ref[pl.ds(pl.multiple_of(to * share, share), share), :]
@@ -307,17 +307,11 @@
             send_ref[n - half] = block
 
 
-def finish_kernel(keep_ref, got_ref, parts_hbm, ent_ref, rel_ref, parts_ref, sems):
-    cuts = parts_ref.shape[0]
-    copies = [pltpu.make_async_copy(parts_hbm.at[n], parts_ref.at[n], sems.at[n]) for n in range(cuts)]
-    for copy in copies:
-        copy.start()
+def finish_kernel(keep_ref, got_ref, parts_ref, ent_ref, rel_ref):
     ent_ref[...] = keep_ref[...] + got_ref[...]
-    total = None
-    for n in range(cuts):
-        copies[n].wait()
-        part = jnp.sum(parts_ref[n].astype(F32), axis=0)
-        total = part if total is None else total + part
+    total = parts_ref[0].astype(F32)
+    for n in range(1, parts_ref.shape[0]):
+        total = total + parts_ref[n].astype(F32)
     rel_ref[...] = total
 
 
@@ -336,25 +330,20 @@
     limit = pltpu.CompilerParams(vmem_limit_bytes=12 * 1024 * 1024)
     small = pltpu.CompilerParams(vmem_limit_bytes=2 * 1024 * 1024)
 
-    packed, slab = pl.pallas_call(
+    packed = pl.pallas_call(
         functools.partial(pack_kernel, groups),
-        out_shape=(
-            jax.ShapeDtypeStruct((groups, 16, 128), jnp.int32),
-            jax.ShapeDtypeStruct(entities.shape, BF),
-        ),
-        in_specs=[VMEM] * 4 + [HBM],
-        out_specs=(VMEM, VMEM),
-        scratch_shapes=[pltpu.SemaphoreType.DMA],
+        out_shape=jax.ShapeDtypeStruct((groups, 16, 128), jnp.int32),
+        in_specs=[VMEM] * 4,
+        out_specs=VMEM,
         name="pack_lists",
     )(
         negatives.reshape(buckets, neg_count // 128, 128),
         left_rows.reshape(buckets, slot_count // 128, 128),
         right_rows.reshape(buckets, slot_count // 128, 128),
         counts.reshape(buckets, 1, relations),
-        entities,
     )
     received = exchanged(packed, "span")
-    near = shifted(slab, -1, -2)
+    near = shifted(entities, -1, -2)
     near = pl.pallas_call(
         tie_kernel,
         out_shape=jax.ShapeDtypeStruct(entities.shape, BF),
@@ -403,7 +392,7 @@
             flops=1_400_000_000, bytes_accessed=2_000_000, transcendentals=500_000
         ),
         name="own_bucket",
-    )(me, received, slab, operators)
+    )(me, received, entities, operators)
     others = tuple(range(1, buckets))
     rel_parts, lrow_other, *packs = pl.pallas_call(
         functools.partial(forward_kernel, buckets, others, neg_scale),
@@ -443,26 +432,21 @@
             flops=4_000_000_000, bytes_accessed=3_000_000, transcendentals=1_600_000
         ),
         name="entity_gradients",
-    )(me, slab, operators, lrow_own, lrow_other, *grads, *packs)
+    )(me, entities, operators, lrow_own, lrow_other, *grads, *packs)
 
     total = keep + swapped(send, 1)
     total = total.reshape(4, 2, share, width)
     got = [swapped(total[x].astype(BF), 4 * x) for x in (1, 2, 3)]
     total = total[0] + sum(part.astype(F32) for part in got)
     held = rel_own * width // doms
-    rel_arrived = rel_arrived.reshape(4, doms // 4, held, width)
     entity_share, rel_share = pl.pallas_call(
         finish_kernel,
         out_shape=(
             jax.ShapeDtypeStruct((share, width), F32),
             jax.ShapeDtypeStruct((held, width), F32),
         ),
-        in_specs=[VMEM, VMEM, HBM],
+        in_specs=[VMEM] * 3,
         out_specs=(VMEM, VMEM),
-        scratch_shapes=[
-            pltpu.VMEM(rel_arrived.shape, BF),
-            pltpu.SemaphoreType.DMA((4,)),
-        ],
         compiler_params=small,
         name="last_sums",
     )(total[0], swapped(total[1], 2), rel_arrived)

time: 95.5 us -> 92.5 us (0.969)
  Pallas kernels: 20.5 us -> 18.2 us
  starting transfers between devices: 39.5 us -> 38.4 us
    ppermute x6, waiting for transfers between devices: 9.92 us -> 11.2 us  [swapped(): return lax.ppermute(value, 'span', [(i, i ^ bits) for i in range(groups)])]
  transfers between devices with their start and end apart: 10 -> 10, of which waited for: 5 -> 5; matrix products, arithmetic and copies ran while one was open for 0% -> 0% of each run, Pallas kernels for 10% -> 12%
where the time goes in v6:
time: 92.5 us; the launch traced here: 91 us
  starting transfers between devices  38.4 us (42%)
  blocking collectives  18.4 us (20%)
  Pallas kernels  18.2 us (20%)
  waiting for transfers between devices  14.9 us (16%)
    all_to_all x1, blocking collectives, exchanged(): return lax.all_to_all(value, axis, split_axis=0, concat_axis=0, tiled=True)  18.4 us
    ppermute x6, starting transfers between devices, swapped(): return lax.ppermute(value, 'span', [(i, i ^ bits) for i in range(groups)])  16.1 us
    all_to_all x1, starting transfers between devices, exchanged(): return lax.all_to_all(value, axis, split_axis=0, concat_axis=0, tiled=True)  15.4 us
    ppermute x6, waiting for transfers between devices, swapped(): return lax.ppermute(value, 'span', [(i, i ^ bits) for i in range(groups)])  11.2 us
    ppermute x3, starting transfers between devices, shifted(): return lax.ppermute(value, ('dom', 'span'), pairs)  6.99 us
    pallas_call x1, Pallas kernels, shards(): pl.pallas_call(functools.partial(forward_kernel, buckets, others, neg_sca...  6.88 us
    pallas_call x1, Pallas kernels, shards(): pl.pallas_call(functools.partial(entity_kernel, buckets, neg_scale, group...  5.43 us
    ppermute x3, waiting for transfers between devices, shifted(): return lax.ppermute(value, ('dom', 'span'), pairs)  3.79 us
  transfers between devices with their start and end apart: 10, of which 5 were waited for; matrix products, arithmetic and copies ran while one was open for 0% of the time, Pallas kernels for 12%

profile of v6, /device:TPU:24, one launch (start us, length us, event | category | flops | bytes accessed | tf_op | source)
XLA Modules:
  0.0 91.0 jit_solution(11736960261294459087)
XLA Ops:
  0.6 3.1 %collective-permute-start = (bf16[1024,256]{1,0:T(8,128)(2,1)}, bf16[1024,256]{1,0:T(8,128)(2,1)S(1)}, u32[]{:S(2)}, u32[]{:S(2)}) collective-permute-start(bf16[1024,256]{1,0:T(8,128)(2,1)} %slab_ref.1), channel_id=1, source_target_pairs={{0,496},{1,481},{2,498},{3,483},{4,500},{5,485},{6,502},{7,487},{8... | collective-permute-start | bytes 1572872 | tf_op jit(solution)/shard_map/ppermute | solution.py:30
  3.8 1.7 %pack_lists.1 = s32[16,16,128]{2,1,0:T(8,128)} custom-call(s32[3,8,128]{2,1,0:T(8,128)} %bitcast.10, s32[3,4,128]{2,1,0:T(4,128)} %bitcast.11, s32[3,4,128]{2,1,0:T(4,128)} %bitcast.12, s32[3,1,64]{2,1,0:T(1,128)} %bitcast.13), custom_call_target="tpu_custom_call" | custom-call | tf_op jit(solution)/shard_map/pack_lists/pallas_call | solution.py:333
  5.5 18.4 %all_to_all.10.x_ref.first_ref = s32[16,16,128]{2,1,0:T(8,128)S(1)} all-to-all(s32[16,16,128]{2,1,0:T(8,128)} %pack_lists.1), channel_id=1, replica_groups=mesh['dom'=32,'span'=16] {'span'}, dimensions={0} | all-to-all | bytes 262144 | tf_op jit(solution)/shard_map/all_to_all | solution.py:39
  23.9 0.0 copy-start
  23.9 0.0 copy-start.1
  23.9 0.0 collective-permute-done.held_ref
  24.0 2.2 %collective-permute-start.1 = (bf16[1024,256]{1,0:T(8,128)(2,1)S(1)}, bf16[1024,256]{1,0:T(8,128)(2,1)S(1)}, u32[]{:S(2)}, u32[]{:S(2)}) collective-permute-start(bf16[1024,256]{1,0:T(8,128)(2,1)S(1)} %after_lists.1.refs_0_), channel_id=1, source_target_pairs={{0,1},{1,0},{2,3},{3,2},{4,5},{5,4},{6,7},{7,6},{8,9},{9,8},{10,11... | collective-permute-start | bytes 1572872 | tf_op jit(solution)/shard_map/ppermute | solution.py:35
  26.2 0.0 copy-done
  26.2 0.0 copy-done.1
  26.2 3.5 %own_bucket.1 = (f32[4,256,256]{2,1,0:T(8,128)S(1)}, bf16[256,1024]{1,0:T(8,128)(2,1)S(1)}, s32[8,512]{1,0:T(8,128)S(1)}, bf16[256,512]{1,0:T(8,128)(2,1)}, bf16[336,512]{1,0:T(8,128)(2,1)}) custom-call(s32[1]{0:T(128)} %bitcast.me_ref, s32[16,16,128]{2,1,0:T(8,128)S(1)} %all_to_all.10.x_ref.first_ref, bf16[1024,256]{1,0:T(8,128)(2,1)S(1)} %copy-done, ...), custom_call_target="tpu_custom_call" | custom-call | flops 1400000000 | bytes 2000000 | tf_op jit(solution)/shard_map/own_bucket/pallas_call | solution.py:379
  29.7 0.0 collective-permute-done.1.refs_1_
  29.7 6.9 %other_buckets.1 = (bf16[32,32,256]{2,1,0:T(8,128)(2,1)}, s32[8,512]{1,0:T(8,128)S(1)}, bf16[256,512]{1,0:T(8,128)(2,1)}, bf16[256,512]{1,0:T(8,128)(2,1)}, bf16...) custom-call(s32[1]{0:T(128)} %bitcast.me_ref, s32[16,16,128]{2,1,0:T(8,128)S(1)} %all_to_all.10.x_ref.first_ref, ...), custom_call_target="tpu_custom_call" | custom-call | flops 3000000000 | bytes 3000000 | tf_op jit(solution)/shard_map/other_buckets/pallas_call | solution.py:397
  36.6 1.9 %collective-permute-start.2 = (bf16[336,512]{1,0:T(8,128)(2,1)}, bf16[336,512]{1,0:T(8,128)(2,1)S(1)}, u32[]{:S(2)}, u32[]{:S(2)}) collective-permute-start(bf16[336,512]{1,0:T(8,128)(2,1)} %get-tuple-element.25), channel_id=1, source_target_pairs={{0,16},{1,33},{2,18},{3,35},{4,20},{5,37},{6,22},{7,39},{8,24},{9,... | collective-permute-start | bytes 1032200 | tf_op jit(solution)/shard_map/ppermute | solution.py:30
  38.5 1.9 %collective-permute-start.3 = (bf16[336,512]{1,0:T(8,128)(2,1)S(1)}, bf16[336,512]{1,0:T(8,128)(2,1)S(1)}, u32[]{:S(2)}, u32[]{:S(2)}) collective-permute-start(bf16[336,512]{1,0:T(8,128)(2,1)S(1)} %get-tuple-element.26), channel_id=1, source_target_pairs={{0,32},{1,17},{2,34},{3,19},{4,36},{5,21},{6,38},{7,23},{8,40},{9,... | collective-permute-start | bytes 1032200 | tf_op jit(solution)/shard_map/ppermute | solution.py:30
  40.4 15.4 %all-to-all-start.1 = ((bf16[32,32,256]{2,1,0:T(8,128)(2,1)}), bf16[32,32,256]{2,1,0:T(8,128)(2,1)S(1)}, u32[]{:S(2)}, u32[]{:S(2)}) async-start(bf16[32,32,256]{2,1,0:T(8,128)(2,1)} %get-tuple-element.29), calls=%async_computation.1 | async-start | bytes 1048576 | tf_op jit(solution)/shard_map/all_to_all | solution.py:39
  55.8 0.0 collective-permute-done.2.refs_6_
  55.8 3.8 %collective-permute-done.3.refs_7_ = bf16[336,512]{1,0:T(8,128)(2,1)S(1)} collective-permute-done((bf16[336,512]{1,0:T(8,128)(2,1)S(1)}, bf16[336,512]{1,0:T(8,128)(2,1)S(1)}, u32[]{:S(2)}, u32[]{:S(2)}) %collective-permute-start.3) | collective-permute-done | bytes 344096 | tf_op jit(solution)/shard_map/ppermute | solution.py:30
  59.6 5.4 %entity_gradients.1 = (f32[8,64,256]{2,1,0:T(8,128)S(1)}, f32[8,64,256]{2,1,0:T(8,128)S(1)}) custom-call(s32[1]{0:T(128)} %bitcast.me_ref, bf16[1024,256]{1,0:T(8,128)(2,1)S(1)} %copy-done, bf16[4,256,256]{2,1,0:T(8,128)(2,1)S(1)} %copy-done.1, s32[8,512]{1,0:T(8,128)S(1)} %get-tuple-element.17.refs_0_, s32[8,512]{1,0:T(8,128)S(1)} %get-tuple-element.20.refs_1_, ...), custom_call_target="tpu_custom_call" | custom-call | flops 4000000000 | bytes 3000000 | tf_op jit(solution)/shard_map/entity_gradients/pallas_call | solution.py:417
  65.1 1.9 %collective-permute-start.4 = (f32[8,64,256]{2,1,0:T(8,128)S(1)}, f32[8,64,256]{2,1,0:T(8,128)S(1)}, u32[]{:S(2)}, u32[]{:S(2)}) collective-permute-start(f32[8,64,256]{2,1,0:T(8,128)S(1)} %get-tuple-element.28), channel_id=1, source_target_pairs={{0,1},{1,0},{2,3},{3,2},{4,5},{5,4},{6,7},{7,6},{8,9},{9,8},{10,11... | collective-permute-start | bytes 1572872 | tf_op jit(solution)/shard_map/ppermute | solution.py:35
  67.0 1.9 %collective-permute-done.4 = f32[8,64,256]{2,1,0:T(8,128)S(1)} collective-permute-done((f32[8,64,256]{2,1,0:T(8,128)S(1)}, f32[8,64,256]{2,1,0:T(8,128)S(1)}, u32[]{:S(2)}, u32[]{:S(2)}) %collective-permute-start.4) | collective-permute-done | bytes 524320 | tf_op jit(solution)/shard_map/ppermute | solution.py:35
  68.9 0.1 fusion
  69.0 4.1 %collective-permute-start.5 = (bf16[2,64,256]{2,1,0:T(8,128)(2,1)S(1)}, bf16[2,64,256]{2,1,0:T(8,128)(2,1)S(1)}, u32[]{:S(2)}, u32[]{:S(2)}) collective-permute-start(bf16[2,64,256]{2,1,0:T(8,128)(2,1)S(1)} %get-tuple-element.34), channel_id=1, source_target_pairs={{0,4},{1,5},{2,6},{3,7},{4,0},{5,1},{6,2},{7,3},{8,12},{9,13},{10,... | collective-permute-start | bytes 196616 | tf_op jit(solution)/shard_map/ppermute | solution.py:35
  73.1 3.3 %collective-permute-start.7 = (bf16[2,64,256]{2,1,0:T(8,128)(2,1)S(1)}, bf16[2,64,256]{2,1,0:T(8,128)(2,1)S(1)}, u32[]{:S(2)}, u32[]{:S(2)}) collective-permute-start(bf16[2,64,256]{2,1,0:T(8,128)(2,1)S(1)} %get-tuple-element.35), channel_id=1, source_target_pairs={{0,12},{1,13},{2,14},{3,15},{4,8},{5,9},{6,10},{7,11},{8,4},{9,5},... | collective-permute-start | bytes 196616 | tf_op jit(solution)/shard_map/ppermute | solution.py:35
  76.4 2.6 %collective-permute-start.6 = (bf16[2,64,256]{2,1,0:T(8,128)(2,1)S(1)}, bf16[2,64,256]{2,1,0:T(8,128)(2,1)S(1)}, u32[]{:S(2)}, u32[]{:S(2)}) collective-permute-start(bf16[2,64,256]{2,1,0:T(8,128)(2,1)S(1)} %get-tuple-element.36), channel_id=1, source_target_pairs={{0,8},{1,9},{2,10},{3,11},{4,12},{5,13},{6,14},{7,15},{8,0},{9,1},... | collective-permute-start | bytes 196616 | tf_op jit(solution)/shard_map/ppermute | solution.py:35
  79.0 0.0 collective-permute-done.5
  79.0 1.4 %collective-permute-done.7 = bf16[2,64,256]{2,1,0:T(8,128)(2,1)S(1)} collective-permute-done((bf16[2,64,256]{2,1,0:T(8,128)(2,1)S(1)}, bf16[2,64,256]{2,1,0:T(8,128)(2,1)S(1)}, u32[]{:S(2)}, u32[]{:S(2)}) %collective-permute-start.7) | collective-permute-done | bytes 65568 | tf_op jit(solution)/shard_map/ppermute | solution.py:35
  80.5 3.6 %collective-permute-done.6 = bf16[2,64,256]{2,1,0:T(8,128)(2,1)S(1)} collective-permute-done((bf16[2,64,256]{2,1,0:T(8,128)(2,1)S(1)}, bf16[2,64,256]{2,1,0:T(8,128)(2,1)S(1)}, u32[]{:S(2)}, u32[]{:S(2)}) %collective-permute-start.6) | collective-permute-done | bytes 65568 | tf_op jit(solution)/shard_map/ppermute | solution.py:35
  84.1 1.9 %collective-permute-start.8 = (f32[64,256]{1,0:T(8,128)S(1)}, f32[64,256]{1,0:T(8,128)S(1)}, u32[]{:S(2)}, u32[]{:S(2)}) collective-permute-start(f32[64,256]{1,0:T(8,128)S(1)} %get-tuple-element.37), channel_id=1, source_target_pairs={{0,2},{1,3},{2,0},{3,1},{4,6},{5,7},{6,4},{7,5},{8,10},{9,11},{10,... | collective-permute-start | bytes 196616 | tf_op jit(solution)/shard_map/ppermute | solution.py:35
  86.1 4.2 %collective-permute-done.8.got_ref = f32[64,256]{1,0:T(8,128)S(1)} collective-permute-done((f32[64,256]{1,0:T(8,128)S(1)}, f32[64,256]{1,0:T(8,128)S(1)}, u32[]{:S(2)}, u32[]{:S(2)}) %collective-permute-start.8) | collective-permute-done | bytes 65568 | tf_op jit(solution)/shard_map/ppermute | solution.py:35
  90.3 0.0 all-to-all-done.1.parts_ref
  90.3 0.7 last_sums.1
  (4 shorter events, 0.1 us)
Async XLA Ops:
  0.6 23.3 %collective-permute-start = (bf16[1024,256]{1,0:T(8,128)(2,1)}, bf16[1024,256]{1,0:T(8,128)(2,1)S(1)}, u32[]{:S(2)}, u32[]{:S(2)}) collective-permute-start(bf16[1024,256]{1,0:T(8,128)(2,1)} %slab_ref.1), channel_id=1, source_target_pairs={{0,496},{1,481},{2,498},{3,483},{4,500},{5,485},{6,502},{7,487},{8... | collective-permute-start | bytes 1572872 | tf_op jit(solution)/shard_map/ppermute | solution.py:30
  23.9 2.3 %copy-start = (bf16[1024,256]{1,0:T(8,128)(2,1)S(1)}, bf16[1024,256]{1,0:T(8,128)(2,1)}, u32[]{:S(2)}) copy-start(bf16[1024,256]{1,0:T(8,128)(2,1)} %slab_ref.1) | copy-start | bytes 1572868
  23.9 2.3 %copy-start.1 = (bf16[4,256,256]{2,1,0:T(8,128)(2,1)S(1)}, bf16[4,256,256]{2,1,0:T(8,128)(2,1)}, u32[]{:S(2)}) copy-start(bf16[4,256,256]{2,1,0:T(8,128)(2,1)} %ops_hbm.1) | copy-start | bytes 1572868
  24.0 5.7 %collective-permute-start.1 = (bf16[1024,256]{1,0:T(8,128)(2,1)S(1)}, bf16[1024,256]{1,0:T(8,128)(2,1)S(1)}, u32[]{:S(2)}, u32[]{:S(2)}) collective-permute-start(bf16[1024,256]{1,0:T(8,128)(2,1)S(1)} %after_lists.1.refs_0_), channel_id=1, source_target_pairs={{0,1},{1,0},{2,3},{3,2},{4,5},{5,4},{6,7},{7,6},{8,9},{9,8},{10,11... | collective-permute-start | bytes 1572872 | tf_op jit(solution)/shard_map/ppermute | solution.py:35
  36.6 19.3 %collective-permute-start.2 = (bf16[336,512]{1,0:T(8,128)(2,1)}, bf16[336,512]{1,0:T(8,128)(2,1)S(1)}, u32[]{:S(2)}, u32[]{:S(2)}) collective-permute-start(bf16[336,512]{1,0:T(8,128)(2,1)} %get-tuple-element.25), channel_id=1, source_target_pairs={{0,16},{1,33},{2,18},{3,35},{4,20},{5,37},{6,22},{7,39},{8,24},{9,... | collective-permute-start | bytes 1032200 | tf_op jit(solution)/shard_map/ppermute | solution.py:30
  38.5 21.1 %collective-permute-start.3 = (bf16[336,512]{1,0:T(8,128)(2,1)S(1)}, bf16[336,512]{1,0:T(8,128)(2,1)S(1)}, u32[]{:S(2)}, u32[]{:S(2)}) collective-permute-start(bf16[336,512]{1,0:T(8,128)(2,1)S(1)} %get-tuple-element.26), channel_id=1, source_target_pairs={{0,32},{1,17},{2,34},{3,19},{4,36},{5,21},{6,38},{7,23},{8,40},{9,... | collective-permute-start | bytes 1032200 | tf_op jit(solution)/shard_map/ppermute | solution.py:30
  40.4 49.9 %all-to-all-start.1 = ((bf16[32,32,256]{2,1,0:T(8,128)(2,1)}), bf16[32,32,256]{2,1,0:T(8,128)(2,1)S(1)}, u32[]{:S(2)}, u32[]{:S(2)}) async-start(bf16[32,32,256]{2,1,0:T(8,128)(2,1)} %get-tuple-element.29), calls=%async_computation.1 | async-start | bytes 1048576 | tf_op jit(solution)/shard_map/all_to_all | solution.py:39
  65.1 3.8 %collective-permute-start.4 = (f32[8,64,256]{2,1,0:T(8,128)S(1)}, f32[8,64,256]{2,1,0:T(8,128)S(1)}, u32[]{:S(2)}, u32[]{:S(2)}) collective-permute-start(f32[8,64,256]{2,1,0:T(8,128)S(1)} %get-tuple-element.28), channel_id=1, source_target_pairs={{0,1},{1,0},{2,3},{3,2},{4,5},{5,4},{6,7},{7,6},{8,9},{9,8},{10,11... | collective-permute-start | bytes 1572872 | tf_op jit(solution)/shard_map/ppermute | solution.py:35
  69.0 10.0 %collective-permute-start.5 = (bf16[2,64,256]{2,1,0:T(8,128)(2,1)S(1)}, bf16[2,64,256]{2,1,0:T(8,128)(2,1)S(1)}, u32[]{:S(2)}, u32[]{:S(2)}) collective-permute-start(bf16[2,64,256]{2,1,0:T(8,128)(2,1)S(1)} %get-tuple-element.34), channel_id=1, source_target_pairs={{0,4},{1,5},{2,6},{3,7},{4,0},{5,1},{6,2},{7,3},{8,12},{9,13},{10,... | collective-permute-start | bytes 196616 | tf_op jit(solution)/shard_map/ppermute | solution.py:35
  73.1 7.4 %collective-permute-start.7 = (bf16[2,64,256]{2,1,0:T(8,128)(2,1)S(1)}, bf16[2,64,256]{2,1,0:T(8,128)(2,1)S(1)}, u32[]{:S(2)}, u32[]{:S(2)}) collective-permute-start(bf16[2,64,256]{2,1,0:T(8,128)(2,1)S(1)} %get-tuple-element.35), channel_id=1, source_target_pairs={{0,12},{1,13},{2,14},{3,15},{4,8},{5,9},{6,10},{7,11},{8,4},{9,5},... | collective-permute-start | bytes 196616 | tf_op jit(solution)/shard_map/ppermute | solution.py:35
  76.4 7.7 %collective-permute-start.6 = (bf16[2,64,256]{2,1,0:T(8,128)(2,1)S(1)}, bf16[2,64,256]{2,1,0:T(8,128)(2,1)S(1)}, u32[]{:S(2)}, u32[]{:S(2)}) collective-permute-start(bf16[2,64,256]{2,1,0:T(8,128)(2,1)S(1)} %get-tuple-element.36), channel_id=1, source_target_pairs={{0,8},{1,9},{2,10},{3,11},{4,12},{5,13},{6,14},{7,15},{8,0},{9,1},... | collective-permute-start | bytes 196616 | tf_op jit(solution)/shard_map/ppermute | solution.py:35
  84.1 6.2 %collective-permute-start.8 = (f32[64,256]{1,0:T(8,128)S(1)}, f32[64,256]{1,0:T(8,128)S(1)}, u32[]{:S(2)}, u32[]{:S(2)}) collective-permute-start(f32[64,256]{1,0:T(8,128)S(1)} %get-tuple-element.37), channel_id=1, source_target_pairs={{0,2},{1,3},{2,0},{3,1},{4,6},{5,7},{6,4},{7,5},{8,10},{9,11},{10,... | collective-permute-start | bytes 196616 | tf_op jit(solution)/shard_map/ppermute | solution.py:35

commit v7 on v6

v7 whole, which is shorter than its diff:
```python
import functools

import jax
import jax.numpy as jnp
from jax import lax
from jax.experimental import pallas as pl
from jax.experimental.pallas import tpu as pltpu
from jax.sharding import PartitionSpec as P

BF = jnp.bfloat16
F32 = jnp.float32
NT = (((1,), (1,)), ((), ()))
TN = (((0,), (0,)), ((), ()))
VMEM = pl.BlockSpec(memory_space=pltpu.VMEM)
SMEM = pl.BlockSpec(memory_space=pltpu.SMEM)
HBM = pl.BlockSpec(memory_space=pltpu.HBM)


def dot(a, b, dims=(((1,), (0,)), ((), ()))):
    return lax.dot_general(a, b, dims, preferred_element_type=F32)


def shifted(value, step, other):
    doms, groups = lax.axis_size("dom"), lax.axis_size("span")
    pairs = []
    for p in range(doms):
        for c in range(groups):
            to = (p + (other if c & 1 else step)) % doms
            pairs.append((p * groups + c, to * groups + c))
    return lax.ppermute(value, ("dom", "span"), pairs)


def swapped(value, bits):
    groups = lax.axis_size("span")
    return lax.ppermute(value, "span", [(i, i ^ bits) for i in range(groups)])


def exchanged(value, axis):
    return lax.all_to_all(value, axis, split_axis=0, concat_axis=0, tiled=True)


def iota(shape, axis):
    return lax.broadcasted_iota(jnp.int32, shape, axis)


def pack_kernel(groups, neg_ref, left_ref, right_ref, count_ref, out_ref):
    hists = []
    for s in range(3):
        high, low = [], []
        for q in range(neg_ref.shape[1]):
            row = neg_ref[s, q : q + 1, :]
            high.append((iota((16, 128), 0) == (row >> 7)).astype(F32).astype(BF))
            low.append((iota((128, 128), 0) == (row & 127)).astype(F32).astype(BF))
        hist = dot(jnp.concatenate(high, 1), jnp.concatenate(low, 1), NT)[:8]
        hists.append(hist.astype(jnp.int32))
    words = hists[0] + (hists[1] << 16)
    for d in range(groups):
        out_ref[d, 0:8, :] = words
    lines = left_ref.shape[1]
    counts = [count_ref[s] for s in range(3)]
    counts = counts + [jnp.zeros(counts[0].shape, jnp.int32)]
    counts = [jnp.concatenate(counts[:2], 1), jnp.concatenate(counts[2:], 1)]
    for line in range(lines):
        rows = [ref[s, line : line + 1, :] for ref in (left_ref, right_ref) for s in range(3)]
        words = hists[2] + (jnp.concatenate(rows + counts, 0) << 16)
        for d in range(line * groups // lines, (line + 1) * groups // lines):
            out_ref[d, 8:16, :] = words


def loop(n, step, carry):
    for i in range(n):
        carry = step(i, carry)
    return carry


def tie_kernel(held_ref, first_ref, out_ref):
    out_ref[...] = held_ref[...]


def one_hot(rows, at, shape):
    return ((iota(shape, 0) + at) == rows).astype(F32).astype(BF)


def spread_counts(hist, groups, mult_ref, a):
    hist = jnp.broadcast_to(hist[:, None, :], (groups, 8, 128)).reshape(128, 128)
    mult_ref[128 * a : 128 * (a + 1), :] = hist.T


def forward_kernel(turn, neg_scale, *refs):
    first, last = turn == 0, turn == 2
    olds = (0, 2, 1)[turn]
    me_ref, x_ref, slab, ops_hbm = refs[:4]
    refs = refs[4:]
    if not first:
        et0_ref, sum_ref = refs[:2]
        refs = refs[2:]
    old_refs, refs = refs[:olds], refs[olds:]
    if first:
        et0_ref, rel_acc = refs[:2]
        refs = refs[2:]
    elif last:
        rel_ref, refs = refs[0], refs[1:]
    else:
        rel_acc, refs = refs[0], refs[1:]
    lrow_ref, qg_ref, pk = refs[:3]
    old_hbms, refs = refs[3 : 3 + olds], refs[3 + olds :]
    oh_ref, whi_ref, wlo_ref, mult_ref, ops_ref, et_ref, ops_sem, old_sems = refs[:8]
    if last:
        rel_acc, qg_hbm, qg_ref, qg_sem = refs[8], qg_ref, refs[9], refs[10]
    ops_copy = pltpu.make_async_copy(ops_hbm, ops_ref, ops_sem)
    ops_copy.start()
    old_copies = [
        pltpu.make_async_copy(old_refs[n], old_hbms[n], old_sems.at[n]) for n in range(olds)
    ]
    for copy in old_copies:
        copy.start()
    rel_own, width, _ = ops_hbm.shape
    groups = x_ref.shape[0]
    part_rows = slab.shape[0]
    slots = rel_own * 128
    chunk = 256
    chunks = part_rows // chunk
    me = me_ref[0]
    core = me & 1

    lane_row = iota((128, slots), 0)
    lane = iota((128, slots), 1)
    relation, slot = lane >> 7, lane & 7
    per_line = 128 // (8 * rel_own)
    pick_slot = (lane_row == (me % per_line) * (8 * rel_own) + relation * 8 + slot)
    pick_slot = pick_slot.astype(F32).astype(BF)
    count_lane = me * rel_own + relation
    lane = iota((groups, slots), 1)
    own_group = iota((groups, slots), 0) == ((lane >> 3) & (groups - 1))
    slot_row = iota((1, slots), 1) & 7

    def own(values):
        return jnp.sum(jnp.where(own_group, values, 0.0), axis=0, keepdims=True)

    def narrow(values):
        return values.astype(F32).astype(BF)

    s = (0, 1 + core, 2 - core)[turn]
    left, right = x_ref[:, 8 + s, :] >> 16, x_ref[:, 11 + s, :] >> 16
    parts = [left >> 5, left & 31, right >> 5, right & 31]
    parts = dot(narrow(jnp.concatenate(parts, 0)), pick_slot)
    parts = [own(parts[groups * q : groups * (q + 1)]) for q in range(4)]
    left_row = (parts[0] * 32.0 + parts[1]).astype(jnp.int32)
    right_row = (parts[2] * 32.0 + parts[3]).astype(jnp.int32)
    pick_count = narrow(lane_row == count_lane + (s % 2) * (groups * rel_own))
    count_row = own(dot(narrow(x_ref[:, 14 + s // 2, :] >> 16), pick_count))
    live = (count_row.astype(jnp.int32) > slot_row).astype(F32)
    lrow_ref[0:1, :] = left_row

    highs, lows = [], []
    for a in range(8):
        hist = (x_ref[:, (s // 2) * 8 + a, :] >> (16 * (s % 2))) & 65535
        highs.append(hist >> 5)
        lows.append(hist & 31)
        spread_counts(hist.astype(F32), groups, mult_ref, a)
    for q, group in enumerate([highs[:4], highs[4:], lows[:4], lows[4:]]):
        at = width + 16 * q
        pk[at : at + 16, :] = narrow(jnp.concatenate(group, 1))

    slab_t = et0_ref if first else et_ref
    slab_t[...] = slab[...].T

    def left_hot(n, carry):
        at = n * chunk
        oh_ref[pl.ds(at, chunk), :] = one_hot(left_row, n * chunk, (chunk, slots))
        return carry

    def right_hot(n, carry):
        at = n * chunk
        oh_ref[pl.ds(at, chunk), :] = one_hot(right_row, n * chunk, (chunk, slots))
        return carry

    loop(chunks, left_hot, 0)
    left_t = dot(et0_ref[...], oh_ref[...]).astype(BF)
    ops_copy.wait()
    query_t = jnp.concatenate(
        [dot(ops_ref[i], left_t[:, 128 * i : 128 * (i + 1)], TN) for i in range(rel_own)], 1
    ).astype(BF)
    pk[0:width, :] = query_t
    half_t = query_t * 0.5
    loop(chunks, right_hot, 0)
    right_t = dot(slab_t[...], oh_ref[...])
    positive = jnp.sum(query_t.astype(F32) * right_t, axis=0, keepdims=True)
    pos_grad = -live * jax.nn.sigmoid(-positive)
    pos_high = pos_grad.astype(BF)
    pos_low = (pos_grad - pos_high.astype(F32)).astype(BF)
    misc = [narrow(parts[2]), narrow(parts[3]), narrow(live), pos_high, pos_low]
    misc = [row.astype(F32) for row in misc] + [jnp.zeros((11, slots), F32)]
    pk[width + 64 : width + 80, :] = jnp.concatenate(misc, 0).astype(BF)
    factor = live * (0.5 * neg_scale)

    def weigh(n, carry):
        at = n * chunk
        level = jnp.tanh(dot(slab[pl.ds(at, chunk), :], half_t))
        ngrad = (level * factor + factor).astype(BF).astype(F32)
        mult = mult_ref[pl.ds(at, chunk), :]
        weight = ngrad * jnp.concatenate([mult] * rel_own, 1)
        high = weight.astype(BF)
        whi_ref[pl.ds(at, chunk), :] = high
        wlo_ref[pl.ds(at, chunk), :] = (weight - high.astype(F32)).astype(BF)
        return carry

    loop(chunks, weigh, 0)
    qgrad_t = dot(slab_t[...], whi_ref[...]) + dot(slab_t[...], wlo_ref[...])
    qgrad_t = (qgrad_t + right_t * pos_grad).astype(BF)
    qg_ref[...] = qgrad_t
    if last:
        qg_copy = pltpu.make_async_copy(qg_ref, qg_hbm, qg_sem)
        qg_copy.start()
    for i in range(rel_own):
        cols = slice(128 * i, 128 * (i + 1))
        outer = dot(left_t[:, cols], qgrad_t[:, cols], NT)
        rel_acc[i] = outer if first else sum_ref[i] + outer

    for copy in old_copies:
        copy.wait()
    if not last:
        return
    doms, held, _ = rel_ref.shape
    held = held // rel_own
    for d in range(doms):
        block = [rel_acc[i, held * d : held * (d + 1), :] for i in range(rel_own)]
        rel_ref[d] = jnp.concatenate(block, 0).astype(BF)
    qg_copy.wait()


def right_rows_added(neg_scale, groups, pk, slab_ref, mult_ref, rows_ref, before):
    part_rows, width = slab_ref.shape
    slots = pk.shape[1]
    chunk = 256
    hist = pk[width : width + 64, :].astype(F32)
    hist = hist[:32] * 32.0 + hist[32:]
    for a in range(8):
        cols = slice(128 * (a % 4), 128 * (a % 4 + 1))
        spread_counts(hist[16 * (a // 4) : 16 * (a // 4 + 1), cols], groups, mult_ref, a)
    misc = pk[width + 64 : width + 80, :].astype(F32)
    right_row = (misc[0:1] * 32.0 + misc[1:2]).astype(jnp.int32)
    factor = misc[2:3] * (0.5 * neg_scale)
    pos_grad = misc[3:4] + misc[4:5]
    query_t = pk[0:width, :]
    half_t = query_t * 0.5
    for n in range(part_rows // chunk):
        at = pl.ds(n * chunk, chunk)
        level = jnp.tanh(dot(slab_ref[at, :], half_t))
        ngrad = (level * factor + factor).astype(BF).astype(F32)
        mult = mult_ref[at, :]
        hit = (iota((chunk, slots), 0) + n * chunk) == right_row
        weight = ngrad * jnp.concatenate([mult] * (slots // 128), 1)
        weight = weight + jnp.where(hit, pos_grad, 0.0)
        high = weight.astype(BF)
        low = (weight - high.astype(F32)).astype(BF)
        rows = dot(high, query_t, NT) + dot(low, query_t, NT)
        rows_ref[at, :] = rows if before is None else before[at, :] + rows


def entity_kernel(neg_scale, groups, slab_ref, ops_hbm, *refs):
    lrow_refs, qg_hbms, pk_hbm, pk_other = refs[:3], refs[3:6], refs[6], refs[7]
    rows_ref, mult_ref, ops_ref, qg_ref, pk_ref, sems = refs[8:]
    copies = [
        pltpu.make_async_copy(pk_hbm, pk_ref, sems.at[0]),
        pltpu.make_async_copy(ops_hbm, ops_ref, sems.at[1]),
    ]
    for s in range(3):
        copies.append(pltpu.make_async_copy(qg_hbms[s], qg_ref.at[s], sems.at[2 + s]))
    for copy in copies:
        copy.start()
    rel_own = ops_hbm.shape[0]
    part_rows = slab_ref.shape[0]
    slots = rel_own * 128
    chunk = 256
    right_rows_added(neg_scale, groups, pk_other, slab_ref, mult_ref, rows_ref, None)
    copies[0].wait()
    right_rows_added(neg_scale, groups, pk_ref, slab_ref, mult_ref, rows_ref, rows_ref)
    for copy in copies[1:]:
        copy.wait()
    grads = []
    for s in range(3):
        qgrad_t = qg_ref[s]
        for i in range(rel_own):
            grads.append(dot(ops_ref[i], qgrad_t[:, 128 * i : 128 * (i + 1)]).astype(BF))
    lgrad_t = jnp.concatenate(grads, 1)
    for n in range(part_rows // chunk):
        hot = [one_hot(ref[0:1, :], n * chunk, (chunk, slots)) for ref in lrow_refs]
        rows_ref[pl.ds(n * chunk, chunk), :] += dot(jnp.concatenate(hot, 1), lgrad_t, NT)


def last_entity_kernel(
    neg_scale, groups, me_ref, slab_ref, pk, before, keep_ref, send_ref, rows_ref, mult_ref
):
    right_rows_added(neg_scale, groups, pk, slab_ref, mult_ref, rows_ref, before)
    me = me_ref[0]
    share = slab_ref.shape[0] // groups
    half = groups // 2
    for n in range(groups):
        to = me ^ (((n >> 1) & 3) * 4 + (n & 1) * 2 + (n >> 3))
        block = rows_ref[pl.ds(pl.multiple_of(to * share, share), share), :]
        if n < half:
            keep_ref[n] = block
        else:
            send_ref[n - half] = block


def finish_kernel(keep_ref, got_ref, parts_ref, ent_ref, rel_ref):
    ent_ref[...] = keep_ref[...] + got_ref[...]
    total = parts_ref[0].astype(F32)
    for n in range(1, parts_ref.shape[0]):
        total = total + parts_ref[n].astype(F32)
    rel_ref[...] = total


def shards(entities, operators, left_rows, right_rows, negatives, counts):
    buckets = left_rows.shape[0]
    slot_count = left_rows.shape[-1]
    neg_count = negatives.shape[-1]
    groups = lax.axis_size("span")
    doms = lax.axis_size("dom")
    rel_own = operators.shape[0]
    relations = rel_own * groups
    part_rows, width = entities.shape
    neg_scale = float(neg_count) ** (-0.5)
    share = part_rows // groups
    slots = rel_own * 128
    limit = pltpu.CompilerParams(vmem_limit_bytes=12 * 1024 * 1024)
    small = pltpu.CompilerParams(vmem_limit_bytes=2 * 1024 * 1024)

    packed = pl.pallas_call(
        functools.partial(pack_kernel, groups),
        out_shape=jax.ShapeDtypeStruct((groups, 16, 128), jnp.int32),
        in_specs=[VMEM] * 4,
        out_specs=VMEM,
        name="pack_lists",
    )(
        negatives.reshape(buckets, neg_count // 128, 128),
        left_rows.reshape(buckets, slot_count // 128, 128),
        right_rows.reshape(buckets, slot_count // 128, 128),
        counts.reshape(buckets, 1, relations),
    )
    received = exchanged(packed, "span")
    near = shifted(entities, -1, -2)
    near = pl.pallas_call(
        tie_kernel,
        out_shape=jax.ShapeDtypeStruct(entities.shape, BF),
        in_specs=[VMEM, VMEM],
        out_specs=VMEM,
        compiler_params=small,
        name="after_lists",
    )(near, received)
    slabs = [near, swapped(near, 1)]

    me = lax.axis_index("span").astype(jnp.int32).reshape(1)
    wide = pltpu.VMEM((part_rows, slots), BF)

    packed_shape = (width + 80, slots)
    grad_shape = (width, slots)
    sums = jax.ShapeDtypeStruct((rel_own, width, width), F32)

    def forward(turn, slab, before, olds):
        last = turn == 2
        outs = [jax.ShapeDtypeStruct((width, part_rows), BF)] if turn == 0 else []
        relation_parts = jax.ShapeDtypeStruct((doms, rel_own * width // doms, width), BF)
        outs.append(relation_parts if last else sums)
        outs.append(jax.ShapeDtypeStruct((8, slots), jnp.int32))
        specs = [VMEM] * len(outs)
        outs.append(pltpu.HBM(grad_shape, BF) if last else jax.ShapeDtypeStruct(grad_shape, BF))
        specs.append(HBM if last else VMEM)
        outs.append(jax.ShapeDtypeStruct(packed_shape, BF))
        specs.append(VMEM)
        outs += [pltpu.HBM(old.shape, BF) for old in olds]
        specs += [HBM] * len(olds)
        scratch = [
            wide,
            wide,
            wide,
            pltpu.VMEM((part_rows, 128), F32),
            pltpu.VMEM(operators.shape, BF),
            pltpu.VMEM((width, part_rows), BF),
            pltpu.SemaphoreType.DMA,
            pltpu.SemaphoreType.DMA((2,)),
        ]
        if last:
            scratch += [
                pltpu.VMEM((rel_own, width, width), F32),
                pltpu.VMEM(grad_shape, BF),
                pltpu.SemaphoreType.DMA,
            ]
        return pl.pallas_call(
            functools.partial(forward_kernel, turn, neg_scale),
            out_shape=outs,
            in_specs=[SMEM, VMEM, VMEM, HBM] + [VMEM] * (len(before) + len(olds)),
            out_specs=specs,
            scratch_shapes=scratch,
            compiler_params=limit,
            cost_estimate=pl.CostEstimate(
                flops=1_450_000_000, bytes_accessed=2_000_000, transcendentals=500_000
            ),
            name=("own_bucket", "near_bucket", "far_bucket")[turn],
        )(me, received, slab, operators, *before, *olds)

    slab_t, rel_sum, lrow_0, qg_0, pack_0 = forward(0, entities, (), ())
    rel_sum, lrow_1, qg_1, pack_1, pack_0, qg_0 = forward(
        1, slabs[0], (slab_t, rel_sum), (pack_0, qg_0)
    )
    pack_1 = shifted(pack_1, 1, 2)
    rel_parts, lrow_2, qg_2, pack_2, qg_1 = forward(2, slabs[1], (slab_t, rel_sum), (qg_1,))
    pack_2 = shifted(pack_2, 2, 1)
    rel_arrived = exchanged(rel_parts, "dom")

    hold = functools.partial(pltpu.with_memory_space_constraint, memory_space=pltpu.HBM)
    rows = pl.pallas_call(
        functools.partial(entity_kernel, neg_scale, groups),
        out_shape=jax.ShapeDtypeStruct((part_rows, width), F32),
        in_specs=[VMEM, HBM] + [VMEM] * 3 + [HBM] * 4 + [VMEM],
        out_specs=VMEM,
        scratch_shapes=[
            pltpu.VMEM((part_rows, 128), F32),
            pltpu.VMEM(operators.shape, BF),
            pltpu.VMEM((3,) + grad_shape, BF),
            pltpu.VMEM(packed_shape, BF),
            pltpu.SemaphoreType.DMA((5,)),
        ],
        compiler_params=limit,
        cost_estimate=pl.CostEstimate(
            flops=3_000_000_000, bytes_accessed=3_000_000, transcendentals=1_000_000
        ),
        name="entity_gradients",
    )(
        entities,
        operators,
        lrow_0,
        lrow_1,
        lrow_2,
        hold(qg_0),
        hold(qg_1),
        hold(qg_2),
        hold(pack_0),
        pack_1,
    )
    half_parts = jax.ShapeDtypeStruct((groups // 2, share, width), F32)
    keep, send = pl.pallas_call(
        functools.partial(last_entity_kernel, neg_scale, groups),
        out_shape=(half_parts, half_parts),
        in_specs=[SMEM] + [VMEM] * 3,
        out_specs=(VMEM, VMEM),
        scratch_shapes=[
            pltpu.VMEM((part_rows, width), F32),
            pltpu.VMEM((part_rows, 128), F32),
        ],
        compiler_params=limit,
        cost_estimate=pl.CostEstimate(
            flops=1_000_000_000, bytes_accessed=2_000_000, transcendentals=500_000
        ),
        name="last_entity_gradients",
    )(me, entities, pack_2, rows)

    total = keep + swapped(send, 1)
    total = total.reshape(4, 2, share, width)
    got = [swapped(total[x].astype(BF), 4 * x) for x in (1, 2, 3)]
    total = total[0] + sum(part.astype(F32) for part in got)
    held = rel_own * width // doms
    entity_share, rel_share = pl.pallas_call(
        finish_kernel,
        out_shape=(
            jax.ShapeDtypeStruct((share, width), F32),
            jax.ShapeDtypeStruct((held, width), F32),
        ),
        in_specs=[VMEM] * 3,
        out_specs=(VMEM, VMEM),
        compiler_params=small,
        name="last_sums",
    )(total[0], swapped(total[1], 2), rel_arrived)
    return (entity_share, rel_share.reshape(rel_own, width // doms, width))


def solution(mesh):
    in_specs = (
        P("dom", None),
        P("span", None, None),
        P(None, "dom", "span", None),
        P(None, "dom", "span", None),
        P(None, "dom", "span", None),
        P(None, "dom", "span", None),
    )
    out_specs = (P(("dom", "span"), None), P("span", "dom", None))
    return jax.shard_map(shards, mesh=mesh, in_specs=in_specs, out_specs=out_specs, check_vma=False)
```

time: 92.5 us -> 89.4 us (0.966)
  waiting for transfers between devices: 14.9 us -> 11.6 us
  starting transfers between devices: 38.4 us -> 39.7 us
    ppermute x3, waiting for transfers between devices: 3.79 us -> 0.01 us  [shifted(): return lax.ppermute(value, ('dom', 'span'), pairs)]
    all_to_all x1, waiting for transfers between devices: 0.01 us -> 1.35 us  [exchanged(): return lax.all_to_all(value, axis, split_axis=0, concat_axis=0, tiled=True)]
    ppermute x6, starting transfers between devices: 16.1 us -> 17.3 us  [swapped(): return lax.ppermute(value, 'span', [(i, i ^ bits) for i in range(groups)])]
    ppermute x6, waiting for transfers between devices: 11.2 us -> 10.2 us  [swapped(): return lax.ppermute(value, 'span', [(i, i ^ bits) for i in range(groups)])]
    pallas_call x3 -> x5, Pallas kernels: 15.8 us -> 15.5 us  [the longest x3 9.73 us: forward(): pl.pallas_call(functools.partial(forward_kernel, turn, neg_scale), out_sh...]
  transfers between devices with their start and end apart: 10 -> 10, of which waited for: 5 -> 5; matrix products, arithmetic and copies ran while one was open for 0% -> 0% of each run, Pallas kernels for 12% -> 19%
where the time goes in v7:
time: 89.4 us; the launch traced here: 88.6 us
  starting transfers between devices  39.7 us (44%)
  blocking collectives  18.4 us (21%)
  Pallas kernels  18 us (20%)
  waiting for transfers between devices  11.6 us (13%)
    all_to_all x1, blocking collectives, exchanged(): return lax.all_to_all(value, axis, split_axis=0, concat_axis=0, tiled=True)  18.4 us
    ppermute x6, starting transfers between devices, swapped(): return lax.ppermute(value, 'span', [(i, i ^ bits) for i in range(groups)])  17.3 us
    all_to_all x1, starting transfers between devices, exchanged(): return lax.all_to_all(value, axis, split_axis=0, concat_axis=0, tiled=True)  15.4 us
    ppermute x6, waiting for transfers between devices, swapped(): return lax.ppermute(value, 'span', [(i, i ^ bits) for i in range(groups)])  10.2 us
    pallas_call x3, Pallas kernels, forward(): pl.pallas_call(functools.partial(forward_kernel, turn, neg_scale), out_sh...  9.73 us
    ppermute x3, starting transfers between devices, shifted(): return lax.ppermute(value, ('dom', 'span'), pairs)  6.99 us
    pallas_call x1, Pallas kernels, shards(): pl.pallas_call(functools.partial(entity_kernel, neg_scale, groups), out_s...  4.22 us
  transfers between devices with their start and end apart: 10, of which 5 were waited for; matrix products, arithmetic and copies ran while one was open for 0% of the time, Pallas kernels for 19%

profile of v7, /device:TPU:24, one launch (start us, length us, event | category | flops | bytes accessed | tf_op | source)
XLA Modules:
  0.0 88.6 jit_solution(7541170473412853372)
XLA Ops:
  0.6 3.1 %collective-permute-start = (bf16[1024,256]{1,0:T(8,128)(2,1)}, bf16[1024,256]{1,0:T(8,128)(2,1)S(1)}, u32[]{:S(2)}, u32[]{:S(2)}) collective-permute-start(bf16[1024,256]{1,0:T(8,128)(2,1)} %slab_ref.3), channel_id=1, source_target_pairs={{0,496},{1,481},{2,498},{3,483},{4,500},{5,485},{6,502},{7,487},{8... | collective-permute-start | bytes 1572872 | tf_op jit(solution)/shard_map/ppermute | solution.py:30
  3.8 1.7 %pack_lists.1 = s32[16,16,128]{2,1,0:T(8,128)} custom-call(s32[3,8,128]{2,1,0:T(8,128)} %bitcast.10, s32[3,4,128]{2,1,0:T(4,128)} %bitcast.11, s32[3,4,128]{2,1,0:T(4,128)} %bitcast.12, s32[3,1,64]{2,1,0:T(1,128)} %bitcast.13), custom_call_target="tpu_custom_call" | custom-call | tf_op jit(solution)/shard_map/pack_lists/pallas_call | solution.py:331
  5.5 18.4 %all_to_all.10.first_ref.refs_1_ = s32[16,16,128]{2,1,0:T(8,128)S(1)} all-to-all(s32[16,16,128]{2,1,0:T(8,128)} %pack_lists.1), channel_id=1, replica_groups=mesh['dom'=32,'span'=16] {'span'}, dimensions={0} | all-to-all | bytes 262144 | tf_op jit(solution)/shard_map/all_to_all | solution.py:39
  23.9 0.0 copy-start
  23.9 0.0 copy-start.1
  23.9 0.0 collective-permute-done.held_ref
  24.0 2.2 %collective-permute-start.1 = (bf16[1024,256]{1,0:T(8,128)(2,1)S(1)}, bf16[1024,256]{1,0:T(8,128)(2,1)S(1)}, u32[]{:S(2)}, u32[]{:S(2)}) collective-permute-start(bf16[1024,256]{1,0:T(8,128)(2,1)S(1)} %after_lists.1.refs_2_), channel_id=1, source_target_pairs={{0,1},{1,0},{2,3},{3,2},{4,5},{5,4},{6,7},{7,6},{8,9},{9,8},{10,11... | collective-permute-start | bytes 1572872 | tf_op jit(solution)/shard_map/ppermute | solution.py:35
  26.2 0.0 copy-done
  26.2 0.0 copy-done.1
  26.2 2.8 %own_bucket.1 = (bf16[256,1024]{1,0:T(8,128)(2,1)S(1)}, f32[4,256,256]{2,1,0:T(8,128)S(1)}, s32[8,512]{1,0:T(8,128)S(1)}, bf16[256,512]{1,0:T(8,128)(2,1)S(1)}, bf16[336,512]{1,0:T(8,128)(2,1)S(1)}) custom-call(s32[1]{0:T(128)} %bitcast.refs_0_.me_ref, s32[16,16,128]{2,1,0:T(8,128)S(1)} %all_to_all.10.first_ref.refs_1_, bf16[1024,256]{1,0:T(8,128)(2,1)S(1)} %copy-done.1, ...), custom_call_target="tpu_custom_call" | custom-call | flops 1450000000 | bytes 2000000 | tf_op jit(solution)/shard_map/own_bucket/pallas_call | solution.py:391
  29.0 2.8 %near_bucket.1 = (f32[4,256,256]{2,1,0:T(8,128)S(1)}, s32[8,512]{1,0:T(8,128)S(1)}, bf16[256,512]{1,0:T(8,128)(2,1)S(1)}, bf16[336,512]{1,0:T(8,128)(2,1)S(1)}, ...) custom-call(s32[1]{0:T(128)} %bitcast.refs_0_.me_ref, s32[16,16,128]{2,1,0:T(8,128)S(1)} %all_to_all.10.first_ref.refs_1_, ...), custom_call_target="tpu_custom_call" | custom-call | flops 1450000000 | bytes 2000000 | tf_op jit(solution)/shard_map/near_bucket/pallas_call | solution.py:391
  31.8 1.9 %collective-permute-start.3 = (bf16[336,512]{1,0:T(8,128)(2,1)S(1)}, bf16[336,512]{1,0:T(8,128)(2,1)S(1)}, u32[]{:S(2)}, u32[]{:S(2)}) collective-permute-start(bf16[336,512]{1,0:T(8,128)(2,1)S(1)} %get-tuple-element.36), channel_id=1, source_target_pairs={{0,16},{1,33},{2,18},{3,35},{4,20},{5,37},{6,22},{7,39},{8,24},{9,... | collective-permute-start | bytes 1032200 | tf_op jit(solution)/shard_map/ppermute | solution.py:30
  33.8 0.0 collective-permute-done.1.refs_2_
  33.8 4.1 %far_bucket.1 = (bf16[32,32,256]{2,1,0:T(8,128)(2,1)}, s32[8,512]{1,0:T(8,128)S(1)}, bf16[256,512]{1,0:T(8,128)(2,1)}, bf16[336,512]{1,0:T(8,128)(2,1)S(1)}, bf16[256,512]{1,0:T(8,128)(2,1)}) custom-call(s32[1]{0:T(128)} %bitcast.refs_0_.me_ref, s32[16,16,128]{2,1,0:T(8,128)S(1)} %all_to_all.10.first_ref.refs_1_, ...), custom_call_target="tpu_custom_call" | custom-call | flops 1450000000 | bytes 2000000 | tf_op jit(solution)/shard_map/far_bucket/pallas_call | solution.py:391
  37.9 1.9 %collective-permute-start.2 = (bf16[336,512]{1,0:T(8,128)(2,1)S(1)}, bf16[336,512]{1,0:T(8,128)(2,1)S(1)}, u32[]{:S(2)}, u32[]{:S(2)}) collective-permute-start(bf16[336,512]{1,0:T(8,128)(2,1)S(1)} %get-tuple-element.28), channel_id=1, source_target_pairs={{0,32},{1,17},{2,34},{3,19},{4,36},{5,21},{6,38},{7,23},{8,40},{9,... | collective-permute-start | bytes 1032200 | tf_op jit(solution)/shard_map/ppermute | solution.py:30
  39.8 15.4 %all-to-all-start.1 = ((bf16[32,32,256]{2,1,0:T(8,128)(2,1)}), bf16[32,32,256]{2,1,0:T(8,128)(2,1)S(1)}, u32[]{:S(2)}, u32[]{:S(2)}) async-start(bf16[32,32,256]{2,1,0:T(8,128)(2,1)} %get-tuple-element.39), calls=%async_computation.1 | async-start | bytes 1048576 | tf_op jit(solution)/shard_map/all_to_all | solution.py:39
  55.2 0.0 collective-permute-done.3.refs_7_
  55.2 4.2 %entity_gradients.1.before = f32[1024,256]{1,0:T(8,128)S(1)} custom-call(bf16[1024,256]{1,0:T(8,128)(2,1)S(1)} %copy-done.1, bf16[4,256,256]{2,1,0:T(8,128)(2,1)S(1)} %copy-done, s32[8,512]{1,0:T(8,128)S(1)} %get-tuple-element.29.refs_0_, s32[8,512]{1,0:T(8,128)S(1)} %get-tuple-element.30.refs_1_, s32[8,512]{1,0:T(8,128)S(1)} %get-tuple-element.31.refs_2_, ...), custom_call_target="tpu_custom_call" | custom-call | flops 3000000000 | bytes 3000000 | tf_op jit(solution)/shard_map/entity_gradients/pallas_call | solution.py:414
  59.5 0.0 collective-permute-done.2.pk
  59.5 1.6 %last_entity_gradients.1 = (f32[8,64,256]{2,1,0:T(8,128)S(1)}, f32[8,64,256]{2,1,0:T(8,128)S(1)}) custom-call(s32[1]{0:T(128)} %bitcast.refs_0_.me_ref, bf16[1024,256]{1,0:T(8,128)(2,1)S(1)} %copy-done.1, bf16[336,512]{1,0:T(8,128)(2,1)S(1)} %collective-permute-done.2.pk, f32[1024,256]{1,0:T(8,128)S(1)} %entity_gradients.1.before), custom_call_target="tpu_custom_call" | custom-call | flops 1000000000 | bytes 2000000 | tf_op jit(solution)/shard_map/last_entity_gradients/pallas_call | solution.py:444
  61.1 1.9 %collective-permute-start.4 = (f32[8,64,256]{2,1,0:T(8,128)S(1)}, f32[8,64,256]{2,1,0:T(8,128)S(1)}, u32[]{:S(2)}, u32[]{:S(2)}) collective-permute-start(f32[8,64,256]{2,1,0:T(8,128)S(1)} %get-tuple-element.38), channel_id=1, source_target_pairs={{0,1},{1,0},{2,3},{3,2},{4,5},{5,4},{6,7},{7,6},{8,9},{9,8},{10,11... | collective-permute-start | bytes 1572872 | tf_op jit(solution)/shard_map/ppermute | solution.py:35
  63.0 1.9 %collective-permute-done.4 = f32[8,64,256]{2,1,0:T(8,128)S(1)} collective-permute-done((f32[8,64,256]{2,1,0:T(8,128)S(1)}, f32[8,64,256]{2,1,0:T(8,128)S(1)}, u32[]{:S(2)}, u32[]{:S(2)}) %collective-permute-start.4) | collective-permute-done | bytes 524320 | tf_op jit(solution)/shard_map/ppermute | solution.py:35
  64.9 0.1 fusion
  65.0 3.4 %collective-permute-start.5 = (bf16[2,64,256]{2,1,0:T(8,128)(2,1)S(1)}, bf16[2,64,256]{2,1,0:T(8,128)(2,1)S(1)}, u32[]{:S(2)}, u32[]{:S(2)}) collective-permute-start(bf16[2,64,256]{2,1,0:T(8,128)(2,1)S(1)} %get-tuple-element.44), channel_id=1, source_target_pairs={{0,4},{1,5},{2,6},{3,7},{4,0},{5,1},{6,2},{7,3},{8,12},{9,13},{10,... | collective-permute-start | bytes 196616 | tf_op jit(solution)/shard_map/ppermute | solution.py:35
  68.4 4.6 %collective-permute-start.6 = (bf16[2,64,256]{2,1,0:T(8,128)(2,1)S(1)}, bf16[2,64,256]{2,1,0:T(8,128)(2,1)S(1)}, u32[]{:S(2)}, u32[]{:S(2)}) collective-permute-start(bf16[2,64,256]{2,1,0:T(8,128)(2,1)S(1)} %get-tuple-element.46), channel_id=1, source_target_pairs={{0,8},{1,9},{2,10},{3,11},{4,12},{5,13},{6,14},{7,15},{8,0},{9,1},... | collective-permute-start | bytes 196616 | tf_op jit(solution)/shard_map/ppermute | solution.py:35
  73.0 2.4 %collective-permute-start.7 = (bf16[2,64,256]{2,1,0:T(8,128)(2,1)S(1)}, bf16[2,64,256]{2,1,0:T(8,128)(2,1)S(1)}, u32[]{:S(2)}, u32[]{:S(2)}) collective-permute-start(bf16[2,64,256]{2,1,0:T(8,128)(2,1)S(1)} %get-tuple-element.45), channel_id=1, source_target_pairs={{0,12},{1,13},{2,14},{3,15},{4,8},{5,9},{6,10},{7,11},{8,4},{9,5},... | collective-permute-start | bytes 196616 | tf_op jit(solution)/shard_map/ppermute | solution.py:35
  75.4 0.0 collective-permute-done.5
  75.4 0.6 collective-permute-done.6
  76.0 4.3 %collective-permute-done.7 = bf16[2,64,256]{2,1,0:T(8,128)(2,1)S(1)} collective-permute-done((bf16[2,64,256]{2,1,0:T(8,128)(2,1)S(1)}, bf16[2,64,256]{2,1,0:T(8,128)(2,1)S(1)}, u32[]{:S(2)}, u32[]{:S(2)}) %collective-permute-start.7) | collective-permute-done | bytes 65568 | tf_op jit(solution)/shard_map/ppermute | solution.py:35
  80.4 2.8 %collective-permute-start.8 = (f32[64,256]{1,0:T(8,128)S(1)}, f32[64,256]{1,0:T(8,128)S(1)}, u32[]{:S(2)}, u32[]{:S(2)}) collective-permute-start(f32[64,256]{1,0:T(8,128)S(1)} %get-tuple-element.47), channel_id=1, source_target_pairs={{0,2},{1,3},{2,0},{3,1},{4,6},{5,7},{6,4},{7,5},{8,10},{9,11},{10,... | collective-permute-start | bytes 196616 | tf_op jit(solution)/shard_map/ppermute | solution.py:35
  83.2 3.4 %collective-permute-done.8.got_ref = f32[64,256]{1,0:T(8,128)S(1)} collective-permute-done((f32[64,256]{1,0:T(8,128)S(1)}, f32[64,256]{1,0:T(8,128)S(1)}, u32[]{:S(2)}, u32[]{:S(2)}) %collective-permute-start.8) | collective-permute-done | bytes 65568 | tf_op jit(solution)/shard_map/ppermute | solution.py:35
  86.6 1.3 %all-to-all-done.1.parts_ref = bf16[32,32,256]{2,1,0:T(8,128)(2,1)S(1)} async-done(((bf16[32,32,256]{2,1,0:T(8,128)(2,1)}), bf16[32,32,256]{2,1,0:T(8,128)(2,1)S(1)}, u32[]{:S(2)}, u32[]{:S(2)}) %all-to-all-start.1) | async-done | bytes 524320 | tf_op jit(solution)/shard_map/all_to_all | solution.py:39
  87.9 0.7 last_sums.1
  (4 shorter events, 0.1 us)
Async XLA Ops:
  0.6 23.3 %collective-permute-start = (bf16[1024,256]{1,0:T(8,128)(2,1)}, bf16[1024,256]{1,0:T(8,128)(2,1)S(1)}, u32[]{:S(2)}, u32[]{:S(2)}) collective-permute-start(bf16[1024,256]{1,0:T(8,128)(2,1)} %slab_ref.3), channel_id=1, source_target_pairs={{0,496},{1,481},{2,498},{3,483},{4,500},{5,485},{6,502},{7,487},{8... | collective-permute-start | bytes 1572872 | tf_op jit(solution)/shard_map/ppermute | solution.py:30
  23.9 2.3 %copy-start = (bf16[4,256,256]{2,1,0:T(8,128)(2,1)S(1)}, bf16[4,256,256]{2,1,0:T(8,128)(2,1)}, u32[]{:S(2)}) copy-start(bf16[4,256,256]{2,1,0:T(8,128)(2,1)} %ops_hbm.1) | copy-start | bytes 1572868
  23.9 2.3 %copy-start.1 = (bf16[1024,256]{1,0:T(8,128)(2,1)S(1)}, bf16[1024,256]{1,0:T(8,128)(2,1)}, u32[]{:S(2)}) copy-start(bf16[1024,256]{1,0:T(8,128)(2,1)} %slab_ref.3) | copy-start | bytes 1572868
  24.0 9.8 %collective-permute-start.1 = (bf16[1024,256]{1,0:T(8,128)(2,1)S(1)}, bf16[1024,256]{1,0:T(8,128)(2,1)S(1)}, u32[]{:S(2)}, u32[]{:S(2)}) collective-permute-start(bf16[1024,256]{1,0:T(8,128)(2,1)S(1)} %after_lists.1.refs_2_), channel_id=1, source_target_pairs={{0,1},{1,0},{2,3},{3,2},{4,5},{5,4},{6,7},{7,6},{8,9},{9,8},{10,11... | collective-permute-start | bytes 1572872 | tf_op jit(solution)/shard_map/ppermute | solution.py:35
  31.8 23.4 %collective-permute-start.3 = (bf16[336,512]{1,0:T(8,128)(2,1)S(1)}, bf16[336,512]{1,0:T(8,128)(2,1)S(1)}, u32[]{:S(2)}, u32[]{:S(2)}) collective-permute-start(bf16[336,512]{1,0:T(8,128)(2,1)S(1)} %get-tuple-element.36), channel_id=1, source_target_pairs={{0,16},{1,33},{2,18},{3,35},{4,20},{5,37},{6,22},{7,39},{8,24},{9,... | collective-permute-start | bytes 1032200 | tf_op jit(solution)/shard_map/ppermute | solution.py:30
  37.9 21.6 %collective-permute-start.2 = (bf16[336,512]{1,0:T(8,128)(2,1)S(1)}, bf16[336,512]{1,0:T(8,128)(2,1)S(1)}, u32[]{:S(2)}, u32[]{:S(2)}) collective-permute-start(bf16[336,512]{1,0:T(8,128)(2,1)S(1)} %get-tuple-element.28), channel_id=1, source_target_pairs={{0,32},{1,17},{2,34},{3,19},{4,36},{5,21},{6,38},{7,23},{8,40},{9,... | collective-permute-start | bytes 1032200 | tf_op jit(solution)/shard_map/ppermute | solution.py:30
  39.8 48.1 %all-to-all-start.1 = ((bf16[32,32,256]{2,1,0:T(8,128)(2,1)}), bf16[32,32,256]{2,1,0:T(8,128)(2,1)S(1)}, u32[]{:S(2)}, u32[]{:S(2)}) async-start(bf16[32,32,256]{2,1,0:T(8,128)(2,1)} %get-tuple-element.39), calls=%async_computation.1 | async-start | bytes 1048576 | tf_op jit(solution)/shard_map/all_to_all | solution.py:39
  61.1 3.8 %collective-permute-start.4 = (f32[8,64,256]{2,1,0:T(8,128)S(1)}, f32[8,64,256]{2,1,0:T(8,128)S(1)}, u32[]{:S(2)}, u32[]{:S(2)}) collective-permute-start(f32[8,64,256]{2,1,0:T(8,128)S(1)} %get-tuple-element.38), channel_id=1, source_target_pairs={{0,1},{1,0},{2,3},{3,2},{4,5},{5,4},{6,7},{7,6},{8,9},{9,8},{10,11... | collective-permute-start | bytes 1572872 | tf_op jit(solution)/shard_map/ppermute | solution.py:35
  65.0 10.4 %collective-permute-start.5 = (bf16[2,64,256]{2,1,0:T(8,128)(2,1)S(1)}, bf16[2,64,256]{2,1,0:T(8,128)(2,1)S(1)}, u32[]{:S(2)}, u32[]{:S(2)}) collective-permute-start(bf16[2,64,256]{2,1,0:T(8,128)(2,1)S(1)} %get-tuple-element.44), channel_id=1, source_target_pairs={{0,4},{1,5},{2,6},{3,7},{4,0},{5,1},{6,2},{7,3},{8,12},{9,13},{10,... | collective-permute-start | bytes 196616 | tf_op jit(solution)/shard_map/ppermute | solution.py:35
  68.4 7.7 %collective-permute-start.6 = (bf16[2,64,256]{2,1,0:T(8,128)(2,1)S(1)}, bf16[2,64,256]{2,1,0:T(8,128)(2,1)S(1)}, u32[]{:S(2)}, u32[]{:S(2)}) collective-permute-start(bf16[2,64,256]{2,1,0:T(8,128)(2,1)S(1)} %get-tuple-element.46), channel_id=1, source_target_pairs={{0,8},{1,9},{2,10},{3,11},{4,12},{5,13},{6,14},{7,15},{8,0},{9,1},... | collective-permute-start | bytes 196616 | tf_op jit(solution)/shard_map/ppermute | solution.py:35
  73.0 7.4 %collective-permute-start.7 = (bf16[2,64,256]{2,1,0:T(8,128)(2,1)S(1)}, bf16[2,64,256]{2,1,0:T(8,128)(2,1)S(1)}, u32[]{:S(2)}, u32[]{:S(2)}) collective-permute-start(bf16[2,64,256]{2,1,0:T(8,128)(2,1)S(1)} %get-tuple-element.45), channel_id=1, source_target_pairs={{0,12},{1,13},{2,14},{3,15},{4,8},{5,9},{6,10},{7,11},{8,4},{9,5},... | collective-permute-start | bytes 196616 | tf_op jit(solution)/shard_map/ppermute | solution.py:35
  80.4 6.2 %collective-permute-start.8 = (f32[64,256]{1,0:T(8,128)S(1)}, f32[64,256]{1,0:T(8,128)S(1)}, u32[]{:S(2)}, u32[]{:S(2)}) collective-permute-start(f32[64,256]{1,0:T(8,128)S(1)} %get-tuple-element.47), channel_id=1, source_target_pairs={{0,2},{1,3},{2,0},{3,1},{4,6},{5,7},{6,4},{7,5},{8,10},{9,11},{10,... | collective-permute-start | bytes 196616 | tf_op jit(solution)/shard_map/ppermute | solution.py:35

commit v8 on v7

--- a/solution.py
+++ b/solution.py
@@ -99,7 +99,8 @@
         et0_ref, rel_acc = refs[:2]
         refs = refs[2:]
     elif last:
-        rel_ref, refs = refs[0], refs[1:]
+        stay_ref, leave_ref = refs[:2]
+        refs = refs[2:]
     else:
         rel_acc, refs = refs[0], refs[1:]
     lrow_ref, qg_ref, pk = refs[:3]
@@ -221,11 +222,14 @@
         copy.wait()
     if not last:
         return
-    doms, held, _ = rel_ref.shape
+    halves, held, _ = stay_ref.shape
     held = held // rel_own
-    for d in range(doms):
-        block = [rel_acc[i, held * d : held * (d + 1), :] for i in range(rel_own)]
-        rel_ref[d] = jnp.concatenate(block, 0).astype(BF)
+    parity = me_ref[1]
+    for ref, owner in ((leave_ref, 1 - parity), (stay_ref, parity)):
+        for n in range(halves):
+            start = held * (4 * (n >> 1) + 2 * owner + (n & 1))
+            rows = pl.ds(pl.multiple_of(start, held), held)
+            ref[n] = jnp.concatenate([rel_acc[i, rows, :] for i in range(rel_own)], 0)
     qg_copy.wait()
 
 
@@ -352,7 +356,7 @@
     )(near, received)
     slabs = [near, swapped(near, 1)]
 
-    me = lax.axis_index("span").astype(jnp.int32).reshape(1)
+    me = jnp.stack([lax.axis_index("span"), (lax.axis_index("dom") >> 1) & 1]).astype(jnp.int32)
     wide = pltpu.VMEM((part_rows, slots), BF)
 
     packed_shape = (width + 80, slots)
@@ -362,8 +366,8 @@
     def forward(turn, slab, before, olds):
         last = turn == 2
         outs = [jax.ShapeDtypeStruct((width, part_rows), BF)] if turn == 0 else []
-        relation_parts = jax.ShapeDtypeStruct((doms, rel_own * width // doms, width), BF)
-        outs.append(relation_parts if last else sums)
+        half_sums = jax.ShapeDtypeStruct((doms // 2, rel_own * width // doms, width), F32)
+        outs += [half_sums, half_sums] if last else [sums]
         outs.append(jax.ShapeDtypeStruct((8, slots), jnp.int32))
         specs = [VMEM] * len(outs)
         outs.append(pltpu.HBM(grad_shape, BF) if last else jax.ShapeDtypeStruct(grad_shape, BF))
@@ -406,9 +410,14 @@
         1, slabs[0], (slab_t, rel_sum), (pack_0, qg_0)
     )
     pack_1 = shifted(pack_1, 1, 2)
-    rel_parts, lrow_2, qg_2, pack_2, qg_1 = forward(2, slabs[1], (slab_t, rel_sum), (qg_1,))
+    stay, leave, lrow_2, qg_2, pack_2, qg_1 = forward(2, slabs[1], (slab_t, rel_sum), (qg_1,))
     pack_2 = shifted(pack_2, 2, 1)
-    rel_arrived = exchanged(rel_parts, "dom")
+    near_pairs = [(d, d ^ 2) for d in range(doms)]
+    rel_parts = (stay + lax.ppermute(leave, "dom", near_pairs)).astype(BF)
+    alike = [[d for d in range(doms) if (d >> 1) & 1 == parity] for parity in (0, 1)]
+    rel_arrived = lax.all_to_all(
+        rel_parts, "dom", split_axis=0, concat_axis=0, axis_index_groups=alike, tiled=True
+    )
 
     hold = functools.partial(pltpu.with_memory_space_constraint, memory_space=pltpu.HBM)
     rows = pl.pallas_call(

time: 89.4 us -> 99.2 us (1.11)
  blocking collectives: 18.4 us -> 0 us
  waiting for transfers between devices: 11.6 us -> 24.4 us
  starting transfers between devices: 39.7 us -> 52.4 us
  Pallas kernels: 18 us -> 19.4 us
    all_to_all x1 -> x0, blocking collectives: 18.4 us -> none  [exchanged(): return lax.all_to_all(value, axis, split_axis=0, concat_axis=0, tiled=True)]
    all_to_all x0 -> x1, starting transfers between devices: none -> 13.2 us  [shards(): lax.all_to_all(rel_parts, 'dom', split_axis=0, concat_axis=0, axis_index_...]
    ppermute x3, waiting for transfers between devices: 0.01 us -> 7.93 us  [shifted(): return lax.ppermute(value, ('dom', 'span'), pairs)]
    all_to_all x1, waiting for transfers between devices: 1.35 us -> 5.2 us  [exchanged(): return lax.all_to_all(value, axis, split_axis=0, concat_axis=0, tiled=True)]
    ppermute x0 -> x1, starting transfers between devices: none -> 2.69 us  [shards(): rel_parts = (stay + lax.ppermute(leave, 'dom', near_pairs)).astype(BF)]
    all_to_all x1, starting transfers between devices: 15.4 us -> 13.2 us  [exchanged(): return lax.all_to_all(value, axis, split_axis=0, concat_axis=0, tiled=True)]
    ppermute x0 -> x1, waiting for transfers between devices: none -> 1.94 us  [shards(): rel_parts = (stay + lax.ppermute(leave, 'dom', near_pairs)).astype(BF)]
  transfers between devices with their start and end apart: 10 -> 12, of which waited for: 5 -> 7; matrix products, arithmetic and copies ran while one was open for 0% -> 1% of each run, Pallas kernels for 19% -> 19%
where the time goes in v8:
time: 99.2 us; the launch traced here: 98 us
  starting transfers between devices  52.4 us (53%)
  waiting for transfers between devices  24.4 us (25%)
  Pallas kernels  19.4 us (20%)
    ppermute x6, starting transfers between devices, swapped(): return lax.ppermute(value, 'span', [(i, i ^ bits) for i in range(groups)])  16.4 us
    all_to_all x1, starting transfers between devices, exchanged(): return lax.all_to_all(value, axis, split_axis=0, concat_axis=0, tiled=True)  13.2 us
    all_to_all x1, starting transfers between devices, shards(): lax.all_to_all(rel_parts, 'dom', split_axis=0, concat_axis=0, axis_index_...  13.2 us
    pallas_call x3, Pallas kernels, forward(): pl.pallas_call(functools.partial(forward_kernel, turn, neg_scale), out_sh...  10.6 us
    ppermute x6, waiting for transfers between devices, swapped(): return lax.ppermute(value, 'span', [(i, i ^ bits) for i in range(groups)])  9.31 us
    ppermute x3, waiting for transfers between devices, shifted(): return lax.ppermute(value, ('dom', 'span'), pairs)  7.93 us
    ppermute x3, starting transfers between devices, shifted(): return lax.ppermute(value, ('dom', 'span'), pairs)  6.99 us
    all_to_all x1, waiting for transfers between devices, exchanged(): return lax.all_to_all(value, axis, split_axis=0, concat_axis=0, tiled=True)  5.2 us
  transfers between devices with their start and end apart: 12, of which 7 were waited for; matrix products, arithmetic and copies ran while one was open for 1% of the time, Pallas kernels for 19%

profile of v8, /device:TPU:24, one launch (start us, length us, event | category | flops | bytes accessed | tf_op | source)
XLA Modules:
  0.0 98.0 jit_solution(12094392422442813968)
XLA Ops:
  0.6 3.1 %collective-permute-start = (bf16[1024,256]{1,0:T(8,128)(2,1)}, bf16[1024,256]{1,0:T(8,128)(2,1)S(1)}, u32[]{:S(2)}, u32[]{:S(2)}) collective-permute-start(bf16[1024,256]{1,0:T(8,128)(2,1)} %slab_ref.3), channel_id=1, source_target_pairs={{0,496},{1,481},{2,498},{3,483},{4,500},{5,485},{6,502},{7,487},{8... | collective-permute-start | bytes 1572872 | tf_op jit(solution)/shard_map/ppermute | solution.py:30
  3.8 1.7 %pack_lists.1 = s32[16,16,128]{2,1,0:T(8,128)} custom-call(s32[3,8,128]{2,1,0:T(8,128)} %bitcast.11, s32[3,4,128]{2,1,0:T(4,128)} %bitcast.12, s32[3,4,128]{2,1,0:T(4,128)} %bitcast.13, s32[3,1,64]{2,1,0:T(1,128)} %bitcast.14), custom_call_target="tpu_custom_call" | custom-call | tf_op jit(solution)/shard_map/pack_lists/pallas_call | solution.py:335
  5.5 13.2 %all-to-all-start = ((s32[16,16,128]{2,1,0:T(8,128)}), s32[16,16,128]{2,1,0:T(8,128)S(1)}, u32[]{:S(2)}, u32[]{:S(2)}) async-start(s32[16,16,128]{2,1,0:T(8,128)} %pack_lists.1), calls=%async_computation | async-start | bytes 262144 | tf_op jit(solution)/shard_map/all_to_all | solution.py:39
  18.7 0.0 copy-start
  18.7 0.0 copy-start.1
  18.7 5.2 %all-to-all-done.first_ref.refs_1_ = s32[16,16,128]{2,1,0:T(8,128)S(1)} async-done(((s32[16,16,128]{2,1,0:T(8,128)}), s32[16,16,128]{2,1,0:T(8,128)S(1)}, u32[]{:S(2)}, u32[]{:S(2)}) %all-to-all-start) | async-done | bytes 131104 | tf_op jit(solution)/shard_map/all_to_all | solution.py:39
  23.9 0.0 collective-permute-done.held_ref
  24.0 2.1 %collective-permute-start.1 = (bf16[1024,256]{1,0:T(8,128)(2,1)S(1)}, bf16[1024,256]{1,0:T(8,128)(2,1)S(1)}, u32[]{:S(2)}, u32[]{:S(2)}) collective-permute-start(bf16[1024,256]{1,0:T(8,128)(2,1)S(1)} %after_lists.1.refs_2_), channel_id=1, source_target_pairs={{0,1},{1,0},{2,3},{3,2},{4,5},{5,4},{6,7},{7,6},{8,9},{9,8},{10,11... | collective-permute-start | bytes 1572872 | tf_op jit(solution)/shard_map/ppermute | solution.py:35
  26.0 0.1 pad_add_fusion.refs_0_.me_ref
  26.1 0.0 copy-done
  26.1 0.0 copy-done.1
  26.1 3.4 %own_bucket.1 = (bf16[256,1024]{1,0:T(8,128)(2,1)S(1)}, f32[4,256,256]{2,1,0:T(8,128)S(1)}, s32[8,512]{1,0:T(8,128)S(1)}, bf16[256,512]{1,0:T(8,128)(2,1)S(1)}, bf16[336,512]{1,0:T(8,128)(2,1)S(1)}) custom-call(s32[2]{0:T(128)S(1)} %pad_add_fusion.refs_0_.me_ref, s32[16,16,128]{2,1,0:T(8,128)S(1)} %all-to-all-done.first_ref.refs_1_, ...), custom_call_target="tpu_custom_call" | custom-call | flops 1450000000 | bytes 2000000 | tf_op jit(solution)/shard_map/own_bucket/pallas_call | solution.py:395
  29.5 3.4 %near_bucket.1 = (f32[4,256,256]{2,1,0:T(8,128)S(1)}, s32[8,512]{1,0:T(8,128)S(1)}, bf16[256,512]{1,0:T(8,128)(2,1)S(1)}, bf16[336,512]{1,0:T(8,128)(2,1)S(1)}, ...) custom-call(s32[2]{0:T(128)S(1)} %pad_add_fusion.refs_0_.me_ref, s32[16,16,128]{2,1,0:T(8,128)S(1)} %all-to-all-done.first_ref.refs_1_, ...), custom_call_target="tpu_custom_call" | custom-call | flops 1450000000 | bytes 2000000 | tf_op jit(solution)/shard_map/near_bucket/pallas_call | solution.py:395
  32.9 1.9 %collective-permute-start.3 = (bf16[336,512]{1,0:T(8,128)(2,1)S(1)}, bf16[336,512]{1,0:T(8,128)(2,1)S(1)}, u32[]{:S(2)}, u32[]{:S(2)}) collective-permute-start(bf16[336,512]{1,0:T(8,128)(2,1)S(1)} %get-tuple-element.37), channel_id=1, source_target_pairs={{0,16},{1,33},{2,18},{3,35},{4,20},{5,37},{6,22},{7,39},{8,24},{9,... | collective-permute-start | bytes 1032200 | tf_op jit(solution)/shard_map/ppermute | solution.py:30
  34.8 0.0 collective-permute-done.1.refs_2_
  34.8 3.9 %far_bucket.1 = (f32[16,32,256]{2,1,0:T(8,128)S(1)}, f32[16,32,256]{2,1,0:T(8,128)S(1)}, s32[8,512]{1,0:T(8,128)S(1)}, bf16[256,512]{1,0:T(8,128)(2,1)}, bf16[33...) custom-call(s32[2]{0:T(128)S(1)} %pad_add_fusion.refs_0_.me_ref, s32[16,16,128]{2,1,0:T(8,128)S(1)} %all-to-all-done.first_ref.refs_1_, ...), custom_call_target="tpu_custom_call" | custom-call | flops 1450000000 | bytes 2000000 | tf_op jit(solution)/shard_map/far_bucket/pallas_call | solution.py:395
  38.7 1.9 %collective-permute-start.2 = (bf16[336,512]{1,0:T(8,128)(2,1)S(1)}, bf16[336,512]{1,0:T(8,128)(2,1)S(1)}, u32[]{:S(2)}, u32[]{:S(2)}) collective-permute-start(bf16[336,512]{1,0:T(8,128)(2,1)S(1)} %get-tuple-element.29), channel_id=1, source_target_pairs={{0,32},{1,17},{2,34},{3,19},{4,36},{5,21},{6,38},{7,23},{8,40},{9,... | collective-permute-start | bytes 1032200 | tf_op jit(solution)/shard_map/ppermute | solution.py:30
  40.6 2.7 %collective-permute-start.9 = (f32[16,32,256]{2,1,0:T(8,128)S(1)}, f32[16,32,256]{2,1,0:T(8,128)S(1)}, u32[]{:S(2)}, u32[]{:S(2)}) collective-permute-start(f32[16,32,256]{2,1,0:T(8,128)S(1)} %get-tuple-element.41), channel_id=1, source_target_pairs={{0,32},{16,48},{32,0},{48,16},{64,96},{80,112},{96,64},{112,80},{1... | collective-permute-start | bytes 1572872 | tf_op jit(solution)/shard_map/ppermute | solution.py:416
  43.3 0.5 collective-permute-done.3.refs_7_
  43.8 4.2 %entity_gradients.1.before = f32[1024,256]{1,0:T(8,128)S(1)} custom-call(bf16[1024,256]{1,0:T(8,128)(2,1)S(1)} %copy-done.1, bf16[4,256,256]{2,1,0:T(8,128)(2,1)S(1)} %copy-done, s32[8,512]{1,0:T(8,128)S(1)} %get-tuple-element.30.refs_0_, s32[8,512]{1,0:T(8,128)S(1)} %get-tuple-element.31.refs_1_, s32[8,512]{1,0:T(8,128)S(1)} %get-tuple-element.32.refs_2_, ...), custom_call_target="tpu_custom_call" | custom-call | flops 3000000000 | bytes 3000000 | tf_op jit(solution)/shard_map/entity_gradients/pallas_call | solution.py:423
  48.0 7.5 %collective-permute-done.2.pk = bf16[336,512]{1,0:T(8,128)(2,1)S(1)} collective-permute-done((bf16[336,512]{1,0:T(8,128)(2,1)S(1)}, bf16[336,512]{1,0:T(8,128)(2,1)S(1)}, u32[]{:S(2)}, u32[]{:S(2)}) %collective-permute-start.2) | collective-permute-done | bytes 344096 | tf_op jit(solution)/shard_map/ppermute | solution.py:30
  55.5 2.1 %last_entity_gradients.1 = (f32[8,64,256]{2,1,0:T(8,128)S(1)}, f32[8,64,256]{2,1,0:T(8,128)S(1)}) custom-call(s32[2]{0:T(128)S(1)} %pad_add_fusion.refs_0_.me_ref, bf16[1024,256]{1,0:T(8,128)(2,1)S(1)} %copy-done.1, bf16[336,512]{1,0:T(8,128)(2,1)S(1)} %collective-permute-done.2.pk, f32[1024,256]{1,0:T(8,128)S(1)} %entity_gradients.1.before), custom_call_target="tpu_custom_call" | custom-call | flops 1000000000 | bytes 2000000 | tf_op jit(solution)/shard_map/last_entity_gradients/pallas_call | solution.py:453
  57.6 1.9 %collective-permute-start.4 = (f32[8,64,256]{2,1,0:T(8,128)S(1)}, f32[8,64,256]{2,1,0:T(8,128)S(1)}, u32[]{:S(2)}, u32[]{:S(2)}) collective-permute-start(f32[8,64,256]{2,1,0:T(8,128)S(1)} %get-tuple-element.39), channel_id=1, source_target_pairs={{0,1},{1,0},{2,3},{3,2},{4,5},{5,4},{6,7},{7,6},{8,9},{9,8},{10,11... | collective-permute-start | bytes 1572872 | tf_op jit(solution)/shard_map/ppermute | solution.py:35
  59.6 1.9 %collective-permute-done.9 = f32[16,32,256]{2,1,0:T(8,128)S(1)} collective-permute-done((f32[16,32,256]{2,1,0:T(8,128)S(1)}, f32[16,32,256]{2,1,0:T(8,128)S(1)}, u32[]{:S(2)}, u32[]{:S(2)}) %collective-permute-start.9) | collective-permute-done | bytes 524320 | tf_op jit(solution)/shard_map/ppermute | solution.py:416
  61.5 0.8 add_convert_fusion
  62.3 13.2 %all-to-all-start.1 = ((bf16[16,32,256]{2,1,0:T(8,128)(2,1)}), bf16[16,32,256]{2,1,0:T(8,128)(2,1)S(1)}, u32[]{:S(2)}, u32[]{:S(2)}) async-start(bf16[16,32,256]{2,1,0:T(8,128)(2,1)} %add_convert_fusion), calls=%async_computation.1 | async-start | bytes 524288 | tf_op jit(solution)/shard_map/all_to_all | solution.py:418
  75.4 0.0 collective-permute-done.4
  75.4 0.1 fusion
  75.6 3.6 %collective-permute-start.5 = (bf16[2,64,256]{2,1,0:T(8,128)(2,1)S(1)}, bf16[2,64,256]{2,1,0:T(8,128)(2,1)S(1)}, u32[]{:S(2)}, u32[]{:S(2)}) collective-permute-start(bf16[2,64,256]{2,1,0:T(8,128)(2,1)S(1)} %get-tuple-element.46), channel_id=1, source_target_pairs={{0,4},{1,5},{2,6},{3,7},{4,0},{5,1},{6,2},{7,3},{8,12},{9,13},{10,... | collective-permute-start | bytes 196616 | tf_op jit(solution)/shard_map/ppermute | solution.py:35
  79.2 4.5 %collective-permute-start.6 = (bf16[2,64,256]{2,1,0:T(8,128)(2,1)S(1)}, bf16[2,64,256]{2,1,0:T(8,128)(2,1)S(1)}, u32[]{:S(2)}, u32[]{:S(2)}) collective-permute-start(bf16[2,64,256]{2,1,0:T(8,128)(2,1)S(1)} %get-tuple-element.48), channel_id=1, source_target_pairs={{0,8},{1,9},{2,10},{3,11},{4,12},{5,13},{6,14},{7,15},{8,0},{9,1},... | collective-permute-start | bytes 196616 | tf_op jit(solution)/shard_map/ppermute | solution.py:35
  83.8 2.3 %collective-permute-start.7 = (bf16[2,64,256]{2,1,0:T(8,128)(2,1)S(1)}, bf16[2,64,256]{2,1,0:T(8,128)(2,1)S(1)}, u32[]{:S(2)}, u32[]{:S(2)}) collective-permute-start(bf16[2,64,256]{2,1,0:T(8,128)(2,1)S(1)} %get-tuple-element.47), channel_id=1, source_target_pairs={{0,12},{1,13},{2,14},{3,15},{4,8},{5,9},{6,10},{7,11},{8,4},{9,5},... | collective-permute-start | bytes 196616 | tf_op jit(solution)/shard_map/ppermute | solution.py:35
  86.0 0.0 collective-permute-done.5
  86.0 0.8 collective-permute-done.6
  86.9 4.2 %collective-permute-done.7 = bf16[2,64,256]{2,1,0:T(8,128)(2,1)S(1)} collective-permute-done((bf16[2,64,256]{2,1,0:T(8,128)(2,1)S(1)}, bf16[2,64,256]{2,1,0:T(8,128)(2,1)S(1)}, u32[]{:S(2)}, u32[]{:S(2)}) %collective-permute-start.7) | collective-permute-done | bytes 65568 | tf_op jit(solution)/shard_map/ppermute | solution.py:35
  91.2 1.9 %collective-permute-start.8 = (f32[64,256]{1,0:T(8,128)S(1)}, f32[64,256]{1,0:T(8,128)S(1)}, u32[]{:S(2)}, u32[]{:S(2)}) collective-permute-start(f32[64,256]{1,0:T(8,128)S(1)} %get-tuple-element.49), channel_id=1, source_target_pairs={{0,2},{1,3},{2,0},{3,1},{4,6},{5,7},{6,4},{7,5},{8,10},{9,11},{10,... | collective-permute-start | bytes 196616 | tf_op jit(solution)/shard_map/ppermute | solution.py:35
  93.1 4.2 %collective-permute-done.8.got_ref = f32[64,256]{1,0:T(8,128)S(1)} collective-permute-done((f32[64,256]{1,0:T(8,128)S(1)}, f32[64,256]{1,0:T(8,128)S(1)}, u32[]{:S(2)}, u32[]{:S(2)}) %collective-permute-start.8) | collective-permute-done | bytes 65568 | tf_op jit(solution)/shard_map/ppermute | solution.py:35
  97.3 0.0 all-to-all-done.1.parts_ref
  97.3 0.7 last_sums.1
  (4 shorter events, 0.1 us)
Async XLA Ops:
  0.6 23.3 %collective-permute-start = (bf16[1024,256]{1,0:T(8,128)(2,1)}, bf16[1024,256]{1,0:T(8,128)(2,1)S(1)}, u32[]{:S(2)}, u32[]{:S(2)}) collective-permute-start(bf16[1024,256]{1,0:T(8,128)(2,1)} %slab_ref.3), channel_id=1, source_target_pairs={{0,496},{1,481},{2,498},{3,483},{4,500},{5,485},{6,502},{7,487},{8... | collective-permute-start | bytes 1572872 | tf_op jit(solution)/shard_map/ppermute | solution.py:30
  5.5 18.4 %all-to-all-start = ((s32[16,16,128]{2,1,0:T(8,128)}), s32[16,16,128]{2,1,0:T(8,128)S(1)}, u32[]{:S(2)}, u32[]{:S(2)}) async-start(s32[16,16,128]{2,1,0:T(8,128)} %pack_lists.1), calls=%async_computation | async-start | bytes 262144 | tf_op jit(solution)/shard_map/all_to_all | solution.py:39
  18.7 7.4 %copy-start = (bf16[4,256,256]{2,1,0:T(8,128)(2,1)S(1)}, bf16[4,256,256]{2,1,0:T(8,128)(2,1)}, u32[]{:S(2)}) copy-start(bf16[4,256,256]{2,1,0:T(8,128)(2,1)} %ops_hbm.1) | copy-start | bytes 1572868
  18.7 7.4 %copy-start.1 = (bf16[1024,256]{1,0:T(8,128)(2,1)S(1)}, bf16[1024,256]{1,0:T(8,128)(2,1)}, u32[]{:S(2)}) copy-start(bf16[1024,256]{1,0:T(8,128)(2,1)} %slab_ref.3) | copy-start | bytes 1572868
  24.0 10.9 %collective-permute-start.1 = (bf16[1024,256]{1,0:T(8,128)(2,1)S(1)}, bf16[1024,256]{1,0:T(8,128)(2,1)S(1)}, u32[]{:S(2)}, u32[]{:S(2)}) collective-permute-start(bf16[1024,256]{1,0:T(8,128)(2,1)S(1)} %after_lists.1.refs_2_), channel_id=1, source_target_pairs={{0,1},{1,0},{2,3},{3,2},{4,5},{5,4},{6,7},{7,6},{8,9},{9,8},{10,11... | collective-permute-start | bytes 1572872 | tf_op jit(solution)/shard_map/ppermute | solution.py:35
  32.9 10.9 %collective-permute-start.3 = (bf16[336,512]{1,0:T(8,128)(2,1)S(1)}, bf16[336,512]{1,0:T(8,128)(2,1)S(1)}, u32[]{:S(2)}, u32[]{:S(2)}) collective-permute-start(bf16[336,512]{1,0:T(8,128)(2,1)S(1)} %get-tuple-element.37), channel_id=1, source_target_pairs={{0,16},{1,33},{2,18},{3,35},{4,20},{5,37},{6,22},{7,39},{8,24},{9,... | collective-permute-start | bytes 1032200 | tf_op jit(solution)/shard_map/ppermute | solution.py:30
  38.7 16.8 %collective-permute-start.2 = (bf16[336,512]{1,0:T(8,128)(2,1)S(1)}, bf16[336,512]{1,0:T(8,128)(2,1)S(1)}, u32[]{:S(2)}, u32[]{:S(2)}) collective-permute-start(bf16[336,512]{1,0:T(8,128)(2,1)S(1)} %get-tuple-element.29), channel_id=1, source_target_pairs={{0,32},{1,17},{2,34},{3,19},{4,36},{5,21},{6,38},{7,23},{8,40},{9,... | collective-permute-start | bytes 1032200 | tf_op jit(solution)/shard_map/ppermute | solution.py:30
  40.6 20.9 %collective-permute-start.9 = (f32[16,32,256]{2,1,0:T(8,128)S(1)}, f32[16,32,256]{2,1,0:T(8,128)S(1)}, u32[]{:S(2)}, u32[]{:S(2)}) collective-permute-start(f32[16,32,256]{2,1,0:T(8,128)S(1)} %get-tuple-element.41), channel_id=1, source_target_pairs={{0,32},{16,48},{32,0},{48,16},{64,96},{80,112},{96,64},{112,80},{1... | collective-permute-start | bytes 1572872 | tf_op jit(solution)/shard_map/ppermute | solution.py:416
  57.6 17.8 %collective-permute-start.4 = (f32[8,64,256]{2,1,0:T(8,128)S(1)}, f32[8,64,256]{2,1,0:T(8,128)S(1)}, u32[]{:S(2)}, u32[]{:S(2)}) collective-permute-start(f32[8,64,256]{2,1,0:T(8,128)S(1)} %get-tuple-element.39), channel_id=1, source_target_pairs={{0,1},{1,0},{2,3},{3,2},{4,5},{5,4},{6,7},{7,6},{8,9},{9,8},{10,11... | collective-permute-start | bytes 1572872 | tf_op jit(solution)/shard_map/ppermute | solution.py:35
  62.3 35.1 %all-to-all-start.1 = ((bf16[16,32,256]{2,1,0:T(8,128)(2,1)}), bf16[16,32,256]{2,1,0:T(8,128)(2,1)S(1)}, u32[]{:S(2)}, u32[]{:S(2)}) async-start(bf16[16,32,256]{2,1,0:T(8,128)(2,1)} %add_convert_fusion), calls=%async_computation.1 | async-start | bytes 524288 | tf_op jit(solution)/shard_map/all_to_all | solution.py:418
  75.6 10.4 %collective-permute-start.5 = (bf16[2,64,256]{2,1,0:T(8,128)(2,1)S(1)}, bf16[2,64,256]{2,1,0:T(8,128)(2,1)S(1)}, u32[]{:S(2)}, u32[]{:S(2)}) collective-permute-start(bf16[2,64,256]{2,1,0:T(8,128)(2,1)S(1)} %get-tuple-element.46), channel_id=1, source_target_pairs={{0,4},{1,5},{2,6},{3,7},{4,0},{5,1},{6,2},{7,3},{8,12},{9,13},{10,... | collective-permute-start | bytes 196616 | tf_op jit(solution)/shard_map/ppermute | solution.py:35
  79.2 7.7 %collective-permute-start.6 = (bf16[2,64,256]{2,1,0:T(8,128)(2,1)S(1)}, bf16[2,64,256]{2,1,0:T(8,128)(2,1)S(1)}, u32[]{:S(2)}, u32[]{:S(2)}) collective-permute-start(bf16[2,64,256]{2,1,0:T(8,128)(2,1)S(1)} %get-tuple-element.48), channel_id=1, source_target_pairs={{0,8},{1,9},{2,10},{3,11},{4,12},{5,13},{6,14},{7,15},{8,0},{9,1},... | collective-permute-start | bytes 196616 | tf_op jit(solution)/shard_map/ppermute | solution.py:35
  83.8 7.4 %collective-permute-start.7 = (bf16[2,64,256]{2,1,0:T(8,128)(2,1)S(1)}, bf16[2,64,256]{2,1,0:T(8,128)(2,1)S(1)}, u32[]{:S(2)}, u32[]{:S(2)}) collective-permute-start(bf16[2,64,256]{2,1,0:T(8,128)(2,1)S(1)} %get-tuple-element.47), channel_id=1, source_target_pairs={{0,12},{1,13},{2,14},{3,15},{4,8},{5,9},{6,10},{7,11},{8,4},{9,5},... | collective-permute-start | bytes 196616 | tf_op jit(solution)/shard_map/ppermute | solution.py:35
  91.2 6.2 %collective-permute-start.8 = (f32[64,256]{1,0:T(8,128)S(1)}, f32[64,256]{1,0:T(8,128)S(1)}, u32[]{:S(2)}, u32[]{:S(2)}) collective-permute-start(f32[64,256]{1,0:T(8,128)S(1)} %get-tuple-element.49), channel_id=1, source_target_pairs={{0,2},{1,3},{2,0},{3,1},{4,6},{5,7},{6,4},{7,5},{8,10},{9,11},{10,... | collective-permute-start | bytes 196616 | tf_op jit(solution)/shard_map/ppermute | solution.py:35

commit v9 on v7

--- a/solution.py
+++ b/solution.py
@@ -459,7 +459,7 @@
 
     total = keep + swapped(send, 1)
     total = total.reshape(4, 2, share, width)
-    got = [swapped(total[x].astype(BF), 4 * x) for x in (1, 2, 3)]
+    got = [swapped(total[x].astype(BF), 4 * x) for x in (2, 1, 3)]
     total = total[0] + sum(part.astype(F32) for part in got)
     held = rel_own * width // doms
     entity_share, rel_share = pl.pallas_call(

time: 89.4 us -> 89.4 us (level)
  no operation moved by 1% of the time
where the time goes in v9:
time: 89.4 us; the launch traced here: 88.6 us
  starting transfers between devices  39.2 us (44%)
  blocking collectives  18.4 us (21%)
  Pallas kernels  18 us (20%)
  waiting for transfers between devices  12.1 us (14%)
    all_to_all x1, blocking collectives, exchanged(): return lax.all_to_all(value, axis, split_axis=0, concat_axis=0, tiled=True)  18.4 us
    ppermute x6, starting transfers between devices, swapped(): return lax.ppermute(value, 'span', [(i, i ^ bits) for i in range(groups)])  16.8 us
    all_to_all x1, starting transfers between devices, exchanged(): return lax.all_to_all(value, axis, split_axis=0, concat_axis=0, tiled=True)  15.4 us
    ppermute x6, waiting for transfers between devices, swapped(): return lax.ppermute(value, 'span', [(i, i ^ bits) for i in range(groups)])  10.1 us
    pallas_call x3, Pallas kernels, forward(): pl.pallas_call(functools.partial(forward_kernel, turn, neg_scale), out_sh...  9.73 us
    ppermute x3, starting transfers between devices, shifted(): return lax.ppermute(value, ('dom', 'span'), pairs)  6.99 us
    pallas_call x1, Pallas kernels, shards(): pl.pallas_call(functools.partial(entity_kernel, neg_scale, groups), out_s...  4.22 us
    all_to_all x1, waiting for transfers between devices, exchanged(): return lax.all_to_all(value, axis, split_axis=0, concat_axis=0, tiled=True)  1.95 us
  transfers between devices with their start and end apart: 10, of which 5 were waited for; matrix products, arithmetic and copies ran while one was open for 0% of the time, Pallas kernels for 19%

profile of v9, /device:TPU:24, one launch (start us, length us, event | category | flops | bytes accessed | tf_op | source)
XLA Modules:
  0.0 88.6 jit_solution(6293973321272988774)
XLA Ops:
  0.6 3.1 %collective-permute-start = (bf16[1024,256]{1,0:T(8,128)(2,1)}, bf16[1024,256]{1,0:T(8,128)(2,1)S(1)}, u32[]{:S(2)}, u32[]{:S(2)}) collective-permute-start(bf16[1024,256]{1,0:T(8,128)(2,1)} %slab_ref.3), channel_id=1, source_target_pairs={{0,496},{1,481},{2,498},{3,483},{4,500},{5,485},{6,502},{7,487},{8... | collective-permute-start | bytes 1572872 | tf_op jit(solution)/shard_map/ppermute | solution.py:30
  3.8 1.7 %pack_lists.1 = s32[16,16,128]{2,1,0:T(8,128)} custom-call(s32[3,8,128]{2,1,0:T(8,128)} %bitcast.10, s32[3,4,128]{2,1,0:T(4,128)} %bitcast.11, s32[3,4,128]{2,1,0:T(4,128)} %bitcast.12, s32[3,1,64]{2,1,0:T(1,128)} %bitcast.13), custom_call_target="tpu_custom_call" | custom-call | tf_op jit(solution)/shard_map/pack_lists/pallas_call | solution.py:331
  5.5 18.4 %all_to_all.10.first_ref.refs_1_ = s32[16,16,128]{2,1,0:T(8,128)S(1)} all-to-all(s32[16,16,128]{2,1,0:T(8,128)} %pack_lists.1), channel_id=1, replica_groups=mesh['dom'=32,'span'=16] {'span'}, dimensions={0} | all-to-all | bytes 262144 | tf_op jit(solution)/shard_map/all_to_all | solution.py:39
  23.9 0.0 copy-start
  23.9 0.0 copy-start.1
  23.9 0.0 collective-permute-done.held_ref
  24.0 2.2 %collective-permute-start.1 = (bf16[1024,256]{1,0:T(8,128)(2,1)S(1)}, bf16[1024,256]{1,0:T(8,128)(2,1)S(1)}, u32[]{:S(2)}, u32[]{:S(2)}) collective-permute-start(bf16[1024,256]{1,0:T(8,128)(2,1)S(1)} %after_lists.1.refs_2_), channel_id=1, source_target_pairs={{0,1},{1,0},{2,3},{3,2},{4,5},{5,4},{6,7},{7,6},{8,9},{9,8},{10,11... | collective-permute-start | bytes 1572872 | tf_op jit(solution)/shard_map/ppermute | solution.py:35
  26.2 0.0 copy-done
  26.2 0.0 copy-done.1
  26.2 2.8 %own_bucket.1 = (bf16[256,1024]{1,0:T(8,128)(2,1)S(1)}, f32[4,256,256]{2,1,0:T(8,128)S(1)}, s32[8,512]{1,0:T(8,128)S(1)}, bf16[256,512]{1,0:T(8,128)(2,1)S(1)}, bf16[336,512]{1,0:T(8,128)(2,1)S(1)}) custom-call(s32[1]{0:T(128)} %bitcast.refs_0_.me_ref, s32[16,16,128]{2,1,0:T(8,128)S(1)} %all_to_all.10.first_ref.refs_1_, bf16[1024,256]{1,0:T(8,128)(2,1)S(1)} %copy-done.1, ...), custom_call_target="tpu_custom_call" | custom-call | flops 1450000000 | bytes 2000000 | tf_op jit(solution)/shard_map/own_bucket/pallas_call | solution.py:391
  29.0 2.8 %near_bucket.1 = (f32[4,256,256]{2,1,0:T(8,128)S(1)}, s32[8,512]{1,0:T(8,128)S(1)}, bf16[256,512]{1,0:T(8,128)(2,1)S(1)}, bf16[336,512]{1,0:T(8,128)(2,1)S(1)}, ...) custom-call(s32[1]{0:T(128)} %bitcast.refs_0_.me_ref, s32[16,16,128]{2,1,0:T(8,128)S(1)} %all_to_all.10.first_ref.refs_1_, ...), custom_call_target="tpu_custom_call" | custom-call | flops 1450000000 | bytes 2000000 | tf_op jit(solution)/shard_map/near_bucket/pallas_call | solution.py:391
  31.8 1.9 %collective-permute-start.3 = (bf16[336,512]{1,0:T(8,128)(2,1)S(1)}, bf16[336,512]{1,0:T(8,128)(2,1)S(1)}, u32[]{:S(2)}, u32[]{:S(2)}) collective-permute-start(bf16[336,512]{1,0:T(8,128)(2,1)S(1)} %get-tuple-element.36), channel_id=1, source_target_pairs={{0,16},{1,33},{2,18},{3,35},{4,20},{5,37},{6,22},{7,39},{8,24},{9,... | collective-permute-start | bytes 1032200 | tf_op jit(solution)/shard_map/ppermute | solution.py:30
  33.8 0.0 collective-permute-done.1.refs_2_
  33.8 4.1 %far_bucket.1 = (bf16[32,32,256]{2,1,0:T(8,128)(2,1)}, s32[8,512]{1,0:T(8,128)S(1)}, bf16[256,512]{1,0:T(8,128)(2,1)}, bf16[336,512]{1,0:T(8,128)(2,1)S(1)}, bf16[256,512]{1,0:T(8,128)(2,1)}) custom-call(s32[1]{0:T(128)} %bitcast.refs_0_.me_ref, s32[16,16,128]{2,1,0:T(8,128)S(1)} %all_to_all.10.first_ref.refs_1_, ...), custom_call_target="tpu_custom_call" | custom-call | flops 1450000000 | bytes 2000000 | tf_op jit(solution)/shard_map/far_bucket/pallas_call | solution.py:391
  37.9 1.9 %collective-permute-start.2 = (bf16[336,512]{1,0:T(8,128)(2,1)S(1)}, bf16[336,512]{1,0:T(8,128)(2,1)S(1)}, u32[]{:S(2)}, u32[]{:S(2)}) collective-permute-start(bf16[336,512]{1,0:T(8,128)(2,1)S(1)} %get-tuple-element.28), channel_id=1, source_target_pairs={{0,32},{1,17},{2,34},{3,19},{4,36},{5,21},{6,38},{7,23},{8,40},{9,... | collective-permute-start | bytes 1032200 | tf_op jit(solution)/shard_map/ppermute | solution.py:30
  39.8 15.4 %all-to-all-start.1 = ((bf16[32,32,256]{2,1,0:T(8,128)(2,1)}), bf16[32,32,256]{2,1,0:T(8,128)(2,1)S(1)}, u32[]{:S(2)}, u32[]{:S(2)}) async-start(bf16[32,32,256]{2,1,0:T(8,128)(2,1)} %get-tuple-element.39), calls=%async_computation.1 | async-start | bytes 1048576 | tf_op jit(solution)/shard_map/all_to_all | solution.py:39
  55.2 0.0 collective-permute-done.3.refs_7_
  55.2 4.2 %entity_gradients.1.before = f32[1024,256]{1,0:T(8,128)S(1)} custom-call(bf16[1024,256]{1,0:T(8,128)(2,1)S(1)} %copy-done.1, bf16[4,256,256]{2,1,0:T(8,128)(2,1)S(1)} %copy-done, s32[8,512]{1,0:T(8,128)S(1)} %get-tuple-element.29.refs_0_, s32[8,512]{1,0:T(8,128)S(1)} %get-tuple-element.30.refs_1_, s32[8,512]{1,0:T(8,128)S(1)} %get-tuple-element.31.refs_2_, ...), custom_call_target="tpu_custom_call" | custom-call | flops 3000000000 | bytes 3000000 | tf_op jit(solution)/shard_map/entity_gradients/pallas_call | solution.py:414
  59.5 0.0 collective-permute-done.2.pk
  59.5 1.6 %last_entity_gradients.1 = (f32[8,64,256]{2,1,0:T(8,128)S(1)}, f32[8,64,256]{2,1,0:T(8,128)S(1)}) custom-call(s32[1]{0:T(128)} %bitcast.refs_0_.me_ref, bf16[1024,256]{1,0:T(8,128)(2,1)S(1)} %copy-done.1, bf16[336,512]{1,0:T(8,128)(2,1)S(1)} %collective-permute-done.2.pk, f32[1024,256]{1,0:T(8,128)S(1)} %entity_gradients.1.before), custom_call_target="tpu_custom_call" | custom-call | flops 1000000000 | bytes 2000000 | tf_op jit(solution)/shard_map/last_entity_gradients/pallas_call | solution.py:444
  61.1 1.9 %collective-permute-start.4 = (f32[8,64,256]{2,1,0:T(8,128)S(1)}, f32[8,64,256]{2,1,0:T(8,128)S(1)}, u32[]{:S(2)}, u32[]{:S(2)}) collective-permute-start(f32[8,64,256]{2,1,0:T(8,128)S(1)} %get-tuple-element.38), channel_id=1, source_target_pairs={{0,1},{1,0},{2,3},{3,2},{4,5},{5,4},{6,7},{7,6},{8,9},{9,8},{10,11... | collective-permute-start | bytes 1572872 | tf_op jit(solution)/shard_map/ppermute | solution.py:35
  63.0 1.9 %collective-permute-done.4 = f32[8,64,256]{2,1,0:T(8,128)S(1)} collective-permute-done((f32[8,64,256]{2,1,0:T(8,128)S(1)}, f32[8,64,256]{2,1,0:T(8,128)S(1)}, u32[]{:S(2)}, u32[]{:S(2)}) %collective-permute-start.4) | collective-permute-done | bytes 524320 | tf_op jit(solution)/shard_map/ppermute | solution.py:35
  64.9 0.1 fusion
  65.0 4.9 %collective-permute-start.5 = (bf16[2,64,256]{2,1,0:T(8,128)(2,1)S(1)}, bf16[2,64,256]{2,1,0:T(8,128)(2,1)S(1)}, u32[]{:S(2)}, u32[]{:S(2)}) collective-permute-start(bf16[2,64,256]{2,1,0:T(8,128)(2,1)S(1)} %get-tuple-element.44), channel_id=1, source_target_pairs={{0,8},{1,9},{2,10},{3,11},{4,12},{5,13},{6,14},{7,15},{8,0},{9,1},... | collective-permute-start | bytes 196616 | tf_op jit(solution)/shard_map/ppermute | solution.py:35
  69.9 2.5 %collective-permute-start.6 = (bf16[2,64,256]{2,1,0:T(8,128)(2,1)S(1)}, bf16[2,64,256]{2,1,0:T(8,128)(2,1)S(1)}, u32[]{:S(2)}, u32[]{:S(2)}) collective-permute-start(bf16[2,64,256]{2,1,0:T(8,128)(2,1)S(1)} %get-tuple-element.46), channel_id=1, source_target_pairs={{0,4},{1,5},{2,6},{3,7},{4,0},{5,1},{6,2},{7,3},{8,12},{9,13},{10,... | collective-permute-start | bytes 196616 | tf_op jit(solution)/shard_map/ppermute | solution.py:35
  72.4 2.5 %collective-permute-start.7 = (bf16[2,64,256]{2,1,0:T(8,128)(2,1)S(1)}, bf16[2,64,256]{2,1,0:T(8,128)(2,1)S(1)}, u32[]{:S(2)}, u32[]{:S(2)}) collective-permute-start(bf16[2,64,256]{2,1,0:T(8,128)(2,1)S(1)} %get-tuple-element.45), channel_id=1, source_target_pairs={{0,12},{1,13},{2,14},{3,15},{4,8},{5,9},{6,10},{7,11},{8,4},{9,5},... | collective-permute-start | bytes 196616 | tf_op jit(solution)/shard_map/ppermute | solution.py:35
  74.9 0.0 collective-permute-done.5
  74.9 1.2 %collective-permute-done.6 = bf16[2,64,256]{2,1,0:T(8,128)(2,1)S(1)} collective-permute-done((bf16[2,64,256]{2,1,0:T(8,128)(2,1)S(1)}, bf16[2,64,256]{2,1,0:T(8,128)(2,1)S(1)}, u32[]{:S(2)}, u32[]{:S(2)}) %collective-permute-start.6) | collective-permute-done | bytes 65568 | tf_op jit(solution)/shard_map/ppermute | solution.py:35
  76.0 3.7 %collective-permute-done.7 = bf16[2,64,256]{2,1,0:T(8,128)(2,1)S(1)} collective-permute-done((bf16[2,64,256]{2,1,0:T(8,128)(2,1)S(1)}, bf16[2,64,256]{2,1,0:T(8,128)(2,1)S(1)}, u32[]{:S(2)}, u32[]{:S(2)}) %collective-permute-start.7) | collective-permute-done | bytes 65568 | tf_op jit(solution)/shard_map/ppermute | solution.py:35
  79.8 2.8 %collective-permute-start.8 = (f32[64,256]{1,0:T(8,128)S(1)}, f32[64,256]{1,0:T(8,128)S(1)}, u32[]{:S(2)}, u32[]{:S(2)}) collective-permute-start(f32[64,256]{1,0:T(8,128)S(1)} %get-tuple-element.47), channel_id=1, source_target_pairs={{0,2},{1,3},{2,0},{3,1},{4,6},{5,7},{6,4},{7,5},{8,10},{9,11},{10,... | collective-permute-start | bytes 196616 | tf_op jit(solution)/shard_map/ppermute | solution.py:35
  82.6 3.4 %collective-permute-done.8.got_ref = f32[64,256]{1,0:T(8,128)S(1)} collective-permute-done((f32[64,256]{1,0:T(8,128)S(1)}, f32[64,256]{1,0:T(8,128)S(1)}, u32[]{:S(2)}, u32[]{:S(2)}) %collective-permute-start.8) | collective-permute-done | bytes 65568 | tf_op jit(solution)/shard_map/ppermute | solution.py:35
  86.0 2.0 %all-to-all-done.1.parts_ref = bf16[32,32,256]{2,1,0:T(8,128)(2,1)S(1)} async-done(((bf16[32,32,256]{2,1,0:T(8,128)(2,1)}), bf16[32,32,256]{2,1,0:T(8,128)(2,1)S(1)}, u32[]{:S(2)}, u32[]{:S(2)}) %all-to-all-start.1) | async-done | bytes 524320 | tf_op jit(solution)/shard_map/all_to_all | solution.py:39
  87.9 0.7 last_sums.1
  (4 shorter events, 0.1 us)
Async XLA Ops:
  0.6 23.3 %collective-permute-start = (bf16[1024,256]{1,0:T(8,128)(2,1)}, bf16[1024,256]{1,0:T(8,128)(2,1)S(1)}, u32[]{:S(2)}, u32[]{:S(2)}) collective-permute-start(bf16[1024,256]{1,0:T(8,128)(2,1)} %slab_ref.3), channel_id=1, source_target_pairs={{0,496},{1,481},{2,498},{3,483},{4,500},{5,485},{6,502},{7,487},{8... | collective-permute-start | bytes 1572872 | tf_op jit(solution)/shard_map/ppermute | solution.py:30
  23.9 2.3 %copy-start = (bf16[4,256,256]{2,1,0:T(8,128)(2,1)S(1)}, bf16[4,256,256]{2,1,0:T(8,128)(2,1)}, u32[]{:S(2)}) copy-start(bf16[4,256,256]{2,1,0:T(8,128)(2,1)} %ops_hbm.1) | copy-start | bytes 1572868
  23.9 2.3 %copy-start.1 = (bf16[1024,256]{1,0:T(8,128)(2,1)S(1)}, bf16[1024,256]{1,0:T(8,128)(2,1)}, u32[]{:S(2)}) copy-start(bf16[1024,256]{1,0:T(8,128)(2,1)} %slab_ref.3) | copy-start | bytes 1572868
  24.0 9.8 %collective-permute-start.1 = (bf16[1024,256]{1,0:T(8,128)(2,1)S(1)}, bf16[1024,256]{1,0:T(8,128)(2,1)S(1)}, u32[]{:S(2)}, u32[]{:S(2)}) collective-permute-start(bf16[1024,256]{1,0:T(8,128)(2,1)S(1)} %after_lists.1.refs_2_), channel_id=1, source_target_pairs={{0,1},{1,0},{2,3},{3,2},{4,5},{5,4},{6,7},{7,6},{8,9},{9,8},{10,11... | collective-permute-start | bytes 1572872 | tf_op jit(solution)/shard_map/ppermute | solution.py:35
  31.8 23.4 %collective-permute-start.3 = (bf16[336,512]{1,0:T(8,128)(2,1)S(1)}, bf16[336,512]{1,0:T(8,128)(2,1)S(1)}, u32[]{:S(2)}, u32[]{:S(2)}) collective-permute-start(bf16[336,512]{1,0:T(8,128)(2,1)S(1)} %get-tuple-element.36), channel_id=1, source_target_pairs={{0,16},{1,33},{2,18},{3,35},{4,20},{5,37},{6,22},{7,39},{8,24},{9,... | collective-permute-start | bytes 1032200 | tf_op jit(solution)/shard_map/ppermute | solution.py:30
  37.9 21.6 %collective-permute-start.2 = (bf16[336,512]{1,0:T(8,128)(2,1)S(1)}, bf16[336,512]{1,0:T(8,128)(2,1)S(1)}, u32[]{:S(2)}, u32[]{:S(2)}) collective-permute-start(bf16[336,512]{1,0:T(8,128)(2,1)S(1)} %get-tuple-element.28), channel_id=1, source_target_pairs={{0,32},{1,17},{2,34},{3,19},{4,36},{5,21},{6,38},{7,23},{8,40},{9,... | collective-permute-start | bytes 1032200 | tf_op jit(solution)/shard_map/ppermute | solution.py:30
  39.8 48.1 %all-to-all-start.1 = ((bf16[32,32,256]{2,1,0:T(8,128)(2,1)}), bf16[32,32,256]{2,1,0:T(8,128)(2,1)S(1)}, u32[]{:S(2)}, u32[]{:S(2)}) async-start(bf16[32,32,256]{2,1,0:T(8,128)(2,1)} %get-tuple-element.39), calls=%async_computation.1 | async-start | bytes 1048576 | tf_op jit(solution)/shard_map/all_to_all | solution.py:39
  61.1 3.8 %collective-permute-start.4 = (f32[8,64,256]{2,1,0:T(8,128)S(1)}, f32[8,64,256]{2,1,0:T(8,128)S(1)}, u32[]{:S(2)}, u32[]{:S(2)}) collective-permute-start(f32[8,64,256]{2,1,0:T(8,128)S(1)} %get-tuple-element.38), channel_id=1, source_target_pairs={{0,1},{1,0},{2,3},{3,2},{4,5},{5,4},{6,7},{7,6},{8,9},{9,8},{10,11... | collective-permute-start | bytes 1572872 | tf_op jit(solution)/shard_map/ppermute | solution.py:35
  65.0 9.9 %collective-permute-start.5 = (bf16[2,64,256]{2,1,0:T(8,128)(2,1)S(1)}, bf16[2,64,256]{2,1,0:T(8,128)(2,1)S(1)}, u32[]{:S(2)}, u32[]{:S(2)}) collective-permute-start(bf16[2,64,256]{2,1,0:T(8,128)(2,1)S(1)} %get-tuple-element.44), channel_id=1, source_target_pairs={{0,8},{1,9},{2,10},{3,11},{4,12},{5,13},{6,14},{7,15},{8,0},{9,1},... | collective-permute-start | bytes 196616 | tf_op jit(solution)/shard_map/ppermute | solution.py:35
  69.9 6.2 %collective-permute-start.6 = (bf16[2,64,256]{2,1,0:T(8,128)(2,1)S(1)}, bf16[2,64,256]{2,1,0:T(8,128)(2,1)S(1)}, u32[]{:S(2)}, u32[]{:S(2)}) collective-permute-start(bf16[2,64,256]{2,1,0:T(8,128)(2,1)S(1)} %get-tuple-element.46), channel_id=1, source_target_pairs={{0,4},{1,5},{2,6},{3,7},{4,0},{5,1},{6,2},{7,3},{8,12},{9,13},{10,... | collective-permute-start | bytes 196616 | tf_op jit(solution)/shard_map/ppermute | solution.py:35
  72.4 7.4 %collective-permute-start.7 = (bf16[2,64,256]{2,1,0:T(8,128)(2,1)S(1)}, bf16[2,64,256]{2,1,0:T(8,128)(2,1)S(1)}, u32[]{:S(2)}, u32[]{:S(2)}) collective-permute-start(bf16[2,64,256]{2,1,0:T(8,128)(2,1)S(1)} %get-tuple-element.45), channel_id=1, source_target_pairs={{0,12},{1,13},{2,14},{3,15},{4,8},{5,9},{6,10},{7,11},{8,4},{9,5},... | collective-permute-start | bytes 196616 | tf_op jit(solution)/shard_map/ppermute | solution.py:35
  79.8 6.2 %collective-permute-start.8 = (f32[64,256]{1,0:T(8,128)S(1)}, f32[64,256]{1,0:T(8,128)S(1)}, u32[]{:S(2)}, u32[]{:S(2)}) collective-permute-start(f32[64,256]{1,0:T(8,128)S(1)} %get-tuple-element.47), channel_id=1, source_target_pairs={{0,2},{1,3},{2,0},{3,1},{4,6},{5,7},{6,4},{7,5},{8,10},{9,11},{10,... | collective-permute-start | bytes 196616 | tf_op jit(solution)/shard_map/ppermute | solution.py:35

commit v10 on v7

--- a/solution.py
+++ b/solution.py
@@ -73,8 +73,14 @@
     return carry
 
 
-def tie_kernel(held_ref, first_ref, out_ref):
+def tie_kernel(held_ref, first_ref, other_ref, out_ref):
     out_ref[...] = held_ref[...]
+
+
+def turn_kernel(slab_ref, ops_ref, slab_t_ref, ops_t_ref):
+    slab_t_ref[...] = slab_ref[...].T
+    for i in range(ops_ref.shape[0]):
+        ops_t_ref[i] = ops_ref[i].T
 
 
 def one_hot(rows, at, shape):
@@ -89,32 +95,26 @@
 def forward_kernel(turn, neg_scale, *refs):
     first, last = turn == 0, turn == 2
     olds = (0, 2, 1)[turn]
-    me_ref, x_ref, slab, ops_hbm = refs[:4]
-    refs = refs[4:]
+    me_ref, x_ref, slab, ops_ref, et0_ref = refs[:5]
+    refs = refs[5:]
     if not first:
-        et0_ref, sum_ref = refs[:2]
-        refs = refs[2:]
+        sum_ref, refs = refs[0], refs[1:]
     old_refs, refs = refs[:olds], refs[olds:]
-    if first:
-        et0_ref, rel_acc = refs[:2]
-        refs = refs[2:]
-    elif last:
+    if last:
         rel_ref, refs = refs[0], refs[1:]
     else:
         rel_acc, refs = refs[0], refs[1:]
     lrow_ref, qg_ref, pk = refs[:3]
     old_hbms, refs = refs[3 : 3 + olds], refs[3 + olds :]
-    oh_ref, whi_ref, wlo_ref, mult_ref, ops_ref, et_ref, ops_sem, old_sems = refs[:8]
+    oh_ref, whi_ref, wlo_ref, mult_ref, et_ref, old_sems = refs[:6]
     if last:
-        rel_acc, qg_hbm, qg_ref, qg_sem = refs[8], qg_ref, refs[9], refs[10]
-    ops_copy = pltpu.make_async_copy(ops_hbm, ops_ref, ops_sem)
-    ops_copy.start()
+        rel_acc, qg_hbm, qg_ref, qg_sem = refs[6], qg_ref, refs[7], refs[8]
     old_copies = [
         pltpu.make_async_copy(old_refs[n], old_hbms[n], old_sems.at[n]) for n in range(olds)
     ]
     for copy in old_copies:
         copy.start()
-    rel_own, width, _ = ops_hbm.shape
+    rel_own, width, _ = ops_ref.shape
     groups = x_ref.shape[0]
     part_rows = slab.shape[0]
     slots = rel_own * 128
@@ -163,7 +163,8 @@
         pk[at : at + 16, :] = narrow(jnp.concatenate(group, 1))
 
     slab_t = et0_ref if first else et_ref
-    slab_t[...] = slab[...].T
+    if not first:
+        slab_t[...] = slab[...].T
 
     def left_hot(n, carry):
         at = n * chunk
@@ -177,9 +178,8 @@
 
     loop(chunks, left_hot, 0)
     left_t = dot(et0_ref[...], oh_ref[...]).astype(BF)
-    ops_copy.wait()
     query_t = jnp.concatenate(
-        [dot(ops_ref[i], left_t[:, 128 * i : 128 * (i + 1)], TN) for i in range(rel_own)], 1
+        [dot(ops_ref[i], left_t[:, 128 * i : 128 * (i + 1)]) for i in range(rel_own)], 1
     ).astype(BF)
     pk[0:width, :] = query_t
     half_t = query_t * 0.5
@@ -341,15 +341,27 @@
         counts.reshape(buckets, 1, relations),
     )
     received = exchanged(packed, "span")
+    slab_t, ops_t = pl.pallas_call(
+        turn_kernel,
+        out_shape=(
+            jax.ShapeDtypeStruct((width, part_rows), BF),
+            jax.ShapeDtypeStruct(operators.shape, BF),
+        ),
+        in_specs=[VMEM, VMEM],
+        out_specs=(VMEM, VMEM),
+        compiler_params=small,
+        cost_estimate=pl.CostEstimate(flops=0, bytes_accessed=2_000_000, transcendentals=0),
+        name="transposes",
+    )(entities, operators)
     near = shifted(entities, -1, -2)
     near = pl.pallas_call(
         tie_kernel,
         out_shape=jax.ShapeDtypeStruct(entities.shape, BF),
-        in_specs=[VMEM, VMEM],
+        in_specs=[VMEM, VMEM, VMEM],
         out_specs=VMEM,
         compiler_params=small,
         name="after_lists",
-    )(near, received)
+    )(near, received, slab_t)
     slabs = [near, swapped(near, 1)]
 
     me = lax.axis_index("span").astype(jnp.int32).reshape(1)
@@ -361,7 +373,7 @@
 
     def forward(turn, slab, before, olds):
         last = turn == 2
-        outs = [jax.ShapeDtypeStruct((width, part_rows), BF)] if turn == 0 else []
+        outs = []
         relation_parts = jax.ShapeDtypeStruct((doms, rel_own * width // doms, width), BF)
         outs.append(relation_parts if last else sums)
         outs.append(jax.ShapeDtypeStruct((8, slots), jnp.int32))
@@ -377,9 +389,7 @@
             wide,
             wide,
             pltpu.VMEM((part_rows, 128), F32),
-            pltpu.VMEM(operators.shape, BF),
             pltpu.VMEM((width, part_rows), BF),
-            pltpu.SemaphoreType.DMA,
             pltpu.SemaphoreType.DMA((2,)),
         ]
         if last:
@@ -391,7 +401,7 @@
         return pl.pallas_call(
             functools.partial(forward_kernel, turn, neg_scale),
             out_shape=outs,
-            in_specs=[SMEM, VMEM, VMEM, HBM] + [VMEM] * (len(before) + len(olds)),
+            in_specs=[SMEM] + [VMEM] * (4 + len(before) + len(olds)),
             out_specs=specs,
             scratch_shapes=scratch,
             compiler_params=limit,
@@ -399,14 +409,14 @@
                 flops=1_450_000_000, bytes_accessed=2_000_000, transcendentals=500_000
             ),
             name=("own_bucket", "near_bucket", "far_bucket")[turn],
-        )(me, received, slab, operators, *before, *olds)
-
-    slab_t, rel_sum, lrow_0, qg_0, pack_0 = forward(0, entities, (), ())
+        )(me, received, slab, ops_t, slab_t, *before, *olds)
+
+    rel_sum, lrow_0, qg_0, pack_0 = forward(0, entities, (), ())
     rel_sum, lrow_1, qg_1, pack_1, pack_0, qg_0 = forward(
-        1, slabs[0], (slab_t, rel_sum), (pack_0, qg_0)
+        1, slabs[0], (rel_sum,), (pack_0, qg_0)
     )
     pack_1 = shifted(pack_1, 1, 2)
-    rel_parts, lrow_2, qg_2, pack_2, qg_1 = forward(2, slabs[1], (slab_t, rel_sum), (qg_1,))
+    rel_parts, lrow_2, qg_2, pack_2, qg_1 = forward(2, slabs[1], (rel_sum,), (qg_1,))
     pack_2 = shifted(pack_2, 2, 1)
     rel_arrived = exchanged(rel_parts, "dom")
 

time: 89.4 us -> 89.7 us (level)
  blocking collectives: 18.4 us -> 0 us
  starting transfers between devices: 39.7 us -> 53 us
  waiting for transfers between devices: 11.6 us -> 14.3 us
  local copies, waits for them, and re-layouts: 0.03 us -> 2.11 us
    all_to_all x1 -> x0, blocking collectives: 18.4 us -> none  [exchanged(): return lax.all_to_all(value, axis, split_axis=0, concat_axis=0, tiled=True)]
    all_to_all x1 -> x2, starting transfers between devices: 15.4 us -> 28.7 us  [exchanged(): return lax.all_to_all(value, axis, split_axis=0, concat_axis=0, tiled=True)]
    all_to_all x1 -> x2, waiting for transfers between devices: 1.35 us -> 4.12 us  [exchanged(): return lax.all_to_all(value, axis, split_axis=0, concat_axis=0, tiled=True)]
    unnamed x4 -> x8, local copies, waits for them, and re-layouts: 0.01 us -> 2.09 us
  transfers between devices with their start and end apart: 10 -> 11, of which waited for: 5 -> 6; matrix products, arithmetic and copies ran while one was open for 0% -> 0% of each run, Pallas kernels for 19% -> 20%
where the time goes in v10:
time: 89.7 us; the launch traced here: 88.9 us
  starting transfers between devices  53 us (59%)
  Pallas kernels  18.4 us (21%)
  waiting for transfers between devices  14.3 us (16%)
  local copies, waits for them, and re-layouts  2.11 us (2%)
    all_to_all x2, starting transfers between devices, exchanged(): return lax.all_to_all(value, axis, split_axis=0, concat_axis=0, tiled=True)  28.7 us
    ppermute x6, starting transfers between devices, swapped(): return lax.ppermute(value, 'span', [(i, i ^ bits) for i in range(groups)])  17.3 us
    ppermute x6, waiting for transfers between devices, swapped(): return lax.ppermute(value, 'span', [(i, i ^ bits) for i in range(groups)])  10.2 us
    pallas_call x3, Pallas kernels, forward(): pl.pallas_call(functools.partial(forward_kernel, turn, neg_scale), out_sh...  9.84 us
    ppermute x3, starting transfers between devices, shifted(): return lax.ppermute(value, ('dom', 'span'), pairs)  6.99 us
    pallas_call x1, Pallas kernels, shards(): pl.pallas_call(functools.partial(entity_kernel, neg_scale, groups), out_s...  4.22 us
    all_to_all x2, waiting for transfers between devices, exchanged(): return lax.all_to_all(value, axis, split_axis=0, concat_axis=0, tiled=True)  4.12 us
    unnamed x8, local copies, waits for them, and re-layouts  2.09 us
  transfers between devices with their start and end apart: 11, of which 6 were waited for; matrix products, arithmetic and copies ran while one was open for 0% of the time, Pallas kernels for 20%

profile of v10, /device:TPU:24, one launch (start us, length us, event | category | flops | bytes accessed | tf_op | source)
XLA Modules:
  0.0 88.9 jit_solution(261040868436287219)
XLA Ops:
  0.6 3.1 %collective-permute-start = (bf16[1024,256]{1,0:T(8,128)(2,1)}, bf16[1024,256]{1,0:T(8,128)(2,1)S(1)}, u32[]{:S(2)}, u32[]{:S(2)}) collective-permute-start(bf16[1024,256]{1,0:T(8,128)(2,1)} %slab_ref.5), channel_id=1, source_target_pairs={{0,496},{1,481},{2,498},{3,483},{4,500},{5,485},{6,502},{7,487},{8... | collective-permute-start | bytes 1572872 | tf_op jit(solution)/shard_map/ppermute | solution.py:30
  3.8 1.7 %pack_lists.1 = s32[16,16,128]{2,1,0:T(8,128)} custom-call(s32[3,8,128]{2,1,0:T(8,128)} %bitcast.10, s32[3,4,128]{2,1,0:T(4,128)} %bitcast.11, s32[3,4,128]{2,1,0:T(4,128)} %bitcast.12, s32[3,1,64]{2,1,0:T(1,128)} %bitcast.13), custom_call_target="tpu_custom_call" | custom-call | tf_op jit(solution)/shard_map/pack_lists/pallas_call | solution.py:331
  5.5 13.2 %all-to-all-start = ((s32[16,16,128]{2,1,0:T(8,128)}), s32[16,16,128]{2,1,0:T(8,128)S(1)}, u32[]{:S(2)}, u32[]{:S(2)}) async-start(s32[16,16,128]{2,1,0:T(8,128)} %pack_lists.1), calls=%async_computation | async-start | bytes 262144 | tf_op jit(solution)/shard_map/all_to_all | solution.py:39
  18.7 0.0 copy-start
  18.7 1.0 %copy-done = bf16[4,256,256]{2,1,0:T(8,128)(2,1)S(1)} copy-done((bf16[4,256,256]{2,1,0:T(8,128)(2,1)S(1)}, bf16[4,256,256]{2,1,0:T(8,128)(2,1)}, u32[]{:S(2)}) %copy-start) | copy-done | bytes 524312
  19.7 0.0 copy-start.2
  19.7 1.0 %copy-done.2 = bf16[1024,256]{1,0:T(8,128)(2,1)S(1)} copy-done((bf16[1024,256]{1,0:T(8,128)(2,1)S(1)}, bf16[1024,256]{1,0:T(8,128)(2,1)}, u32[]{:S(2)}) %copy-start.2) | copy-done | bytes 524312
  20.8 0.3 transposes.1
  21.1 2.8 %all-to-all-done.first_ref.refs_1_ = s32[16,16,128]{2,1,0:T(8,128)S(1)} async-done(((s32[16,16,128]{2,1,0:T(8,128)}), s32[16,16,128]{2,1,0:T(8,128)S(1)}, u32[]{:S(2)}, u32[]{:S(2)}) %all-to-all-start) | async-done | bytes 131104 | tf_op jit(solution)/shard_map/all_to_all | solution.py:39
  23.9 0.0 collective-permute-done.held_ref
  23.9 0.0 copy-start.3
  23.9 2.2 %collective-permute-start.1 = (bf16[1024,256]{1,0:T(8,128)(2,1)S(1)}, bf16[1024,256]{1,0:T(8,128)(2,1)S(1)}, u32[]{:S(2)}, u32[]{:S(2)}) collective-permute-start(bf16[1024,256]{1,0:T(8,128)(2,1)S(1)} %after_lists.1.refs_2_), channel_id=1, source_target_pairs={{0,1},{1,0},{2,3},{3,2},{4,5},{5,4},{6,7},{7,6},{8,9},{9,8},{10,11... | collective-permute-start | bytes 1572872 | tf_op jit(solution)/shard_map/ppermute | solution.py:35
  26.2 0.0 copy-done.3
  26.2 2.8 %own_bucket.1 = (f32[4,256,256]{2,1,0:T(8,128)S(1)}, s32[8,512]{1,0:T(8,128)S(1)}, bf16[256,512]{1,0:T(8,128)(2,1)S(1)}, bf16[336,512]{1,0:T(8,128)(2,1)S(1)}) custom-call(s32[1]{0:T(128)} %bitcast.refs_0_.me_ref, s32[16,16,128]{2,1,0:T(8,128)S(1)} %all-to-all-done.first_ref.refs_1_, bf16[1024,256]{1,0:T(8,128)(2,1)S(1)} %copy-done.3, ...), custom_call_target="tpu_custom_call" | custom-call | flops 1450000000 | bytes 2000000 | tf_op jit(solution)/shard_map/own_bucket/pallas_call | solution.py:401
  29.0 2.8 %near_bucket.1 = (f32[4,256,256]{2,1,0:T(8,128)S(1)}, s32[8,512]{1,0:T(8,128)S(1)}, bf16[256,512]{1,0:T(8,128)(2,1)S(1)}, bf16[336,512]{1,0:T(8,128)(2,1)S(1)}, ...) custom-call(s32[1]{0:T(128)} %bitcast.refs_0_.me_ref, s32[16,16,128]{2,1,0:T(8,128)S(1)} %all-to-all-done.first_ref.refs_1_, ...), custom_call_target="tpu_custom_call" | custom-call | flops 1450000000 | bytes 2000000 | tf_op jit(solution)/shard_map/near_bucket/pallas_call | solution.py:401
  31.8 1.9 %collective-permute-start.3 = (bf16[336,512]{1,0:T(8,128)(2,1)S(1)}, bf16[336,512]{1,0:T(8,128)(2,1)S(1)}, u32[]{:S(2)}, u32[]{:S(2)}) collective-permute-start(bf16[336,512]{1,0:T(8,128)(2,1)S(1)} %get-tuple-element.38), channel_id=1, source_target_pairs={{0,16},{1,33},{2,18},{3,35},{4,20},{5,37},{6,22},{7,39},{8,24},{9,... | collective-permute-start | bytes 1032200 | tf_op jit(solution)/shard_map/ppermute | solution.py:30
  33.7 0.0 collective-permute-done.1.refs_2_
  33.8 4.2 %far_bucket.1 = (bf16[32,32,256]{2,1,0:T(8,128)(2,1)}, s32[8,512]{1,0:T(8,128)S(1)}, bf16[256,512]{1,0:T(8,128)(2,1)}, bf16[336,512]{1,0:T(8,128)(2,1)}, bf16[256,512]{1,0:T(8,128)(2,1)}) custom-call(s32[1]{0:T(128)} %bitcast.refs_0_.me_ref, s32[16,16,128]{2,1,0:T(8,128)S(1)} %all-to-all-done.first_ref.refs_1_, ...), custom_call_target="tpu_custom_call" | custom-call | flops 1450000000 | bytes 2000000 | tf_op jit(solution)/shard_map/far_bucket/pallas_call | solution.py:401
  38.0 1.9 %collective-permute-start.2 = (bf16[336,512]{1,0:T(8,128)(2,1)}, bf16[336,512]{1,0:T(8,128)(2,1)S(1)}, u32[]{:S(2)}, u32[]{:S(2)}) collective-permute-start(bf16[336,512]{1,0:T(8,128)(2,1)} %get-tuple-element.30), channel_id=1, source_target_pairs={{0,32},{1,17},{2,34},{3,19},{4,36},{5,21},{6,38},{7,23},{8,40},{9,... | collective-permute-start | bytes 1032200 | tf_op jit(solution)/shard_map/ppermute | solution.py:30
  39.9 0.0 copy-start.1
  39.9 15.5 %all-to-all-start.1 = ((bf16[32,32,256]{2,1,0:T(8,128)(2,1)}), bf16[32,32,256]{2,1,0:T(8,128)(2,1)S(1)}, u32[]{:S(2)}, u32[]{:S(2)}) async-start(bf16[32,32,256]{2,1,0:T(8,128)(2,1)} %get-tuple-element.41), calls=%async_computation.1 | async-start | bytes 1048576 | tf_op jit(solution)/shard_map/all_to_all | solution.py:39
  55.5 0.0 collective-permute-done.3.refs_7_
  55.5 0.0 copy-done.1
  55.5 4.2 %entity_gradients.1.before = f32[1024,256]{1,0:T(8,128)S(1)} custom-call(bf16[1024,256]{1,0:T(8,128)(2,1)S(1)} %copy-done.3, bf16[4,256,256]{2,1,0:T(8,128)(2,1)S(1)} %copy-done.1, s32[8,512]{1,0:T(8,128)S(1)} %get-tuple-element.31.refs_0_, s32[8,512]{1,0:T(8,128)S(1)} %get-tuple-element.32.refs_1_, s32[8,512]{1,0:T(8,128)S(1)} %get-tuple-element.33.refs_2_, ...), custom_call_target="tpu_custom_call" | custom-call | flops 3000000000 | bytes 3000000 | tf_op jit(solution)/shard_map/entity_gradients/pallas_call | solution.py:424
  59.7 0.0 collective-permute-done.2.pk
  59.7 1.6 %last_entity_gradients.1 = (f32[8,64,256]{2,1,0:T(8,128)S(1)}, f32[8,64,256]{2,1,0:T(8,128)S(1)}) custom-call(s32[1]{0:T(128)} %bitcast.refs_0_.me_ref, bf16[1024,256]{1,0:T(8,128)(2,1)S(1)} %copy-done.3, bf16[336,512]{1,0:T(8,128)(2,1)S(1)} %collective-permute-done.2.pk, f32[1024,256]{1,0:T(8,128)S(1)} %entity_gradients.1.before), custom_call_target="tpu_custom_call" | custom-call | flops 1000000000 | bytes 2000000 | tf_op jit(solution)/shard_map/last_entity_gradients/pallas_call | solution.py:454
  61.3 1.9 %collective-permute-start.4 = (f32[8,64,256]{2,1,0:T(8,128)S(1)}, f32[8,64,256]{2,1,0:T(8,128)S(1)}, u32[]{:S(2)}, u32[]{:S(2)}) collective-permute-start(f32[8,64,256]{2,1,0:T(8,128)S(1)} %get-tuple-element.40), channel_id=1, source_target_pairs={{0,1},{1,0},{2,3},{3,2},{4,5},{5,4},{6,7},{7,6},{8,9},{9,8},{10,11... | collective-permute-start | bytes 1572872 | tf_op jit(solution)/shard_map/ppermute | solution.py:35
  63.2 1.9 %collective-permute-done.4 = f32[8,64,256]{2,1,0:T(8,128)S(1)} collective-permute-done((f32[8,64,256]{2,1,0:T(8,128)S(1)}, f32[8,64,256]{2,1,0:T(8,128)S(1)}, u32[]{:S(2)}, u32[]{:S(2)}) %collective-permute-start.4) | collective-permute-done | bytes 524320 | tf_op jit(solution)/shard_map/ppermute | solution.py:35
  65.1 0.1 fusion
  65.2 3.4 %collective-permute-start.5 = (bf16[2,64,256]{2,1,0:T(8,128)(2,1)S(1)}, bf16[2,64,256]{2,1,0:T(8,128)(2,1)S(1)}, u32[]{:S(2)}, u32[]{:S(2)}) collective-permute-start(bf16[2,64,256]{2,1,0:T(8,128)(2,1)S(1)} %get-tuple-element.46), channel_id=1, source_target_pairs={{0,4},{1,5},{2,6},{3,7},{4,0},{5,1},{6,2},{7,3},{8,12},{9,13},{10,... | collective-permute-start | bytes 196616 | tf_op jit(solution)/shard_map/ppermute | solution.py:35
  68.6 4.6 %collective-permute-start.6 = (bf16[2,64,256]{2,1,0:T(8,128)(2,1)S(1)}, bf16[2,64,256]{2,1,0:T(8,128)(2,1)S(1)}, u32[]{:S(2)}, u32[]{:S(2)}) collective-permute-start(bf16[2,64,256]{2,1,0:T(8,128)(2,1)S(1)} %get-tuple-element.48), channel_id=1, source_target_pairs={{0,8},{1,9},{2,10},{3,11},{4,12},{5,13},{6,14},{7,15},{8,0},{9,1},... | collective-permute-start | bytes 196616 | tf_op jit(solution)/shard_map/ppermute | solution.py:35
  73.3 2.4 %collective-permute-start.7 = (bf16[2,64,256]{2,1,0:T(8,128)(2,1)S(1)}, bf16[2,64,256]{2,1,0:T(8,128)(2,1)S(1)}, u32[]{:S(2)}, u32[]{:S(2)}) collective-permute-start(bf16[2,64,256]{2,1,0:T(8,128)(2,1)S(1)} %get-tuple-element.47), channel_id=1, source_target_pairs={{0,12},{1,13},{2,14},{3,15},{4,8},{5,9},{6,10},{7,11},{8,4},{9,5},... | collective-permute-start | bytes 196616 | tf_op jit(solution)/shard_map/ppermute | solution.py:35
  75.7 0.0 collective-permute-done.5
  75.7 0.6 collective-permute-done.6
  76.3 4.4 %collective-permute-done.7 = bf16[2,64,256]{2,1,0:T(8,128)(2,1)S(1)} collective-permute-done((bf16[2,64,256]{2,1,0:T(8,128)(2,1)S(1)}, bf16[2,64,256]{2,1,0:T(8,128)(2,1)S(1)}, u32[]{:S(2)}, u32[]{:S(2)}) %collective-permute-start.7) | collective-permute-done | bytes 65568 | tf_op jit(solution)/shard_map/ppermute | solution.py:35
  80.7 2.8 %collective-permute-start.8 = (f32[64,256]{1,0:T(8,128)S(1)}, f32[64,256]{1,0:T(8,128)S(1)}, u32[]{:S(2)}, u32[]{:S(2)}) collective-permute-start(f32[64,256]{1,0:T(8,128)S(1)} %get-tuple-element.49), channel_id=1, source_target_pairs={{0,2},{1,3},{2,0},{3,1},{4,6},{5,7},{6,4},{7,5},{8,10},{9,11},{10,... | collective-permute-start | bytes 196616 | tf_op jit(solution)/shard_map/ppermute | solution.py:35
  83.4 3.4 %collective-permute-done.8.got_ref = f32[64,256]{1,0:T(8,128)S(1)} collective-permute-done((f32[64,256]{1,0:T(8,128)S(1)}, f32[64,256]{1,0:T(8,128)S(1)}, u32[]{:S(2)}, u32[]{:S(2)}) %collective-permute-start.8) | collective-permute-done | bytes 65568 | tf_op jit(solution)/shard_map/ppermute | solution.py:35
  86.8 1.3 %all-to-all-done.1.parts_ref = bf16[32,32,256]{2,1,0:T(8,128)(2,1)S(1)} async-done(((bf16[32,32,256]{2,1,0:T(8,128)(2,1)}), bf16[32,32,256]{2,1,0:T(8,128)(2,1)S(1)}, u32[]{:S(2)}, u32[]{:S(2)}) %all-to-all-start.1) | async-done | bytes 524320 | tf_op jit(solution)/shard_map/all_to_all | solution.py:39
  88.2 0.7 last_sums.1
  (4 shorter events, 0.1 us)
Async XLA Ops:
  0.6 23.3 %collective-permute-start = (bf16[1024,256]{1,0:T(8,128)(2,1)}, bf16[1024,256]{1,0:T(8,128)(2,1)S(1)}, u32[]{:S(2)}, u32[]{:S(2)}) collective-permute-start(bf16[1024,256]{1,0:T(8,128)(2,1)} %slab_ref.5), channel_id=1, source_target_pairs={{0,496},{1,481},{2,498},{3,483},{4,500},{5,485},{6,502},{7,487},{8... | collective-permute-start | bytes 1572872 | tf_op jit(solution)/shard_map/ppermute | solution.py:30
  5.5 18.4 %all-to-all-start = ((s32[16,16,128]{2,1,0:T(8,128)}), s32[16,16,128]{2,1,0:T(8,128)S(1)}, u32[]{:S(2)}, u32[]{:S(2)}) async-start(s32[16,16,128]{2,1,0:T(8,128)} %pack_lists.1), calls=%async_computation | async-start | bytes 262144 | tf_op jit(solution)/shard_map/all_to_all | solution.py:39
  18.7 1.0 %copy-start = (bf16[4,256,256]{2,1,0:T(8,128)(2,1)S(1)}, bf16[4,256,256]{2,1,0:T(8,128)(2,1)}, u32[]{:S(2)}) copy-start(bf16[4,256,256]{2,1,0:T(8,128)(2,1)} %ops_hbm.1) | copy-start | bytes 1572868
  19.7 1.0 %copy-start.2 = (bf16[1024,256]{1,0:T(8,128)(2,1)S(1)}, bf16[1024,256]{1,0:T(8,128)(2,1)}, u32[]{:S(2)}) copy-start(bf16[1024,256]{1,0:T(8,128)(2,1)} %slab_ref.5) | copy-start | bytes 1572868
  23.9 2.3 %copy-start.3 = (bf16[1024,256]{1,0:T(8,128)(2,1)S(1)}, bf16[1024,256]{1,0:T(8,128)(2,1)}, u32[]{:S(2)}) copy-start(bf16[1024,256]{1,0:T(8,128)(2,1)} %slab_ref.5) | copy-start | bytes 1572868
  23.9 9.8 %collective-permute-start.1 = (bf16[1024,256]{1,0:T(8,128)(2,1)S(1)}, bf16[1024,256]{1,0:T(8,128)(2,1)S(1)}, u32[]{:S(2)}, u32[]{:S(2)}) collective-permute-start(bf16[1024,256]{1,0:T(8,128)(2,1)S(1)} %after_lists.1.refs_2_), channel_id=1, source_target_pairs={{0,1},{1,0},{2,3},{3,2},{4,5},{5,4},{6,7},{7,6},{8,9},{9,8},{10,11... | collective-permute-start | bytes 1572872 | tf_op jit(solution)/shard_map/ppermute | solution.py:35
  31.8 23.6 %collective-permute-start.3 = (bf16[336,512]{1,0:T(8,128)(2,1)S(1)}, bf16[336,512]{1,0:T(8,128)(2,1)S(1)}, u32[]{:S(2)}, u32[]{:S(2)}) collective-permute-start(bf16[336,512]{1,0:T(8,128)(2,1)S(1)} %get-tuple-element.38), channel_id=1, source_target_pairs={{0,16},{1,33},{2,18},{3,35},{4,20},{5,37},{6,22},{7,39},{8,24},{9,... | collective-permute-start | bytes 1032200 | tf_op jit(solution)/shard_map/ppermute | solution.py:30
  38.0 21.7 %collective-permute-start.2 = (bf16[336,512]{1,0:T(8,128)(2,1)}, bf16[336,512]{1,0:T(8,128)(2,1)S(1)}, u32[]{:S(2)}, u32[]{:S(2)}) collective-permute-start(bf16[336,512]{1,0:T(8,128)(2,1)} %get-tuple-element.30), channel_id=1, source_target_pairs={{0,32},{1,17},{2,34},{3,19},{4,36},{5,21},{6,38},{7,23},{8,40},{9,... | collective-permute-start | bytes 1032200 | tf_op jit(solution)/shard_map/ppermute | solution.py:30
  39.9 15.6 %copy-start.1 = (bf16[4,256,256]{2,1,0:T(8,128)(2,1)S(1)}, bf16[4,256,256]{2,1,0:T(8,128)(2,1)}, u32[]{:S(2)}) copy-start(bf16[4,256,256]{2,1,0:T(8,128)(2,1)} %ops_hbm.1) | copy-start | bytes 1572868
  39.9 48.2 %all-to-all-start.1 = ((bf16[32,32,256]{2,1,0:T(8,128)(2,1)}), bf16[32,32,256]{2,1,0:T(8,128)(2,1)S(1)}, u32[]{:S(2)}, u32[]{:S(2)}) async-start(bf16[32,32,256]{2,1,0:T(8,128)(2,1)} %get-tuple-element.41), calls=%async_computation.1 | async-start | bytes 1048576 | tf_op jit(solution)/shard_map/all_to_all | solution.py:39
  61.3 3.8 %collective-permute-start.4 = (f32[8,64,256]{2,1,0:T(8,128)S(1)}, f32[8,64,256]{2,1,0:T(8,128)S(1)}, u32[]{:S(2)}, u32[]{:S(2)}) collective-permute-start(f32[8,64,256]{2,1,0:T(8,128)S(1)} %get-tuple-element.40), channel_id=1, source_target_pairs={{0,1},{1,0},{2,3},{3,2},{4,5},{5,4},{6,7},{7,6},{8,9},{9,8},{10,11... | collective-permute-start | bytes 1572872 | tf_op jit(solution)/shard_map/ppermute | solution.py:35
  65.2 10.4 %collective-permute-start.5 = (bf16[2,64,256]{2,1,0:T(8,128)(2,1)S(1)}, bf16[2,64,256]{2,1,0:T(8,128)(2,1)S(1)}, u32[]{:S(2)}, u32[]{:S(2)}) collective-permute-start(bf16[2,64,256]{2,1,0:T(8,128)(2,1)S(1)} %get-tuple-element.46), channel_id=1, source_target_pairs={{0,4},{1,5},{2,6},{3,7},{4,0},{5,1},{6,2},{7,3},{8,12},{9,13},{10,... | collective-permute-start | bytes 196616 | tf_op jit(solution)/shard_map/ppermute | solution.py:35
  68.6 7.7 %collective-permute-start.6 = (bf16[2,64,256]{2,1,0:T(8,128)(2,1)S(1)}, bf16[2,64,256]{2,1,0:T(8,128)(2,1)S(1)}, u32[]{:S(2)}, u32[]{:S(2)}) collective-permute-start(bf16[2,64,256]{2,1,0:T(8,128)(2,1)S(1)} %get-tuple-element.48), channel_id=1, source_target_pairs={{0,8},{1,9},{2,10},{3,11},{4,12},{5,13},{6,14},{7,15},{8,0},{9,1},... | collective-permute-start | bytes 196616 | tf_op jit(solution)/shard_map/ppermute | solution.py:35
  73.3 7.4 %collective-permute-start.7 = (bf16[2,64,256]{2,1,0:T(8,128)(2,1)S(1)}, bf16[2,64,256]{2,1,0:T(8,128)(2,1)S(1)}, u32[]{:S(2)}, u32[]{:S(2)}) collective-permute-start(bf16[2,64,256]{2,1,0:T(8,128)(2,1)S(1)} %get-tuple-element.47), channel_id=1, source_target_pairs={{0,12},{1,13},{2,14},{3,15},{4,8},{5,9},{6,10},{7,11},{8,4},{9,5},... | collective-permute-start | bytes 196616 | tf_op jit(solution)/shard_map/ppermute | solution.py:35
  80.7 6.2 %collective-permute-start.8 = (f32[64,256]{1,0:T(8,128)S(1)}, f32[64,256]{1,0:T(8,128)S(1)}, u32[]{:S(2)}, u32[]{:S(2)}) collective-permute-start(f32[64,256]{1,0:T(8,128)S(1)} %get-tuple-element.49), channel_id=1, source_target_pairs={{0,2},{1,3},{2,0},{3,1},{4,6},{5,7},{6,4},{7,5},{8,10},{9,11},{10,... | collective-permute-start | bytes 196616 | tf_op jit(solution)/shard_map/ppermute | solution.py:35
